TPU v7x, 32 devices: a whole 2x2x4 slice. The times are simulated.
32 devices in a mesh: group: 4 (over x, core), tensor: 8 (over z, y).
Axes of the slice: x: 2, y: 2, z: 4, core: 2. Of those that a mesh axis runs over, the one named last changes fastest.
Arguments:
- hidden_in: bfloat16 [8192, 1536], P(('group', 'tensor')), may hold values from -6 to 6
- request_ids: int32 [32, 256], P(('group', 'tensor')), may hold values from 0 to 3, never falling along the last dimension, each value on 1 to 128 neighbouring positions
- norm_gains: float32 [2, 1536], replicated, may hold values from 0.5 to 1.5
- query_key_value_weight: bfloat16 [1536, 3072], replicated, may hold values from -0.15625 to 0.15625
- w_out: bfloat16 [1536, 1536], replicated, may hold values from -0.15625 to 0.15625
- w_in: bfloat16 [2, 1536, 4096], P(None, None, 'tensor'), may hold values from -0.15625 to 0.15625
- w_down: bfloat16 [4096, 1536], P('tensor'), may hold values from -0.09375 to 0.09375
- prefix_cache: bfloat16 [4, 1024, 1536], P('group', 'tensor'), may hold values from -210 to 210
- prefix_owner: int32 [8], replicated, may hold values from 0 to 3
- page_dest: int32 [512, 1], P(('group', 'tensor')), may hold values from 0 to 3; in each aligned block of 16 rows (0 to 15, 16 to 31, ...) at most 8 rows name the same one
Outputs:
- hidden_out: bfloat16 [8192, 1536], P(('group', 'tensor'))
- suffix_cache: bfloat16 [4, 8, 4, 8, 16, 1536], P('group', 'tensor')
Inputs may be any that keep to these rules, and one draw needn't show every extreme that they name: `request_ids`: each row numbers its requests from 0 in order of tokens, never falling, each request holding 1 to 128 tokens. `prefix_owner`: each block of the prefix cache is read from the slot of its owner only. `page_dest`: among the 16 pages of one device at most 8 have the same destination, and exactly 8 in some devices.
All inputs are finite; a program needn't handle non-finite values.
Results may differ from a plain program's by a relative error of at most 0.013.
The roundings to bfloat16 on the way count: a program that leaves them out, or rounds other values in their place, can miss the bound.
Values may be sent and summed in bfloat16 or wider, within the bound.
No kernel may reach another device: no remote copies, remote signals or barrier semaphores. Data moves between devices by JAX's collectives and lax.ppermute only.
A program may use at most 192 MiB of HBM per device.

v0:
```python
import jax
import jax.numpy as jnp
from jax import lax
from jax.sharding import PartitionSpec as P

QUERY_HEADS = 16
KEY_VALUE_HEADS = 8
HEAD_DIMENSION = 96
PREFIX_TOKENS = 1024
CAP = 8


ROPE_BASE = 100000.0
EPSILON = 1e-05
NEGATIVE_FILLER = -1e30


def from_root(shard, axis, root):
    mine = lax.axis_index(axis) == root
    return lax.psum(jnp.where(mine, shard, jnp.zeros_like(shard)), axis)


def rms_norm(inputs, gain_row):
    floated = inputs.astype(jnp.float32)
    return (
        floated
        * lax.rsqrt(jnp.mean(floated * floated, axis=-1, keepdims=True) + EPSILON)
        * gain_row
    )


def apply_rotary(head_values, locate_position):
    half_dim = head_values.shape[-1] // 2
    frequency = ROPE_BASE ** (-jnp.arange(half_dim, dtype=jnp.float32) / half_dim)
    angles = locate_position.astype(jnp.float32)[:, None] * frequency[None, :]
    cosine = jnp.cos(angles)[:, None, :]
    sine_part = jnp.sin(angles)[:, None, :]
    first_half = head_values[..., :half_dim]
    second_half = head_values[..., half_dim:]
    return jnp.concatenate(
        [
            first_half * cosine - second_half * sine_part,
            second_half * cosine + first_half * sine_part,
        ],
        axis=-1,
    )


def positions(segment):
    row_number = segment.shape[0]
    row_index = jnp.arange(row_number, dtype=jnp.int32)
    same_request = segment[:, None] == segment[None, :]
    first_row = jnp.min(jnp.where(same_request, row_index[None, :], row_number), axis=1)
    return PREFIX_TOKENS + row_index - first_row


def attend_update(attn_state, scores, value_head_rows):
    row_max, row_total, weighted = attn_state
    new_max = jnp.maximum(row_max, jnp.max(scores, axis=-1))
    weights = jnp.exp(scores - new_max[..., None])
    row_total = jnp.sum(weights, axis=-1)
    weighted = jnp.einsum(
        "rkgn,nkd->rkgd",
        weights.astype(jnp.bfloat16),
        value_head_rows,
        preferred_element_type=jnp.float32,
    )
    return (new_max, row_total, weighted)


def combine_states(left_state, right_state):
    new_max = jnp.maximum(left_state[0], right_state[0])
    left_factor = jnp.exp(left_state[0] - new_max)
    right_factor = jnp.exp(right_state[0] - new_max)
    row_total = left_state[1] * left_factor + right_state[1] * right_factor
    weighted = left_state[2] * left_factor[..., None] + right_state[2] * right_factor[..., None]
    return (new_max, row_total, weighted)


def expand_with(token_block, loaded_pages):
    gate_proj = jnp.dot(token_block, loaded_pages[0], preferred_element_type=jnp.float32)
    up_proj = jnp.dot(token_block, loaded_pages[1], preferred_element_type=jnp.float32)
    return (jax.nn.silu(gate_proj) * up_proj).astype(jnp.bfloat16)


def contract_with(activated, loaded_pages):
    return jnp.dot(activated, loaded_pages, preferred_element_type=jnp.float32)


def on_device(
    hidden_in,
    request_ids,
    norm_gains,
    query_key_value_weight,
    w_out,
    w_in,
    w_down,
    prefix_cache,
    prefix_owner,
    page_dest,
):
    token_rows = hidden_in.shape[0]
    query_columns = QUERY_HEADS * HEAD_DIMENSION
    key_value_width = KEY_VALUE_HEADS * HEAD_DIMENSION
    segment = request_ids[0]
    normed = rms_norm(hidden_in, norm_gains[0]).astype(jnp.bfloat16)
    projected_rows = jnp.dot(normed, query_key_value_weight, preferred_element_type=jnp.float32)
    locate_position = positions(segment)
    query_rows = apply_rotary(
        projected_rows[:, :query_columns].reshape(token_rows, QUERY_HEADS, HEAD_DIMENSION),
        locate_position,
    ).astype(jnp.bfloat16)
    fresh_keys = apply_rotary(
        projected_rows[:, query_columns : query_columns + key_value_width].reshape(
            token_rows, KEY_VALUE_HEADS, HEAD_DIMENSION
        ),
        locate_position,
    ).astype(jnp.bfloat16)
    fresh_values = (
        projected_rows[:, query_columns + key_value_width :]
        .reshape(token_rows, KEY_VALUE_HEADS, HEAD_DIMENSION)
        .astype(jnp.bfloat16)
    )
    query_groups = query_rows.reshape(
        token_rows, KEY_VALUE_HEADS, QUERY_HEADS // KEY_VALUE_HEADS, HEAD_DIMENSION
    )
    score_scale = HEAD_DIMENSION ** (-0.5)
    row_index = jnp.arange(token_rows, dtype=jnp.int32)
    allowed = (segment[None, :] == segment[:, None]) & (row_index[None, :] <= row_index[:, None])
    local_scores = (
        jnp.einsum("rkgd,nkd->rkgn", query_groups, fresh_keys, preferred_element_type=jnp.float32)
        * score_scale
    )
    local_scores = jnp.where(allowed[:, None, None, :], local_scores, NEGATIVE_FILLER)
    empty_state = (
        jnp.full(
            (token_rows, KEY_VALUE_HEADS, QUERY_HEADS // KEY_VALUE_HEADS),
            NEGATIVE_FILLER,
            jnp.float32,
        ),
        jnp.zeros((token_rows, KEY_VALUE_HEADS, QUERY_HEADS // KEY_VALUE_HEADS), jnp.float32),
        jnp.zeros(
            (token_rows, KEY_VALUE_HEADS, QUERY_HEADS // KEY_VALUE_HEADS, HEAD_DIMENSION),
            jnp.float32,
        ),
    )
    local_state = attend_update(empty_state, local_scores, fresh_values)
    owner_row = prefix_owner[lax.axis_index("tensor")]
    block_prefix = from_root(prefix_cache[0], "group", owner_row)
    loaded_pages = lax.all_gather(block_prefix, "tensor", axis=0, tiled=True)
    key_total = loaded_pages.shape[0]
    key_head_rows = loaded_pages[:, :key_value_width].reshape(
        key_total, KEY_VALUE_HEADS, HEAD_DIMENSION
    )
    value_head_rows = loaded_pages[:, key_value_width:].reshape(
        key_total, KEY_VALUE_HEADS, HEAD_DIMENSION
    )
    scores = (
        jnp.einsum(
            "rkgd,nkd->rkgn", query_groups, key_head_rows, preferred_element_type=jnp.float32
        )
        * score_scale
    )
    attn_state = attend_update(empty_state, scores, value_head_rows)
    attn_state = combine_states(attn_state, local_state)
    attended = (
        (attn_state[2] / attn_state[1][..., None])
        .reshape(token_rows, QUERY_HEADS * HEAD_DIMENSION)
        .astype(jnp.bfloat16)
    )
    middle = (
        hidden_in.astype(jnp.float32) + jnp.dot(attended, w_out, preferred_element_type=jnp.float32)
    ).astype(jnp.bfloat16)
    second = rms_norm(middle, norm_gains[1]).astype(jnp.bfloat16)
    activated = expand_with(second, lax.all_gather(w_in, "tensor", axis=2, tiled=True))
    mlp_out = contract_with(activated, lax.all_gather(w_down, "tensor", axis=0, tiled=True))
    hidden_out = (middle.astype(jnp.float32) + mlp_out).astype(jnp.bfloat16)
    cache_rows = jnp.concatenate(
        [
            fresh_keys.reshape(token_rows, key_value_width),
            fresh_values.reshape(token_rows, key_value_width),
        ],
        axis=1,
    )
    page_count = page_dest.shape[0]
    page_blocks = cache_rows.reshape(page_count, token_rows // page_count, 2 * key_value_width)
    destination = page_dest[:, 0]
    dest_count = lax.axis_size("group")
    group_iota = jnp.arange(dest_count, dtype=jnp.int32)
    onehot = (destination[:, None] == group_iota[None, :]).astype(jnp.int32)
    page_rank = jnp.sum((jnp.cumsum(onehot, axis=0) - onehot) * onehot, axis=1)
    slot_iota = jnp.arange(CAP, dtype=jnp.int32)
    select = (
        (destination[:, None, None] == group_iota[None, :, None])
        & (page_rank[:, None, None] == slot_iota[None, None, :])
    ).astype(jnp.bfloat16)
    outgoing = jnp.einsum(
        "pdj,pxc->djxc", select, page_blocks, preferred_element_type=jnp.float32
    ).astype(jnp.bfloat16)
    received = lax.all_to_all(outgoing, "group", split_axis=0, concat_axis=0, tiled=True)
    return (hidden_out, received[None, None])


def solution(mesh):
    return jax.shard_map(
        on_device,
        mesh=mesh,
        in_specs=(
            P(("group", "tensor"), None),
            P(("group", "tensor"), None),
            P(),
            P(),
            P(),
            P(None, None, "tensor"),
            P("tensor", None),
            P("group", "tensor", None),
            P(),
            P(("group", "tensor"), None),
        ),
        out_specs=(P(("group", "tensor"), None), P("group", "tensor", None, None, None, None)),
        check_vma=False,
    )
```

profile of v0, /device:TPU:0, one launch (start us, length us, event | category | flops | bytes accessed | tf_op | source)
XLA Modules:
  0.0 789.0 jit_solution(4159007739537823863)
XLA Ops:
  7.2 0.0 all-reduce.2.cloned.1.call-start
  7.2 1.2 dynamic_slice.3
  9.1 0.0 copy-start.18
  9.1 0.0 copy-start
  9.1 0.8 select_bitcast_fusion
  9.9 0.0 all-reduce.2.cloned.1.call-update
  9.9 0.0 all-gather.4.cloned.1.call-start
  10.0 36.2 %all-reduce.2.cloned.1.call-done = bf16[128,1536]{1,0:T(8,128)(2,1)} async-done(((bf16[128,1536]{1,0:T(8,128)(2,1)}), bf16[128,1536]{1,0:T(8,128)(2,1)}) %all-reduce.2.cloned.1.call-update) | async-done | bytes 393232 | tf_op jit(solution)/shard_map/psum | solution.py:20
  46.2 0.0 all-gather.4.cloned.1.call-update
  46.3 0.0 all-gather.6.cloned.1.call-start
  46.3 0.7 all-gather.6.cloned.1.call-update
  47.0 0.0 all-gather.8.cloned.1.call-start
  47.0 0.5 all-gather.8.cloned.1.call-update
  47.6 0.6 slice_reduce_fusion
  48.2 0.2 fusion.28
  48.4 5.2 fusion.36
  53.7 0.0 copy-start.17
  53.7 0.1 slice.57
  53.8 1.6 copy-done.2
  55.4 0.3 copy.31
  55.7 0.0 copy-start.20
  55.8 0.1 select_reduce_fusion
  55.9 0.3 multiply_cosine_fusion
  56.2 0.1 multiply_subtract_fusion
  56.3 0.5 copy-done.13
  56.8 0.0 copy-done.14
  56.8 0.2 copy-done.9
  57.0 0.1 copy-done.11
  57.1 0.3 copy.35
  57.4 0.4 convert_element_type.83
  57.8 0.1 copy.36
  57.9 0.1 copy.37
  58.1 0.1 iota_compare_fusion.1
  58.2 0.1 copy.34
  58.3 0.2 select_reduce_fusion.1
  58.5 1.7 convolution_convert_fusion
  60.2 3.6 all-to-all-start
  63.7 2.7 slice.54
  66.4 0.9 copy.32
  67.3 1.9 copy.29
  69.3 0.1 fusion.51
  69.4 1.0 subtract_convert_fusion
  70.4 0.7 copy-done.6
  71.2 0.9 fusion.16
  72.1 0.0 copy-start.4
  72.1 0.6 copy-done.15
  72.7 0.9 fusion.14
  73.6 2.3 fusion.21
  75.8 8.0 %all-to-all-done = bf16[4,8,16,1536]{3,1,2,0:T(8,128)(2,1)S(1)} async-done(((bf16[4,8,16,1536]{3,1,2,0:T(8,128)(2,1)}), bf16[4,8,16,1536]{3,1,2,0:T(8,128)(2,1)S(1)}, u32[]{:S(2)}, u32[]{:S(2)}) %all-to-all-start) | async-done | bytes 1572896 | tf_op jit(solution)/shard_map/all_to_all | solution.py:200
  83.8 1.6 copy.38
  85.4 23.7 %all-gather.4.cloned.1.call-done = bf16[1024,1536]{1,0:T(8,128)(2,1)} async-done(((bf16[128,1536]{1,0:T(8,128)(2,1)}), bf16[1024,1536]{1,0:T(8,128)(2,1)}) %all-gather.4.cloned.1.call-update) | async-done | bytes 3145744 | tf_op jit(solution)/shard_map/all_gather | solution.py:150
  109.1 3.3 fusion.68
  112.4 1.8 copy.28
  114.2 1.6 copy.27
  115.8 9.1 %bitcast_reduce_fusion = (f32[256,8,2]{0,2,1:T(2,128)S(1)}, f32[8,1024,256,2]{2,1,3,0:T(8,128)}) fusion(bf16[1024,8,96,1]{0,2,3,1:T(8,128)(2,1)S(1)} %bitcast.100, bf16[256,8,2,48]{0,3,2,1:T(8,128)(2,1)} %bitcast.111, bf16[256,8,2,48]{0,3,2,1:T(8,128)(2,1)S(1)} %bitcast.109), kind=kOutput, calls=%fused_computation.1 | convolution fusion | flops 815263744 | bytes 19152896 | tf_op jit(solution)/shard_map/rkgd,nkd->rkgn/dot_general | solution.py:159
  125.0 0.0 slice-start
  125.0 8.7 %fusion.1 = f32[256,8,2]{0,2,1:T(2,128)S(1)} fusion(f32[8,1024,256,2]{2,1,3,0:T(8,128)} %get-tuple-element.24, f32[256,8,2]{0,2,1:T(2,128)S(1)} %broadcast_maximum_fusion.1), kind=kLoop, calls=%fused_computation.3 | loop fusion | flops 12578816 | bytes 16809984 | tf_op jit(solution)/shard_map/reduce_sum | solution.py:61
  133.8 0.0 slice-start.1
  133.8 9.0 %fusion.33 = bf16[256,8,2,96]{0,3,2,1:T(8,128)(2,1)S(1)} fusion(f32[8,96,256,2]{2,1,3,0:T(8,128)S(1)} %copy-done.5, bf16[1024,8,96,1]{0,2,3,1:T(8,128)(2,1)S(1)} %bitcast.106, f32[8,1024,256,2]{2,1,3,0:T(8,128)} %get-tuple-element.24, f32[256,8,2]{0,2,1:T(2,128)S(1)} %broadcast_maximum_fusion.1, f32[256,8,2]{0,2,1:T(2,128)S(1)} %get-tuple-element.8, ...), kind=kOutput, calls=%fused_computation.42 | convolution fusion | flops 819855360 | bytes 20774912 | tf_op jit(solution)/shard_map/rkgn,nkd->rkgd/dot_general | solution.py:62
  142.9 1.5 multiply_reduce_fusion
  144.4 445.4 %all-gather.6.cloned.1.call-done = bf16[2,1536,4096]{2,1,0:T(8,128)(2,1)} async-done(((bf16[2,1536,512]{2,1,0:T(8,128)(2,1)}), bf16[2,1536,4096]{2,1,0:T(8,128)(2,1)}) %all-gather.6.cloned.1.call-update) | async-done | bytes 25165840 | tf_op jit(solution)/shard_map/all_gather | solution.py:175
  589.8 10.4 %fusion.4 = f32[256,4096]{1,0:T(8,128)} fusion(bf16[2,1536,4096]{2,1,0:T(8,128)(2,1)} %all-gather.6.cloned.1.call-done, f32[256,1536]{1,0:T(8,128)S(1)} %get-tuple-element.26, f32[1536]{0:T(1024)S(1)} %copy-done.19, f32[256]{0:T(256)S(1)} %add_rsqrt_fusion), kind=kOutput, calls=%fused_computation.8 | convolution fusion | flops 3222405120 | bytes 18357248 | tf_op jit(solution)/shard_map/dot_general | solution.py:81
  600.2 168.4 %all-gather.8.cloned.1.call-done = bf16[4096,1536]{1,0:T(8,128)(2,1)} async-done(((bf16[512,1536]{1,0:T(8,128)(2,1)}), bf16[4096,1536]{1,0:T(8,128)(2,1)}) %all-gather.8.cloned.1.call-update) | async-done | bytes 12582928 | tf_op jit(solution)/shard_map/all_gather | solution.py:176
  768.6 13.9 %fusion.18 = bf16[256,1536]{1,0:T(8,128)(2,1)} fusion(f32[256,1536]{1,0:T(8,128)S(1)} %get-tuple-element.26, bf16[4096,1536]{1,0:T(8,128)(2,1)} %all-gather.8.cloned.1.call-done, bf16[2,1536,4096]{2,1,0:T(8,128)(2,1)} %all-gather.6.cloned.1.call-done, f32[256,4096]{1,0:T(8,128)} %fusion.4, f32[1536]{0:T(1024)S(1)} %copy-done.19, f32[256]{0:T(256)S(1)} %add_rsqrt_fusion), kind=kOutput, calls=%fused_computation.25 | convolution fusion | flops 6450708480 | bytes 33301504 | tf_op jit(solution)/shard_map/dot_general | solution.py:87
  (44 shorter events, 0.3 us)
Async XLA Ops:
  7.2 39.1 %all-reduce.2.cloned.1.call-start = ((), (), s32[]{:S(2)}) async-start(), calls=%async_computation.1 | async-start | bytes 786432 | tf_op jit(solution)/shard_map/psum | solution.py:20
  9.1 38.5 %copy-start.18 = (f32[2,1536]{1,0:T(2,128)S(1)}, f32[2,1536]{1,0:T(2,128)}, u32[]{:S(2)}) copy-start(f32[2,1536]{1,0:T(2,128)} %param.12) | copy-start | bytes 36868
  9.1 39.1 %copy-start = (bf16[256,1536]{1,0:T(8,128)(2,1)S(1)}, bf16[256,1536]{1,0:T(8,128)(2,1)}, u32[]{:S(2)}) copy-start(bf16[256,1536]{1,0:T(8,128)(2,1)} %param.10) | copy-start | bytes 2359300
  9.9 99.2 %all-gather.4.cloned.1.call-start = ((), (), s32[]{:S(2)}) async-start(), calls=%async_computation.2 | async-start | bytes 3538944 | tf_op jit(solution)/shard_map/all_gather | solution.py:150
  46.3 543.5 %all-gather.6.cloned.1.call-start = ((), (), s32[]{:S(2)}) async-start(), calls=%async_computation.3 | async-start | bytes 28311552 | tf_op jit(solution)/shard_map/all_gather | solution.py:175
  47.0 721.6 %all-gather.8.cloned.1.call-start = ((), (), s32[]{:S(2)}) async-start(), calls=%async_computation.4 | async-start | bytes 14155776 | tf_op jit(solution)/shard_map/all_gather | solution.py:176
  53.7 1.7 copy-start.2
  53.7 2.1 copy-start.17
  55.7 2.3 copy-start.20
  56.1 0.6 copy-start.13
  56.2 0.6 copy-start.14
  56.3 0.7 copy-start.9
  56.3 0.7 copy-start.11
  60.2 23.6 %all-to-all-start = ((bf16[4,8,16,1536]{3,1,2,0:T(8,128)(2,1)}), bf16[4,8,16,1536]{3,1,2,0:T(8,128)(2,1)S(1)}, u32[]{:S(2)}, u32[]{:S(2)}) async-start(bf16[4,8,16,1536]{3,1,2,0:T(8,128)(2,1)} %convolution_convert_fusion), calls=%async_computation | async-start | bytes 3145728 | tf_op jit(solution)/shard_map/all_to_all | solution.py:200
  67.3 3.9 copy-start.10
  67.3 3.9 copy-start.12
  70.4 0.8 copy-start.6
  70.4 1.6 copy-start.8
  72.1 0.6 copy-start.15
  72.1 1.5 copy-start.4
  112.4 3.4 copy-start.7
  125.0 8.8 %copy-start.16 = (f32[256,8,2]{0,2,1:T(2,128)S(1)}, f32[256,8,2]{0,2,1:T(2,128)}, u32[]{:S(2)}) copy-start(f32[256,8,2]{0,2,1:T(2,128)} %copy-done.15) | copy-start | bytes 49156
  125.0 8.8 %copy-start.3 = (bf16[1024,768]{0,1:T(8,128)(2,1)S(1)}, bf16[1024,768]{0,1:T(8,128)(2,1)}, u32[]{:S(2)}) copy-start(bf16[1024,768]{0,1:T(8,128)(2,1)} %copy.27) | copy-start | bytes 4718596
  125.0 8.8 %copy-start.5 = (f32[8,96,256,2]{2,1,3,0:T(8,128)S(1)}, f32[8,96,256,2]{2,1,3,0:T(8,128)}, u32[]{:S(2)}) copy-start(f32[8,96,256,2]{2,1,3,0:T(8,128)} %fusion.21) | copy-start | bytes 4718596
  125.0 17.8 %slice-start = ((s8[4718592]{0:T(1024)(128)(4,1)}), s8[524288]{0:T(1024)(128)(4,1)S(1)}, s32[]{:S(2)}) async-start(s8[4718592]{0:T(1024)(128)(4,1)} %bitcast.98), calls=%async_computation.5 | async-start | bytes 1048576
  133.8 9.0 %slice-start.1 = ((s8[4718592]{0:T(1024)(128)(4,1)}), s8[4194304]{0:T(1024)(128)(4,1)S(1)}, s32[]{:S(2)}) async-start(s8[4718592]{0:T(1024)(128)(4,1)} %bitcast.98), calls=%async_computation.6 | async-start | bytes 8388608
  133.8 9.0 %copy-start.1 = (bf16[256,1536]{1,0:T(8,128)(2,1)S(1)}, bf16[256,1536]{1,0:T(8,128)(2,1)}, u32[]{:S(2)}) copy-start(bf16[256,1536]{1,0:T(8,128)(2,1)} %param.10) | copy-start | bytes 2359300
  142.9 446.9 %copy-start.19 = (f32[1536]{0:T(1024)S(1)}, f32[1536]{0:T(1024)}, u32[]{:S(2)}) copy-start(f32[1536]{0:T(1024)} %get-tuple-element.6) | copy-start | bytes 18436
Sparse Core Ops, SparseCore 0:
  10.9 35.2 all-reduce.1
  48.7 60.3 all-gather.3
  110.7 479.0 all-gather.5
  592.1 176.4 all-gather.7
where the time goes:
time: 789 us
  waiting for transfers between devices  683 us (87%)
  matrix products  54 us (7%)
  local copies, waits for them, and re-layouts  20.9 us (3%)
  between operations  14.8 us (2%)
  other arithmetic  12.7 us (2%)
    all_gather x1, waiting for transfers between devices, on_device(): lax.all_gather(w_in, 'tensor', axis=2, tiled=True)  445 us
    all_gather x1, waiting for transfers between devices, on_device(): lax.all_gather(w_down, 'tensor', axis=0, tiled=True)  168 us
    psum x1, waiting for transfers between devices, from_root(): return lax.psum(jnp.where(mine, shard, jnp.zeros_like(shard)), axis)  36.2 us
    all_gather x1, waiting for transfers between devices, on_device(): loaded_pages = lax.all_gather(block_prefix, 'tensor', axis=0, tiled=True)  23.7 us
  transfers between devices with their start and end apart: 5, of which 5 were waited for; matrix products, arithmetic and copies ran while one was open for 9% of the time, Pallas kernels for 0%

commit v1 on v0

--- a/solution.py
+++ b/solution.py
@@ -15,9 +15,90 @@
 NEGATIVE_FILLER = -1e30
 
 
-def from_root(shard, axis, root):
-    mine = lax.axis_index(axis) == root
-    return lax.psum(jnp.where(mine, shard, jnp.zeros_like(shard)), axis)
+Z_SIZE = 4
+
+
+def tensor_xor(value, tensor_count, z_bits):
+    width = tensor_count // Z_SIZE
+    pairs = [
+        (z * width + y, (z ^ z_bits) * width + y) for z in range(Z_SIZE) for y in range(width)
+    ]
+    return lax.ppermute(value, "tensor", pairs)
+
+
+def tensor_turn(value, tensor_count, step):
+    width = tensor_count // Z_SIZE
+    pairs = [
+        (z * width + y, z * width + (y + step) % width)
+        for z in range(Z_SIZE)
+        for y in range(width)
+    ]
+    return lax.ppermute(value, "tensor", pairs)
+
+
+def group_xor(value, group_count, bits):
+    return lax.ppermute(value, "group", [(g, g ^ bits) for g in range(group_count)])
+
+
+def gather_prefix(block, prefix_owner, group_count, tensor_count):
+    group = lax.axis_index("group")
+    owner = prefix_owner[lax.axis_index("tensor")]
+    rows = block.shape[0] // group_count
+    width = tensor_count // Z_SIZE
+    quarter = lax.dynamic_slice_in_dim(block, group * rows, rows, 0)
+    for bits in range(1, group_count):
+        sent = lax.dynamic_slice_in_dim(block, (group ^ bits) * rows, rows, 0)
+        came = group_xor(sent, group_count, bits)
+        quarter = jnp.where(owner == (group ^ bits), came, quarter)
+    line = jnp.concatenate(
+        [quarter] + [tensor_xor(quarter, tensor_count, bits) for bits in range(1, Z_SIZE)]
+    )
+    plane = jnp.concatenate(
+        [line] + [tensor_turn(line, tensor_count, step) for step in range(1, width)]
+    )
+    across = group_xor(plane, group_count, 2)
+    own_rows = jnp.concatenate([plane, across])
+    return [own_rows, group_xor(own_rows, group_count, 1)]
+
+
+def gather_weights(w_in, w_down, group_count, tensor_count):
+    group = lax.axis_index("group")
+    across, core = group // 2, group % 2
+    width = tensor_count // Z_SIZE
+    part = w_in.shape[2] // 4
+
+    def piece(side):
+        start = (core * 2 + side) * part
+        sliced = lax.dynamic_slice_in_dim(w_in, start, part, 2)
+        return (
+            jnp.concatenate([sliced[0], sliced[1]], axis=1),
+            lax.dynamic_slice_in_dim(w_down, start, part, 0),
+        )
+
+    mine, other = piece(across), piece(1 - across)
+    pieces = [mine, other]
+    plane = [tuple(tensor_turn(v, tensor_count, step) for v in mine) for step in range(1, width)]
+    far = tuple(tensor_xor(v, tensor_count, 2) for v in mine)
+    pieces += plane
+    pieces += [tuple(group_xor(v, group_count, 2) for v in got) for got in plane]
+    far_across = tuple(group_xor(v, group_count, 2) for v in far)
+    pieces += [far, far_across]
+    for step in range(1, width):
+        far_plane = tuple(tensor_turn(v, tensor_count, step) for v in far)
+        pieces.append(far_plane)
+        last = []
+        for by_x, by_y in zip(far_plane, far_across):
+            half = by_x.shape[0] // 2
+            last.append(
+                jnp.concatenate(
+                    [
+                        group_xor(by_x[:half], group_count, 2),
+                        tensor_turn(by_y[half:], tensor_count, step),
+                    ]
+                )
+            )
+        pieces.append(tuple(last))
+    return pieces
 
 
 def rms_norm(inputs, gain_row):
@@ -77,14 +158,30 @@
     return (new_max, row_total, weighted)
 
 
-def expand_with(token_block, loaded_pages):
-    gate_proj = jnp.dot(token_block, loaded_pages[0], preferred_element_type=jnp.float32)
-    up_proj = jnp.dot(token_block, loaded_pages[1], preferred_element_type=jnp.float32)
-    return (jax.nn.silu(gate_proj) * up_proj).astype(jnp.bfloat16)
-
-
-def contract_with(activated, loaded_pages):
-    return jnp.dot(activated, loaded_pages, preferred_element_type=jnp.float32)
+def expand_with(token_block, gate_and_up):
+    both = jnp.dot(token_block, gate_and_up, preferred_element_type=jnp.float32)
+    half = both.shape[1] // 2
+    return (jax.nn.silu(both[:, :half]) * both[:, half:]).astype(jnp.bfloat16)
+
+
+def feed_forward(second, pieces, group_count, tensor_count):
+    beside = group_xor(second, group_count, 1)
+    far = tensor_xor(second, tensor_count, 1)
+    far_beside = group_xor(far, group_count, 1)
+    down = jnp.concatenate([p[1] for p in pieces])
+
+    def partial(left, right):
+        tokens = jnp.concatenate([left, right])
+        acts = jnp.concatenate([expand_with(tokens, p[0]) for p in pieces], axis=1)
+        sums = jnp.dot(acts, down, preferred_element_type=jnp.float32)
+        return sums[: left.shape[0]], sums[left.shape[0] :]
+
+    far_sum, far_beside_sum = partial(far, far_beside)
+    far_sum += group_xor(far_beside_sum.astype(jnp.bfloat16), group_count, 1).astype(jnp.float32)
+    returned = tensor_xor(far_sum.astype(jnp.bfloat16), tensor_count, 1)
+    own_sum, beside_sum = partial(second, beside)
+    own_sum += group_xor(beside_sum.astype(jnp.bfloat16), group_count, 1).astype(jnp.float32)
+    return own_sum + returned.astype(jnp.float32)
 
 
 def on_device(
@@ -102,6 +199,8 @@
     token_rows = hidden_in.shape[0]
     query_columns = QUERY_HEADS * HEAD_DIMENSION
     key_value_width = KEY_VALUE_HEADS * HEAD_DIMENSION
+    group_count, tensor_count = lax.axis_size("group"), lax.axis_size("tensor")
+    pieces = gather_weights(w_in, w_down, group_count, tensor_count)
     segment = request_ids[0]
     normed = rms_norm(hidden_in, norm_gains[0]).astype(jnp.bfloat16)
     projected_rows = jnp.dot(normed, query_key_value_weight, preferred_element_type=jnp.float32)
@@ -145,9 +244,9 @@
         ),
     )
     local_state = attend_update(empty_state, local_scores, fresh_values)
-    owner_row = prefix_owner[lax.axis_index("tensor")]
-    block_prefix = from_root(prefix_cache[0], "group", owner_row)
-    loaded_pages = lax.all_gather(block_prefix, "tensor", axis=0, tiled=True)
+    loaded_pages = jnp.concatenate(
+        gather_prefix(prefix_cache[0], prefix_owner, group_count, tensor_count)
+    )
     key_total = loaded_pages.shape[0]
     key_head_rows = loaded_pages[:, :key_value_width].reshape(
         key_total, KEY_VALUE_HEADS, HEAD_DIMENSION
@@ -172,8 +271,7 @@
         hidden_in.astype(jnp.float32) + jnp.dot(attended, w_out, preferred_element_type=jnp.float32)
     ).astype(jnp.bfloat16)
     second = rms_norm(middle, norm_gains[1]).astype(jnp.bfloat16)
-    activated = expand_with(second, lax.all_gather(w_in, "tensor", axis=2, tiled=True))
-    mlp_out = contract_with(activated, lax.all_gather(w_down, "tensor", axis=0, tiled=True))
+    mlp_out = feed_forward(second, pieces, group_count, tensor_count)
     hidden_out = (middle.astype(jnp.float32) + mlp_out).astype(jnp.bfloat16)
     cache_rows = jnp.concatenate(
         [

time: 789 us -> 251 us (0.32)
  waiting for transfers between devices: 683 us -> 94.1 us
  starting transfers between devices: 3.72 us -> 36 us
  local copies, waits for them, and re-layouts: 20.9 us -> 43 us
  between operations: 14.8 us -> 3.5 us
    all_gather x3 -> x0, waiting for transfers between devices: 637 us -> none  [the longest x1 445 us: on_device(): lax.all_gather(w_in, 'tensor', axis=2, tiled=True)]
    ppermute x0 -> x29, waiting for transfers between devices: none -> 94.1 us  [the longest x15 42 us: group_xor(): lax.ppermute(value, 'group', [(g, g ^ bits) for g in range(group_count)])]
    psum x1 -> x0, waiting for transfers between devices: 36.2 us -> none  [from_root(): return lax.psum(jnp.where(mine, shard, jnp.zeros_like(shard)), axis)]
    ppermute x0 -> x29, starting transfers between devices: none -> 32.4 us  [the longest x7 14.6 us: tensor_xor(): return lax.ppermute(value, 'tensor', pairs)]
    unnamed x47 -> x88, local copies, waits for them, and re-layouts: 5.39 us -> 18.3 us
    all_to_all x1, waiting for transfers between devices: 7.96 us -> 0.01 us  [on_device(): lax.all_to_all(outgoing, 'group', split_axis=0, concat_axis=0, tiled=True)]
    dot_general x2 -> x18, matrix products: 24.3 us -> 22.6 us  [the longest x16 18.9 us: expand_with(): both = jnp.dot(token_block, gate_and_up, preferred_element_type=jnp.float32)]
  transfers between devices with their start and end apart: 5 -> 30, of which waited for: 5 -> 9; matrix products, arithmetic and copies ran while one was open for 9% -> 43% of each run, Pallas kernels for 0% -> 0%
where the time goes in v1:
time: 251 us; the launch traced here: 250 us
  waiting for transfers between devices  94.1 us (37%)
  matrix products  54.2 us (22%)
  local copies, waits for them, and re-layouts  43 us (17%)
  starting transfers between devices  36 us (14%)
  other arithmetic  19.5 us (8%)
  between operations  3.5 us (1%)
    ppermute x15, waiting for transfers between devices, group_xor(): lax.ppermute(value, 'group', [(g, g ^ bits) for g in range(group_count)])  42 us
    ppermute x7, waiting for transfers between devices, tensor_xor(): return lax.ppermute(value, 'tensor', pairs)  32.3 us
    ppermute x7, waiting for transfers between devices, tensor_turn(): return lax.ppermute(value, 'tensor', pairs)  19.9 us
    dot_general x16, matrix products, expand_with(): both = jnp.dot(token_block, gate_and_up, preferred_element_type=jnp.float32)  18.9 us
    unnamed x88, local copies, waits for them, and re-layouts  18.3 us
    ppermute x7, starting transfers between devices, tensor_xor(): return lax.ppermute(value, 'tensor', pairs)  14.6 us
    dot_general x2, matrix products, attend_update(): jnp.einsum('rkgn,nkd->rkgd', weights.astype(jnp.bfloat16), value_head_row...  11.6 us
    ppermute x15, starting transfers between devices, group_xor(): lax.ppermute(value, 'group', [(g, g ^ bits) for g in range(group_count)])  10.7 us
  transfers between devices with their start and end apart: 30, of which 9 were waited for; matrix products, arithmetic and copies ran while one was open for 43% of the time, Pallas kernels for 0%

profile of v1, /device:TPU:0, one launch (start us, length us, event | category | flops | bytes accessed | tf_op | source)
XLA Modules:
  0.0 250.3 jit_solution(5343547958734376655)
XLA Ops:
  0.7 2.4 dynamic-slice_bitcast_fusion.1
  3.1 1.1 pad_maximum_fusion.2
  4.2 3.0 %collective-permute-start.10 = (bf16[1536,256]{1,0:T(8,128)(2,1)}, bf16[1536,256]{1,0:T(8,128)(2,1)}, u32[]{:S(2)}, u32[]{:S(2)}) collective-permute-start(bf16[1536,256]{1,0:T(8,128)(2,1)} %pad_maximum_fusion.2), channel_id=1, source_target_pairs={{0,1},{1,0},{2,3},{3,2},{4,5},{5,4},{6,7},{7,6},{8,9},{9,8},{10,11... | collective-permute-start | bytes 2359304 | tf_op jit(solution)/shard_map/ppermute | solution.py:36
  7.1 2.6 %collective-permute-start.12 = (bf16[1536,256]{1,0:T(8,128)(2,1)}, bf16[1536,256]{1,0:T(8,128)(2,1)}, u32[]{:S(2)}, u32[]{:S(2)}) collective-permute-start(bf16[1536,256]{1,0:T(8,128)(2,1)} %pad_maximum_fusion.2), channel_id=1, source_target_pairs={{0,4},{1,5},{2,6},{3,7},{4,0},{5,1},{6,2},{7,3},{8,12},{9,13},{10,... | collective-permute-start | bytes 2359304 | tf_op jit(solution)/shard_map/ppermute | solution.py:26
  10.8 1.2 collective-permute-start.1
  13.2 5.2 %fusion.30 = f32[256,3072]{1,0:T(8,128)S(1)} fusion(bf16[1536,3072]{1,0:T(8,128)(2,1)} %param.13, bf16[256,1536]{1,0:T(8,128)(2,1)S(1)} %copy-done, f32[1536]{0:T(1024)S(1)} %get-tuple-element.7, f32[256]{0:T(256)S(1)} %add_rsqrt_fusion.1), kind=kOutput, calls=%fused_computation.43 | convolution fusion | flops 2417491968 | bytes 13376512 | tf_op jit(solution)/shard_map/dot_general | solution.py:206
  22.9 1.7 convolution_convert_fusion
  24.7 3.6 %all-to-all-start = ((bf16[4,8,16,1536]{3,1,2,0:T(8,128)(2,1)}), bf16[4,8,16,1536]{3,1,2,0:T(8,128)(2,1)S(1)}, u32[]{:S(2)}, u32[]{:S(2)}) async-start(bf16[4,8,16,1536]{3,1,2,0:T(8,128)(2,1)} %convolution_convert_fusion), calls=%async_computation | async-start | bytes 3145728 | tf_op jit(solution)/shard_map/all_to_all | solution.py:298
  28.2 1.9 constant_dynamic-update-slice_fusion.27
  30.2 2.7 %slice.224 = f32[256,1536]{1,0:T(8,128)} slice(f32[256,3072]{1,0:T(8,128)} %copy-done.2), slice={[0:256], [0:1536]} | slice | bytes 3145728 | tf_op jit(solution)/shard_map/slice | solution.py:209
  35.3 1.9 copy.27
  37.2 1.0 constant_dynamic-update-slice_fusion.10
  38.3 1.6 collective-permute-start.3
  40.2 2.5 collective-permute-start.5
  43.4 2.9 %collective-permute-done.3 = bf16[32,1536]{1,0:T(8,128)(2,1)S(1)} collective-permute-done((bf16[32,1536]{1,0:T(8,128)(2,1)S(1)}, bf16[32,1536]{1,0:T(8,128)(2,1)S(1)}, u32[]{:S(2)}, u32[]{:S(2)}) %collective-permute-start.3) | collective-permute-done | bytes 98336 | tf_op jit(solution)/shard_map/ppermute | solution.py:26
  46.8 4.1 %collective-permute-done.4 = bf16[32,1536]{1,0:T(8,128)(2,1)S(1)} collective-permute-done((bf16[32,1536]{1,0:T(8,128)(2,1)S(1)}, bf16[32,1536]{1,0:T(8,128)(2,1)S(1)}, u32[]{:S(2)}, u32[]{:S(2)}) %collective-permute-start.4) | collective-permute-done | bytes 98336 | tf_op jit(solution)/shard_map/ppermute | solution.py:26
  53.6 12.5 %collective-permute-done.6 = bf16[128,1536]{1,0:T(8,128)(2,1)S(1)} collective-permute-done((bf16[128,1536]{1,0:T(8,128)(2,1)S(1)}, bf16[128,1536]{1,0:T(8,128)(2,1)S(1)}, u32[]{:S(2)}, u32[]{:S(2)}) %collective-permute-start.6) | collective-permute-done | bytes 393248 | tf_op jit(solution)/shard_map/ppermute | solution.py:36
  66.1 1.0 constant_dynamic-update-slice_fusion.6
  67.1 1.9 collective-permute-start.7
  69.0 1.1 subtract_convert_fusion
  70.4 2.3 fusion.9
  72.7 13.6 %collective-permute-done.7 = bf16[256,1536]{1,0:T(8,128)(2,1)} collective-permute-done((bf16[256,1536]{1,0:T(8,128)(2,1)}, bf16[256,1536]{1,0:T(8,128)(2,1)}, u32[]{:S(2)}, u32[]{:S(2)}) %collective-permute-start.7) | collective-permute-done | bytes 786464 | tf_op jit(solution)/shard_map/ppermute | solution.py:40
  86.3 2.1 constant_dynamic-update-slice_fusion.5
  88.4 2.3 fusion.12
  90.7 0.9 fusion.7
  91.6 1.8 collective-permute-start.18
  93.9 1.8 dynamic-slice_dynamic-update-slice_fusion
  95.7 1.8 constant_dynamic-update-slice_fusion.26
  97.5 7.4 %collective-permute-done.21 = bf16[128,1536]{1,0:T(8,128)(2,1)S(1)} collective-permute-done((bf16[128,1536]{1,0:T(8,128)(2,1)}, bf16[128,1536]{1,0:T(8,128)(2,1)S(1)}, u32[]{:S(2)}, u32[]{:S(2)}) %collective-permute-start.21) | collective-permute-done | bytes 393248 | tf_op jit(solution)/shard_map/ppermute | solution.py:36
  105.9 1.7 collective-permute-start.22
  108.7 1.8 constant_dynamic-update-slice_fusion.24
  110.5 6.6 %collective-permute-done.20 = bf16[128,1536]{1,0:T(8,128)(2,1)S(1)} collective-permute-done((bf16[128,1536]{1,0:T(8,128)(2,1)}, bf16[128,1536]{1,0:T(8,128)(2,1)S(1)}, u32[]{:S(2)}, u32[]{:S(2)}) %collective-permute-start.20) | collective-permute-done | bytes 393248 | tf_op jit(solution)/shard_map/ppermute | solution.py:40
  118.4 1.2 constant_dynamic-update-slice_fusion.11
  119.7 3.3 %fusion.102 = (bf16[1024,768]{1,0:T(8,128)(2,1)}, bf16[1024,768]{1,0:T(8,128)(2,1)S(1)}) fusion(bf16[1024,1536]{1,0:T(8,128)(2,1)} %constant_dynamic-update-slice_fusion.11), kind=kLoop, calls=%fused_computation.196 | loop fusion | bytes 6291456 | tf_op jit(solution)/shard_map/slice | solution.py:251
  122.9 1.6 copy.25
  124.6 1.9 copy.26
  126.5 9.2 %bitcast_reduce_fusion = (f32[256,8,2]{0,2,1:T(2,128)S(1)}, f32[8,1024,256,2]{2,1,3,0:T(8,128)}) fusion(bf16[1024,8,96,1]{0,2,3,1:T(8,128)(2,1)S(1)} %bitcast.126, bf16[256,8,2,48]{0,3,2,1:T(8,128)(2,1)} %bitcast.137, bf16[256,8,2,48]{0,3,2,1:T(8,128)(2,1)S(1)} %bitcast.135), kind=kOutput, calls=%fused_computation.1 | convolution fusion | flops 815263744 | bytes 19152896 | tf_op jit(solution)/shard_map/rkgd,nkd->rkgn/dot_general | solution.py:258
  135.8 8.7 %fusion.1 = f32[256,8,2]{0,2,1:T(2,128)S(1)} fusion(f32[8,1024,256,2]{2,1,3,0:T(8,128)} %get-tuple-element.51, f32[256,8,2]{0,2,1:T(2,128)S(1)} %broadcast_maximum_fusion.1), kind=kLoop, calls=%fused_computation.3 | loop fusion | flops 12578816 | bytes 16809984 | tf_op jit(solution)/shard_map/reduce_sum | solution.py:142
  144.6 9.4 %fusion.27 = bf16[256,8,2,96]{0,3,2,1:T(8,128)(2,1)S(1)} fusion(f32[8,96,256,2]{2,1,3,0:T(8,128)} %fusion.12, bf16[1024,8,96,1]{0,2,3,1:T(8,128)(2,1)S(1)} %bitcast.132, f32[8,1024,256,2]{2,1,3,0:T(8,128)} %get-tuple-element.51, f32[256,8,2]{0,2,1:T(2,128)S(1)} %broadcast_maximum_fusion.1, f32[256,8,2]{0,2,1:T(2,128)S(1)} %get-tuple-element.10, ...), kind=kOutput, calls=%fused_computation.39 | convolution fusion | flops 819855360 | bytes 20774912 | tf_op jit(solution)/shard_map/rkgn,nkd->rkgd/dot_general | solution.py:143
  154.0 1.5 multiply_reduce_fusion
  156.7 1.6 collective-permute-start.23
  158.7 1.0 slice.245
  159.7 1.7 collective-permute-start.15
  161.5 1.0 slice.246
  163.1 0.9 constant_dynamic-update-slice_fusion.21
  164.1 21.7 %collective-permute-done.15 = bf16[768,256]{1,0:T(8,128)(2,1)S(1)} collective-permute-done((bf16[768,256]{1,0:T(8,128)(2,1)S(1)}, bf16[768,256]{1,0:T(8,128)(2,1)S(1)}, u32[]{:S(2)}, u32[]{:S(2)}) %collective-permute-start.15) | collective-permute-done | bytes 393248 | tf_op jit(solution)/shard_map/ppermute | solution.py:40
  185.9 5.8 %collective-permute-start.25 = (bf16[256,1536]{1,0:T(8,128)(2,1)S(1)}, bf16[256,1536]{1,0:T(8,128)(2,1)S(1)}, u32[]{:S(2)}, u32[]{:S(2)}) collective-permute-start(bf16[256,1536]{1,0:T(8,128)(2,1)S(1)} %multiply_convert_fusion), channel_id=1, source_target_pairs={{0,2},{1,3},{2,0},{3,1},{4,6},{5,7},{6,4},{7,5},{8,10},{9,11},{10,... | collective-permute-start | bytes 2359304 | tf_op jit(solution)/shard_map/ppermute | solution.py:26
  193.1 1.8 fusion.98
  195.9 1.8 fusion.96
  197.8 1.8 fusion.95
  199.5 8.3 %collective-permute-done.25 = bf16[256,1536]{1,0:T(8,128)(2,1)S(1)} collective-permute-done((bf16[256,1536]{1,0:T(8,128)(2,1)S(1)}, bf16[256,1536]{1,0:T(8,128)(2,1)S(1)}, u32[]{:S(2)}, u32[]{:S(2)}) %collective-permute-start.25) | collective-permute-done | bytes 786464 | tf_op jit(solution)/shard_map/ppermute | solution.py:26
  208.0 1.8 fusion.94
  212.5 1.8 fusion.104
  215.1 1.8 fusion.106
  216.9 1.8 fusion.107
  218.8 1.8 fusion.108
  220.7 1.8 fusion.110
  223.4 1.8 fusion.103
  225.2 1.1 slice.423
  226.3 1.1 fusion.21
  227.4 1.7 collective-permute-start.28
  229.1 1.6 copy.36
  230.8 16.9 %collective-permute-done.28 = bf16[256,1536]{1,0:T(8,128)(2,1)} collective-permute-done((bf16[256,1536]{1,0:T(8,128)(2,1)}, bf16[256,1536]{1,0:T(8,128)(2,1)}, u32[]{:S(2)}, u32[]{:S(2)}) %collective-permute-start.28) | collective-permute-done | bytes 786464 | tf_op jit(solution)/shard_map/ppermute | solution.py:26
  247.6 2.7 %fusion.24 = bf16[256,1536]{1,0:T(8,128)(2,1)} fusion(f32[256,1536]{1,0:T(8,128)S(1)} %get-tuple-element.53, f32[512,1536]{1,0:T(8,128)S(1)} %copy-done.4, bf16[256,1536]{1,0:T(8,128)(2,1)} %collective-permute-done.28, bf16[256,1536]{1,0:T(8,128)(2,1)} %collective-permute-done.24), kind=kLoop, calls=%fused_computation.34 | loop fusion | flops 2359296 | bytes 5505024 | tf_op jit(solution)/shard_map/convert_element_type | solution.py:275
  (181 shorter events, 25.3 us)
Async XLA Ops:
  3.0 15.4 %copy-start.6 = (bf16[1536,128]{1,0:T(8,128)(2,1)}, bf16[1536,128]{1,0:T(8,128)(2,1)S(1)}, u32[]{:S(2)}) copy-start(bf16[1536,128]{1,0:T(8,128)(2,1)S(1)} %get-tuple-element.16) | copy-start | bytes 1179652
  3.1 15.4 %copy-start.8 = (bf16[1536,128]{1,0:T(8,128)(2,1)}, bf16[1536,128]{1,0:T(8,128)(2,1)S(1)}, u32[]{:S(2)}) copy-start(bf16[1536,128]{1,0:T(8,128)(2,1)S(1)} %get-tuple-element.18) | copy-start | bytes 1179652
  3.1 6.7 %copy-start.23 = (bf16[1,128,1536]{2,1,0:T(8,128)(2,1)S(1)}, bf16[1,128,1536]{2,1,0:T(8,128)(2,1)}, u32[]{:S(2)}) copy-start(bf16[1,128,1536]{2,1,0:T(8,128)(2,1)} %param.17) | copy-start | bytes 1179652
  3.1 9.2 %copy-start.29 = (f32[2,1536]{1,0:T(2,128)S(1)}, f32[2,1536]{1,0:T(2,128)}, u32[]{:S(2)}) copy-start(f32[2,1536]{1,0:T(2,128)} %param.12) | copy-start | bytes 36868
  3.1 9.9 %copy-start = (bf16[256,1536]{1,0:T(8,128)(2,1)S(1)}, bf16[256,1536]{1,0:T(8,128)(2,1)}, u32[]{:S(2)}) copy-start(bf16[256,1536]{1,0:T(8,128)(2,1)} %param.10) | copy-start | bytes 2359300
  4.2 152.6 %collective-permute-start.10 = (bf16[1536,256]{1,0:T(8,128)(2,1)}, bf16[1536,256]{1,0:T(8,128)(2,1)}, u32[]{:S(2)}, u32[]{:S(2)}) collective-permute-start(bf16[1536,256]{1,0:T(8,128)(2,1)} %pad_maximum_fusion.2), channel_id=1, source_target_pairs={{0,1},{1,0},{2,3},{3,2},{4,5},{5,4},{6,7},{7,6},{8,9},{9,8},{10,11... | collective-permute-start | bytes 2359304 | tf_op jit(solution)/shard_map/ppermute | solution.py:36
  7.1 98.8 %collective-permute-start.12 = (bf16[1536,256]{1,0:T(8,128)(2,1)}, bf16[1536,256]{1,0:T(8,128)(2,1)}, u32[]{:S(2)}, u32[]{:S(2)}) collective-permute-start(bf16[1536,256]{1,0:T(8,128)(2,1)} %pad_maximum_fusion.2), channel_id=1, source_target_pairs={{0,4},{1,5},{2,6},{3,7},{4,0},{5,1},{6,2},{7,3},{8,12},{9,13},{10,... | collective-permute-start | bytes 2359304 | tf_op jit(solution)/shard_map/ppermute | solution.py:26
  10.4 26.8 %collective-permute-start = (bf16[32,1536]{1,0:T(8,128)(2,1)}, bf16[32,1536]{1,0:T(8,128)(2,1)}, u32[]{:S(2)}, u32[]{:S(2)}) collective-permute-start(bf16[32,1536]{1,0:T(8,128)(2,1)} %get-tuple-element.32), channel_id=1, source_target_pairs={{0,24},{8,16},{16,8},{24,0},{1,25},{9,17},{17,9},{25,1},{2,26},{10... | collective-permute-start | bytes 294920 | tf_op jit(solution)/shard_map/ppermute | solution.py:40
  10.8 26.4 %collective-permute-start.1 = (bf16[32,1536]{1,0:T(8,128)(2,1)}, bf16[32,1536]{1,0:T(8,128)(2,1)}, u32[]{:S(2)}, u32[]{:S(2)}) collective-permute-start(bf16[32,1536]{1,0:T(8,128)(2,1)} %get-tuple-element.31), channel_id=1, source_target_pairs={{0,16},{8,24},{16,0},{24,8},{1,17},{9,25},{17,1},{25,9},{2,18},{10... | collective-permute-start | bytes 294920 | tf_op jit(solution)/shard_map/ppermute | solution.py:40
  12.0 25.3 %collective-permute-start.2 = (bf16[32,1536]{1,0:T(8,128)(2,1)}, bf16[32,1536]{1,0:T(8,128)(2,1)}, u32[]{:S(2)}, u32[]{:S(2)}) collective-permute-start(bf16[32,1536]{1,0:T(8,128)(2,1)} %get-tuple-element.30), channel_id=1, source_target_pairs={{0,8},{8,0},{16,24},{24,16},{1,9},{9,1},{17,25},{25,17},{2,10},{10... | collective-permute-start | bytes 294920 | tf_op jit(solution)/shard_map/ppermute | solution.py:40
  18.4 1.6 copy-start.2
  18.4 0.7 copy-start.28
  20.9 0.7 copy-start.15
  20.9 0.8 copy-start.16
  21.6 0.9 copy-start.32
  24.7 204.5 %all-to-all-start = ((bf16[4,8,16,1536]{3,1,2,0:T(8,128)(2,1)}), bf16[4,8,16,1536]{3,1,2,0:T(8,128)(2,1)S(1)}, u32[]{:S(2)}, u32[]{:S(2)}) async-start(bf16[4,8,16,1536]{3,1,2,0:T(8,128)(2,1)} %convolution_convert_fusion), calls=%async_computation | async-start | bytes 3145728 | tf_op jit(solution)/shard_map/all_to_all | solution.py:298
  30.2 2.7 %copy-start.33 = (s32[8]{0:T(128)S(1)}, s32[8]{0:T(128)}, u32[]{:S(2)}) copy-start(s32[8]{0:T(128)} %param.18) | copy-start | bytes 100
  38.3 8.1 %collective-permute-start.3 = (bf16[32,1536]{1,0:T(8,128)(2,1)S(1)}, bf16[32,1536]{1,0:T(8,128)(2,1)S(1)}, u32[]{:S(2)}, u32[]{:S(2)}) collective-permute-start(bf16[32,1536]{1,0:T(8,128)(2,1)S(1)} %get-tuple-element.14), channel_id=1, source_target_pairs={{0,2},{1,3},{2,0},{3,1},{4,6},{5,7},{6,4},{7,5},{8,10},{9,11},{10,... | collective-permute-start | bytes 294920 | tf_op jit(solution)/shard_map/ppermute | solution.py:26
  39.9 11.1 %collective-permute-start.4 = (bf16[32,1536]{1,0:T(8,128)(2,1)S(1)}, bf16[32,1536]{1,0:T(8,128)(2,1)S(1)}, u32[]{:S(2)}, u32[]{:S(2)}) collective-permute-start(bf16[32,1536]{1,0:T(8,128)(2,1)S(1)} %get-tuple-element.14), channel_id=1, source_target_pairs={{0,4},{1,5},{2,6},{3,7},{4,0},{5,1},{6,2},{7,3},{8,12},{9,13},{10,... | collective-permute-start | bytes 294920 | tf_op jit(solution)/shard_map/ppermute | solution.py:26
  40.2 10.8 %collective-permute-start.5 = (bf16[32,1536]{1,0:T(8,128)(2,1)S(1)}, bf16[32,1536]{1,0:T(8,128)(2,1)S(1)}, u32[]{:S(2)}, u32[]{:S(2)}) collective-permute-start(bf16[32,1536]{1,0:T(8,128)(2,1)S(1)} %get-tuple-element.14), channel_id=1, source_target_pairs={{0,6},{1,7},{2,4},{3,5},{4,2},{5,3},{6,0},{7,1},{8,14},{9,15},{10,... | collective-permute-start | bytes 294920 | tf_op jit(solution)/shard_map/ppermute | solution.py:26
  46.3 45.3 %collective-permute-start.17 = (bf16[128,1536]{1,0:T(8,128)(2,1)}, bf16[128,1536]{1,0:T(8,128)(2,1)}, u32[]{:S(2)}, u32[]{:S(2)}) collective-permute-start(bf16[128,1536]{1,0:T(8,128)(2,1)} %get-tuple-element.9), channel_id=1, source_target_pairs={{0,1},{1,0},{2,3},{3,2},{4,5},{5,4},{6,7},{7,6},{8,9},{9,8},{10,11... | collective-permute-start | bytes 1179656 | tf_op jit(solution)/shard_map/ppermute | solution.py:36
  51.0 42.4 %collective-permute-start.19 = (bf16[128,1536]{1,0:T(8,128)(2,1)}, bf16[128,1536]{1,0:T(8,128)(2,1)}, u32[]{:S(2)}, u32[]{:S(2)}) collective-permute-start(bf16[128,1536]{1,0:T(8,128)(2,1)} %get-tuple-element.9), channel_id=1, source_target_pairs={{0,4},{1,5},{2,6},{3,7},{4,0},{5,1},{6,2},{7,3},{8,12},{9,13},{10,... | collective-permute-start | bytes 1179656 | tf_op jit(solution)/shard_map/ppermute | solution.py:26
  51.0 17.9 %copy-start.18 = (f32[256,48]{0,1:T(8,128)S(1)}, f32[256,48]{0,1:T(8,128)}, u32[]{:S(2)}) copy-start(f32[256,48]{0,1:T(8,128)} %copy-done.17) | copy-start | bytes 147460
  51.0 17.9 %copy-start.20 = (f32[256,48]{0,1:T(8,128)S(1)}, f32[256,48]{0,1:T(8,128)}, u32[]{:S(2)}) copy-start(f32[256,48]{0,1:T(8,128)} %copy-done.19) | copy-start | bytes 147460
  51.0 15.1 %collective-permute-start.6 = (bf16[128,1536]{1,0:T(8,128)(2,1)S(1)}, bf16[128,1536]{1,0:T(8,128)(2,1)S(1)}, u32[]{:S(2)}, u32[]{:S(2)}) collective-permute-start(bf16[128,1536]{1,0:T(8,128)(2,1)S(1)} %pad_maximum_fusion.8), channel_id=1, source_target_pairs={{0,1},{1,0},{2,3},{3,2},{4,5},{5,4},{6,7},{7,6},{8,9},{9,8},{10,11... | collective-permute-start | bytes 1179656 | tf_op jit(solution)/shard_map/ppermute | solution.py:36
  67.1 1.9 copy-start.30
  67.1 19.2 %collective-permute-start.7 = (bf16[256,1536]{1,0:T(8,128)(2,1)}, bf16[256,1536]{1,0:T(8,128)(2,1)}, u32[]{:S(2)}, u32[]{:S(2)}) collective-permute-start(bf16[256,1536]{1,0:T(8,128)(2,1)} %get-tuple-element.29), channel_id=1, source_target_pairs={{0,16},{8,24},{16,0},{24,8},{1,17},{9,25},{17,1},{25,9},{2,18},{10... | collective-permute-start | bytes 2359304 | tf_op jit(solution)/shard_map/ppermute | solution.py:40
  70.4 15.9 %copy-start.31 = (bf16[512,1536]{1,0:T(8,128)(2,1)S(1)}, bf16[512,1536]{1,0:T(8,128)(2,1)}, u32[]{:S(2)}) copy-start(bf16[512,1536]{1,0:T(8,128)(2,1)} %copy-done.30) | copy-start | bytes 4718596
  72.7 15.7 %copy-start.24 = (f32[256,8,2]{0,2,1:T(2,128)}, f32[256,8,2]{0,2,1:T(2,128)S(1)}, u32[]{:S(2)}) copy-start(f32[256,8,2]{0,2,1:T(2,128)S(1)} %get-tuple-element.48) | copy-start | bytes 49156
  88.4 30.0 %collective-permute-start.8 = (bf16[512,1536]{1,0:T(8,128)(2,1)S(1)}, bf16[512,1536]{1,0:T(8,128)(2,1)S(1)}, u32[]{:S(2)}, u32[]{:S(2)}) collective-permute-start(bf16[512,1536]{1,0:T(8,128)(2,1)S(1)} %get-tuple-element.25), channel_id=1, source_target_pairs={{0,8},{8,0},{16,24},{24,16},{1,9},{9,1},{17,25},{25,17},{2,10},{10... | collective-permute-start | bytes 4718600 | tf_op jit(solution)/shard_map/ppermute | solution.py:40
  91.6 16.0 %collective-permute-start.18 = (bf16[128,1536]{1,0:T(8,128)(2,1)}, bf16[128,1536]{1,0:T(8,128)(2,1)S(1)}, u32[]{:S(2)}, u32[]{:S(2)}) collective-permute-start(bf16[128,1536]{1,0:T(8,128)(2,1)} %collective-permute-done.17), channel_id=1, source_target_pairs={{0,16},{8,24},{16,0},{24,8},{1,17},{9,25},{17,1},{25,9},{2,18},{10... | collective-permute-start | bytes 1179656 | tf_op jit(solution)/shard_map/ppermute | solution.py:40
  93.4 11.5 %collective-permute-start.21 = (bf16[128,1536]{1,0:T(8,128)(2,1)}, bf16[128,1536]{1,0:T(8,128)(2,1)S(1)}, u32[]{:S(2)}, u32[]{:S(2)}) collective-permute-start(bf16[128,1536]{1,0:T(8,128)(2,1)} %collective-permute-done.19), channel_id=1, source_target_pairs={{0,1},{1,0},{2,3},{3,2},{4,5},{5,4},{6,7},{7,6},{8,9},{9,8},{10,11... | collective-permute-start | bytes 1179656 | tf_op jit(solution)/shard_map/ppermute | solution.py:36
  104.9 13.6 %copy-start.11 = (bf16[128,1536]{1,0:T(8,128)(2,1)}, bf16[128,1536]{1,0:T(8,128)(2,1)S(1)}, u32[]{:S(2)}) copy-start(bf16[128,1536]{1,0:T(8,128)(2,1)S(1)} %collective-permute-done.21) | copy-start | bytes 1179652
  104.9 12.3 %collective-permute-start.20 = (bf16[128,1536]{1,0:T(8,128)(2,1)}, bf16[128,1536]{1,0:T(8,128)(2,1)S(1)}, u32[]{:S(2)}, u32[]{:S(2)}) collective-permute-start(bf16[128,1536]{1,0:T(8,128)(2,1)} %collective-permute-done.19), channel_id=1, source_target_pairs={{0,16},{8,24},{16,0},{24,8},{1,17},{9,25},{17,1},{25,9},{2,18},{10... | collective-permute-start | bytes 1179656 | tf_op jit(solution)/shard_map/ppermute | solution.py:40
  105.9 56.6 %collective-permute-start.22 = (bf16[64,1536]{1,0:T(8,128)(2,1)}, bf16[64,1536]{1,0:T(8,128)(2,1)}, u32[]{:S(2)}, u32[]{:S(2)}) collective-permute-start(bf16[64,1536]{1,0:T(8,128)(2,1)} %slice.249), channel_id=1, source_target_pairs={{0,16},{8,24},{16,0},{24,8},{1,17},{9,25},{17,1},{25,9},{2,18},{10... | collective-permute-start | bytes 589832 | tf_op jit(solution)/shard_map/ppermute | solution.py:40
  107.6 52.1 %collective-permute-start.13 = (bf16[1536,256]{1,0:T(8,128)(2,1)}, bf16[1536,256]{1,0:T(8,128)(2,1)}, u32[]{:S(2)}, u32[]{:S(2)}) collective-permute-start(bf16[1536,256]{1,0:T(8,128)(2,1)} %collective-permute-done.12), channel_id=1, source_target_pairs={{0,16},{8,24},{16,0},{24,8},{1,17},{9,25},{17,1},{25,9},{2,18},{10... | collective-permute-start | bytes 2359304 | tf_op jit(solution)/shard_map/ppermute | solution.py:40
  117.1 1.3 copy-start.13
  117.1 41.2 %collective-permute-start.14 = (bf16[1536,256]{1,0:T(8,128)(2,1)}, bf16[1536,256]{1,0:T(8,128)(2,1)}, u32[]{:S(2)}, u32[]{:S(2)}) collective-permute-start(bf16[1536,256]{1,0:T(8,128)(2,1)} %collective-permute-done.12), channel_id=1, source_target_pairs={{0,1},{1,0},{2,3},{3,2},{4,5},{5,4},{6,7},{7,6},{8,9},{9,8},{10,11... | collective-permute-start | bytes 2359304 | tf_op jit(solution)/shard_map/ppermute | solution.py:36
  124.6 2.0 copy-start.10
  135.7 8.7 %copy-start.25 = (f32[256,8,2]{0,2,1:T(2,128)S(1)}, f32[256,8,2]{0,2,1:T(2,128)}, u32[]{:S(2)}) copy-start(f32[256,8,2]{0,2,1:T(2,128)} %copy-done.24) | copy-start | bytes 49156
  135.8 8.8 %copy-start.5 = (bf16[1024,768]{0,1:T(8,128)(2,1)S(1)}, bf16[1024,768]{0,1:T(8,128)(2,1)}, u32[]{:S(2)}) copy-start(bf16[1024,768]{0,1:T(8,128)(2,1)} %copy.25) | copy-start | bytes 4718596
  135.8 18.2 %slice-start = ((s8[4718592]{0:T(1024)(128)(4,1)}), s8[524288]{0:T(1024)(128)(4,1)S(1)}, s32[]{:S(2)}) async-start(s8[4718592]{0:T(1024)(128)(4,1)} %bitcast.124), calls=%async_computation.1 | async-start | bytes 1048576
  144.5 9.4 %slice-start.1 = ((s8[4718592]{0:T(1024)(128)(4,1)}), s8[4194304]{0:T(1024)(128)(4,1)S(1)}, s32[]{:S(2)}) async-start(s8[4718592]{0:T(1024)(128)(4,1)} %bitcast.124), calls=%async_computation.2 | async-start | bytes 8388608
  144.6 9.4 %copy-start.1 = (bf16[256,1536]{1,0:T(8,128)(2,1)S(1)}, bf16[256,1536]{1,0:T(8,128)(2,1)}, u32[]{:S(2)}) copy-start(bf16[256,1536]{1,0:T(8,128)(2,1)} %param.10) | copy-start | bytes 2359300
  154.0 1.5 copy-start.27
  154.0 1.9 copy-start.26
  155.5 1.1 copy-start.12
  155.5 1.2 copy-start.14
  155.7 35.9 %collective-permute-start.9 = (bf16[256,1536]{1,0:T(8,128)(2,1)S(1)}, bf16[256,1536]{1,0:T(8,128)(2,1)S(1)}, u32[]{:S(2)}, u32[]{:S(2)}) collective-permute-start(bf16[256,1536]{1,0:T(8,128)(2,1)S(1)} %multiply_convert_fusion), channel_id=1, source_target_pairs={{0,8},{8,0},{16,24},{24,16},{1,9},{9,1},{17,25},{25,17},{2,10},{10... | collective-permute-start | bytes 2359304 | tf_op jit(solution)/shard_map/ppermute | solution.py:40
  156.7 7.3 %collective-permute-start.23 = (bf16[64,1536]{1,0:T(8,128)(2,1)S(1)}, bf16[64,1536]{1,0:T(8,128)(2,1)S(1)}, u32[]{:S(2)}, u32[]{:S(2)}) collective-permute-start(bf16[64,1536]{1,0:T(8,128)(2,1)S(1)} %slice.250), channel_id=1, source_target_pairs={{0,1},{1,0},{2,3},{3,2},{4,5},{5,4},{6,7},{7,6},{8,9},{9,8},{10,11... | collective-permute-start | bytes 589832 | tf_op jit(solution)/shard_map/ppermute | solution.py:36
  158.3 36.9 %collective-permute-start.11 = (bf16[1536,256]{1,0:T(8,128)(2,1)}, bf16[1536,256]{1,0:T(8,128)(2,1)S(1)}, u32[]{:S(2)}, u32[]{:S(2)}) collective-permute-start(bf16[1536,256]{1,0:T(8,128)(2,1)} %collective-permute-done.10), channel_id=1, source_target_pairs={{0,16},{8,24},{16,0},{24,8},{1,17},{9,25},{17,1},{25,9},{2,18},{10... | collective-permute-start | bytes 2359304 | tf_op jit(solution)/shard_map/ppermute | solution.py:40
  159.7 32.0 %copy-start.7 = (bf16[1536,128]{1,0:T(8,128)(2,1)S(1)}, bf16[1536,128]{1,0:T(8,128)(2,1)}, u32[]{:S(2)}) copy-start(bf16[1536,128]{1,0:T(8,128)(2,1)} %copy-done.6) | copy-start | bytes 1179652
  159.7 32.0 %copy-start.9 = (bf16[1536,128]{1,0:T(8,128)(2,1)S(1)}, bf16[1536,128]{1,0:T(8,128)(2,1)}, u32[]{:S(2)}) copy-start(bf16[1536,128]{1,0:T(8,128)(2,1)} %copy-done.8) | copy-start | bytes 1179652
  159.7 26.0 %collective-permute-start.15 = (bf16[768,256]{1,0:T(8,128)(2,1)S(1)}, bf16[768,256]{1,0:T(8,128)(2,1)S(1)}, u32[]{:S(2)}, u32[]{:S(2)}) collective-permute-start(bf16[768,256]{1,0:T(8,128)(2,1)S(1)} %slice.245), channel_id=1, source_target_pairs={{0,16},{8,24},{16,0},{24,8},{1,17},{9,25},{17,1},{25,9},{2,18},{10... | collective-permute-start | bytes 1179656 | tf_op jit(solution)/shard_map/ppermute | solution.py:40
  162.5 23.3 %collective-permute-start.16 = (bf16[768,256]{1,0:T(8,128)(2,1)S(1)}, bf16[768,256]{1,0:T(8,128)(2,1)S(1)}, u32[]{:S(2)}, u32[]{:S(2)}) collective-permute-start(bf16[768,256]{1,0:T(8,128)(2,1)S(1)} %slice.246), channel_id=1, source_target_pairs={{0,1},{1,0},{2,3},{3,2},{4,5},{5,4},{6,7},{7,6},{8,9},{9,8},{10,11... | collective-permute-start | bytes 1179656 | tf_op jit(solution)/shard_map/ppermute | solution.py:36
  185.9 6.5 %copy-start.21 = (bf16[1536,128]{1,0:T(8,128)(2,1)S(1)}, bf16[1536,128]{1,0:T(8,128)(2,1)}, u32[]{:S(2)}) copy-start(bf16[1536,128]{1,0:T(8,128)(2,1)} %get-tuple-element.15) | copy-start | bytes 1179652
  185.9 6.5 %copy-start.22 = (bf16[1536,128]{1,0:T(8,128)(2,1)S(1)}, bf16[1536,128]{1,0:T(8,128)(2,1)}, u32[]{:S(2)}) copy-start(bf16[1536,128]{1,0:T(8,128)(2,1)} %get-tuple-element.17) | copy-start | bytes 1179652
  185.9 22.0 %collective-permute-start.25 = (bf16[256,1536]{1,0:T(8,128)(2,1)S(1)}, bf16[256,1536]{1,0:T(8,128)(2,1)S(1)}, u32[]{:S(2)}, u32[]{:S(2)}) collective-permute-start(bf16[256,1536]{1,0:T(8,128)(2,1)S(1)} %multiply_convert_fusion), channel_id=1, source_target_pairs={{0,2},{1,3},{2,0},{3,1},{4,6},{5,7},{6,4},{7,5},{8,10},{9,11},{10,... | collective-permute-start | bytes 2359304 | tf_op jit(solution)/shard_map/ppermute | solution.py:26
  207.8 2.5 %collective-permute-start.26 = (bf16[256,1536]{1,0:T(8,128)(2,1)S(1)}, bf16[256,1536]{1,0:T(8,128)(2,1)S(1)}, u32[]{:S(2)}, u32[]{:S(2)}) collective-permute-start(bf16[256,1536]{1,0:T(8,128)(2,1)S(1)} %collective-permute-done.25), channel_id=1, source_target_pairs={{0,8},{8,0},{16,24},{24,16},{1,9},{9,1},{17,25},{25,17},{2,10},{10... | collective-permute-start | bytes 2359304 | tf_op jit(solution)/shard_map/ppermute | solution.py:40
  222.6 3.7 %collective-permute-start.27 = (bf16[256,1536]{1,0:T(8,128)(2,1)S(1)}, bf16[256,1536]{1,0:T(8,128)(2,1)S(1)}, u32[]{:S(2)}, u32[]{:S(2)}) collective-permute-start(bf16[256,1536]{1,0:T(8,128)(2,1)S(1)} %slice.422), channel_id=1, source_target_pairs={{0,8},{8,0},{16,24},{24,16},{1,9},{9,1},{17,25},{25,17},{2,10},{10... | collective-permute-start | bytes 2359304 | tf_op jit(solution)/shard_map/ppermute | solution.py:40
  225.2 2.2 copy-start.3
  226.3 4.5 %collective-permute-start.24 = (bf16[256,1536]{1,0:T(8,128)(2,1)}, bf16[256,1536]{1,0:T(8,128)(2,1)}, u32[]{:S(2)}, u32[]{:S(2)}) collective-permute-start(bf16[256,1536]{1,0:T(8,128)(2,1)} %slice.423), channel_id=1, source_target_pairs={{0,8},{8,0},{16,24},{24,16},{1,9},{9,1},{17,25},{25,17},{2,10},{10... | collective-permute-start | bytes 2359304 | tf_op jit(solution)/shard_map/ppermute | solution.py:40
  227.4 20.3 %collective-permute-start.28 = (bf16[256,1536]{1,0:T(8,128)(2,1)}, bf16[256,1536]{1,0:T(8,128)(2,1)}, u32[]{:S(2)}, u32[]{:S(2)}) collective-permute-start(bf16[256,1536]{1,0:T(8,128)(2,1)} %fusion.21), channel_id=1, source_target_pairs={{0,2},{1,3},{2,0},{3,1},{4,6},{5,7},{6,4},{7,5},{8,10},{9,11},{10,... | collective-permute-start | bytes 2359304 | tf_op jit(solution)/shard_map/ppermute | solution.py:26
  229.1 18.5 %copy-start.4 = (f32[512,1536]{1,0:T(8,128)S(1)}, f32[512,1536]{1,0:T(8,128)}, u32[]{:S(2)}) copy-start(f32[512,1536]{1,0:T(8,128)} %copy-done.3) | copy-start | bytes 9437188
  (2 other events, 1.3 us)

commit v2 on v1

--- a/solution.py
+++ b/solution.py
@@ -1,6 +1,10 @@
+import functools
+
 import jax
 import jax.numpy as jnp
 from jax import lax
+from jax.experimental import pallas as pl
+from jax.experimental.pallas import tpu as pltpu
 from jax.sharding import PartitionSpec as P
 
 QUERY_HEADS = 16
@@ -13,6 +17,7 @@
 ROPE_BASE = 100000.0
 EPSILON = 1e-05
 NEGATIVE_FILLER = -1e30
+LOG2_E = 1.4426950408889634
 
 
 Z_SIZE = 4
@@ -53,12 +58,15 @@
     line = jnp.concatenate(
         [quarter] + [tensor_xor(quarter, tensor_count, bits) for bits in range(1, Z_SIZE)]
     )
-    plane = jnp.concatenate(
-        [line] + [tensor_turn(line, tensor_count, step) for step in range(1, width)]
-    )
-    across = group_xor(plane, group_count, 2)
-    own_rows = jnp.concatenate([plane, across])
-    return [own_rows, group_xor(own_rows, group_count, 1)]
+    across = group_xor(line, group_count, 2)
+    half = line.shape[0] // 2
+    beside = [tensor_turn(line, tensor_count, step) for step in range(1, width)]
+    corner = []
+    for step in range(1, width):
+        corner.append(group_xor(beside[step - 1][:half], group_count, 2))
+        corner.append(tensor_turn(across[half:], tensor_count, step))
+    pieces = [line, across] + beside + corner
+    return pieces + [group_xor(piece, group_count, 1) for piece in pieces], quarter
 
 
 def gather_weights(w_in, w_down, group_count, tensor_count):
@@ -110,23 +118,6 @@
     )
 
 
-def apply_rotary(head_values, locate_position):
-    half_dim = head_values.shape[-1] // 2
-    frequency = ROPE_BASE ** (-jnp.arange(half_dim, dtype=jnp.float32) / half_dim)
-    angles = locate_position.astype(jnp.float32)[:, None] * frequency[None, :]
-    cosine = jnp.cos(angles)[:, None, :]
-    sine_part = jnp.sin(angles)[:, None, :]
-    first_half = head_values[..., :half_dim]
-    second_half = head_values[..., half_dim:]
-    return jnp.concatenate(
-        [
-            first_half * cosine - second_half * sine_part,
-            second_half * cosine + first_half * sine_part,
-        ],
-        axis=-1,
-    )
-
-
 def positions(segment):
     row_number = segment.shape[0]
     row_index = jnp.arange(row_number, dtype=jnp.int32)
@@ -135,27 +126,135 @@
     return PREFIX_TOKENS + row_index - first_row
 
 
-def attend_update(attn_state, scores, value_head_rows):
-    row_max, row_total, weighted = attn_state
-    new_max = jnp.maximum(row_max, jnp.max(scores, axis=-1))
-    weights = jnp.exp(scores - new_max[..., None])
-    row_total = jnp.sum(weights, axis=-1)
-    weighted = jnp.einsum(
-        "rkgn,nkd->rkgd",
-        weights.astype(jnp.bfloat16),
-        value_head_rows,
-        preferred_element_type=jnp.float32,
-    )
-    return (new_max, row_total, weighted)
-
-
-def combine_states(left_state, right_state):
-    new_max = jnp.maximum(left_state[0], right_state[0])
-    left_factor = jnp.exp(left_state[0] - new_max)
-    right_factor = jnp.exp(right_state[0] - new_max)
-    row_total = left_state[1] * left_factor + right_state[1] * right_factor
-    weighted = left_state[2] * left_factor[..., None] + right_state[2] * right_factor[..., None]
-    return (new_max, row_total, weighted)
+def rotary_tables(locate_position, width):
+    half_dim = HEAD_DIMENSION // 2
+    frequency = ROPE_BASE ** (-jnp.arange(half_dim, dtype=jnp.float32) / half_dim)
+    angles = locate_position.astype(jnp.float32)[:, None] * frequency[None, :]
+    cosine, sine = jnp.cos(angles), jnp.sin(angles)
+    heads = width // HEAD_DIMENSION
+    return jnp.tile(cosine, (1, 2 * heads)), jnp.tile(
+        jnp.concatenate([-sine, sine], axis=1), (1, heads)
+    )
+
+
+def project_kernel(hidden, gain, weight, cosine, sine, *rest):
+    out, normed = rest[-2:]
+    step = pl.program_id(0)
+    width = weight.shape[1]
+    rotated_steps = (QUERY_HEADS + KEY_VALUE_HEADS) * HEAD_DIMENSION // width
+
+    @pl.when(step == 0)
+    def _():
+        normed[...] = rms_norm(hidden[...], gain[...]).astype(jnp.bfloat16)
+
+    projected = jnp.dot(normed[...], weight[...], preferred_element_type=jnp.float32)
+
+    @pl.when(step < rotated_steps)
+    def _():
+        half_dim = HEAD_DIMENSION // 2
+        lane = lax.broadcasted_iota(jnp.int32, projected.shape, 1)
+        swapped = jnp.where(
+            lane % HEAD_DIMENSION < half_dim,
+            pltpu.roll(projected, width - half_dim, 1),
+            pltpu.roll(projected, half_dim, 1),
+        )
+        out[...] = (projected * cosine[...] + swapped * sine[...]).astype(jnp.bfloat16)
+
+    @pl.when(step >= rotated_steps)
+    def _():
+        out[...] = projected.astype(jnp.bfloat16)
+
+
+def project(hidden_in, gain_row, weight, locate_position, earlier):
+    rows, depth = hidden_in.shape
+    columns = weight.shape[1]
+    width = 4 * HEAD_DIMENSION
+    cosine, sine = rotary_tables(locate_position, width)
+    whole = lambda shape: pl.BlockSpec(shape, lambda i: (0, 0))
+    return pl.pallas_call(
+        project_kernel,
+        grid=(columns // width,),
+        in_specs=[
+            whole((rows, depth)),
+            whole((1, depth)),
+            pl.BlockSpec((depth, width), lambda i: (0, i)),
+            whole((rows, width)),
+            whole((rows, width)),
+        ]
+        + [pl.BlockSpec(memory_space=pl.ANY)] * len(earlier),
+        out_specs=pl.BlockSpec((rows, width), lambda i: (0, i)),
+        out_shape=jax.ShapeDtypeStruct((rows, columns), jnp.bfloat16),
+        scratch_shapes=[pltpu.VMEM((rows, depth), jnp.bfloat16)],
+        compiler_params=pltpu.CompilerParams(vmem_limit_bytes=24 << 20),
+        cost_estimate=pl.CostEstimate(
+            flops=2 * rows * depth * columns,
+            bytes_accessed=2 * depth * columns,
+            transcendentals=0,
+        ),
+    )(hidden_in, gain_row[None, :], weight, cosine, sine, *earlier)
+
+
+def attention_kernel(piece_count, row_ids, column_ids, projected, *rest):
+    pieces, out, joined = rest[:piece_count], rest[-2], rest[-1]
+    rows = projected.shape[0]
+    query_columns = QUERY_HEADS * HEAD_DIMENSION
+    key_value_width = KEY_VALUE_HEADS * HEAD_DIMENSION
+    repeats = QUERY_HEADS // KEY_VALUE_HEADS
+    at = 0
+    for piece in pieces:
+        joined[at : at + piece.shape[0], :] = piece[...]
+        at += piece.shape[0]
+    joined[at : at + rows, :] = projected[:, query_columns:]
+    row_index = lax.broadcasted_iota(jnp.int32, (rows, rows), 0)
+    column_index = lax.broadcasted_iota(jnp.int32, (rows, rows), 1)
+    allowed = (row_ids[...] == column_ids[...]) & (column_index <= row_index)
+    allowed = jnp.concatenate([allowed] * repeats, axis=0)
+    scale = HEAD_DIMENSION ** (-0.5) * LOG2_E
+
+    def head_columns(index):
+        return slice(index * HEAD_DIMENSION, (index + 1) * HEAD_DIMENSION)
+
+    for head in range(KEY_VALUE_HEADS):
+        queries = jnp.concatenate(
+            [projected[:, head_columns(head * repeats + g)] for g in range(repeats)], axis=0
+        )
+        keys = joined[:, head_columns(head)]
+        values = joined[:, head_columns(KEY_VALUE_HEADS + head)]
+        scores = lax.dot_general(
+            queries, keys, (((1,), (1,)), ((), ())), preferred_element_type=jnp.float32
+        )
+        scores = jnp.concatenate(
+            [scores[:, :at], jnp.where(allowed, scores[:, at:], NEGATIVE_FILLER)], axis=1
+        )
+        top = jnp.max(scores, axis=1, keepdims=True)
+        weights = jnp.exp2((scores - top) * scale)
+        total = jnp.sum(weights, axis=1, keepdims=True)
+        summed = jnp.dot(
+            weights.astype(jnp.bfloat16), values, preferred_element_type=jnp.float32
+        )
+        attended = (summed / total).astype(jnp.bfloat16)
+        for g in range(repeats):
+            out[:, head_columns(head * repeats + g)] = attended[g * rows : (g + 1) * rows]
+
+
+def attend(segment, projected, pieces, earlier):
+    rows = projected.shape[0]
+    columns = QUERY_HEADS * HEAD_DIMENSION
+    key_count = rows + sum(piece.shape[0] for piece in pieces)
+    vmem = pl.BlockSpec(memory_space=pltpu.VMEM)
+    return pl.pallas_call(
+        functools.partial(attention_kernel, len(pieces)),
+        in_specs=[vmem] * (3 + len(pieces)) + [pl.BlockSpec(memory_space=pl.ANY)] * len(earlier),
+        out_specs=vmem,
+        out_shape=jax.ShapeDtypeStruct((rows, columns), jnp.bfloat16),
+        scratch_shapes=[pltpu.VMEM((key_count, pieces[0].shape[1]), jnp.bfloat16)],
+        compiler_params=pltpu.CompilerParams(vmem_limit_bytes=40 << 20),
+        cost_estimate=pl.CostEstimate(
+            flops=4 * rows * key_count * columns,
+            bytes_accessed=2 * key_count * columns,
+            transcendentals=rows * QUERY_HEADS * key_count,
+        ),
+    )(segment[:, None], segment[None, :], projected, *pieces, *earlier)
 
 
 def expand_with(token_block, gate_and_up):
@@ -198,90 +297,27 @@
 ):
     token_rows = hidden_in.shape[0]
     query_columns = QUERY_HEADS * HEAD_DIMENSION
-    key_value_width = KEY_VALUE_HEADS * HEAD_DIMENSION
     group_count, tensor_count = lax.axis_size("group"), lax.axis_size("tensor")
     pieces = gather_weights(w_in, w_down, group_count, tensor_count)
     segment = request_ids[0]
-    normed = rms_norm(hidden_in, norm_gains[0]).astype(jnp.bfloat16)
-    projected_rows = jnp.dot(normed, query_key_value_weight, preferred_element_type=jnp.float32)
-    locate_position = positions(segment)
-    query_rows = apply_rotary(
-        projected_rows[:, :query_columns].reshape(token_rows, QUERY_HEADS, HEAD_DIMENSION),
-        locate_position,
-    ).astype(jnp.bfloat16)
-    fresh_keys = apply_rotary(
-        projected_rows[:, query_columns : query_columns + key_value_width].reshape(
-            token_rows, KEY_VALUE_HEADS, HEAD_DIMENSION
-        ),
-        locate_position,
-    ).astype(jnp.bfloat16)
-    fresh_values = (
-        projected_rows[:, query_columns + key_value_width :]
-        .reshape(token_rows, KEY_VALUE_HEADS, HEAD_DIMENSION)
-        .astype(jnp.bfloat16)
-    )
-    query_groups = query_rows.reshape(
-        token_rows, KEY_VALUE_HEADS, QUERY_HEADS // KEY_VALUE_HEADS, HEAD_DIMENSION
-    )
-    score_scale = HEAD_DIMENSION ** (-0.5)
-    row_index = jnp.arange(token_rows, dtype=jnp.int32)
-    allowed = (segment[None, :] == segment[:, None]) & (row_index[None, :] <= row_index[:, None])
-    local_scores = (
-        jnp.einsum("rkgd,nkd->rkgn", query_groups, fresh_keys, preferred_element_type=jnp.float32)
-        * score_scale
-    )
-    local_scores = jnp.where(allowed[:, None, None, :], local_scores, NEGATIVE_FILLER)
-    empty_state = (
-        jnp.full(
-            (token_rows, KEY_VALUE_HEADS, QUERY_HEADS // KEY_VALUE_HEADS),
-            NEGATIVE_FILLER,
-            jnp.float32,
-        ),
-        jnp.zeros((token_rows, KEY_VALUE_HEADS, QUERY_HEADS // KEY_VALUE_HEADS), jnp.float32),
-        jnp.zeros(
-            (token_rows, KEY_VALUE_HEADS, QUERY_HEADS // KEY_VALUE_HEADS, HEAD_DIMENSION),
-            jnp.float32,
-        ),
-    )
-    local_state = attend_update(empty_state, local_scores, fresh_values)
-    loaded_pages = jnp.concatenate(
-        gather_prefix(prefix_cache[0], prefix_owner, group_count, tensor_count)
-    )
-    key_total = loaded_pages.shape[0]
-    key_head_rows = loaded_pages[:, :key_value_width].reshape(
-        key_total, KEY_VALUE_HEADS, HEAD_DIMENSION
-    )
-    value_head_rows = loaded_pages[:, key_value_width:].reshape(
-        key_total, KEY_VALUE_HEADS, HEAD_DIMENSION
-    )
-    scores = (
-        jnp.einsum(
-            "rkgd,nkd->rkgn", query_groups, key_head_rows, preferred_element_type=jnp.float32
-        )
-        * score_scale
-    )
-    attn_state = attend_update(empty_state, scores, value_head_rows)
-    attn_state = combine_states(attn_state, local_state)
-    attended = (
-        (attn_state[2] / attn_state[1][..., None])
-        .reshape(token_rows, QUERY_HEADS * HEAD_DIMENSION)
-        .astype(jnp.bfloat16)
-    )
+    prefix_pieces, quarter = gather_prefix(
+        prefix_cache[0], prefix_owner, group_count, tensor_count
+    )
+    projected = project(
+        hidden_in, norm_gains[0], query_key_value_weight, positions(segment), [quarter]
+    )
+    attended = attend(segment, projected, prefix_pieces, [])
     middle = (
         hidden_in.astype(jnp.float32) + jnp.dot(attended, w_out, preferred_element_type=jnp.float32)
     ).astype(jnp.bfloat16)
     second = rms_norm(middle, norm_gains[1]).astype(jnp.bfloat16)
     mlp_out = feed_forward(second, pieces, group_count, tensor_count)
     hidden_out = (middle.astype(jnp.float32) + mlp_out).astype(jnp.bfloat16)
-    cache_rows = jnp.concatenate(
-        [
-            fresh_keys.reshape(token_rows, key_value_width),
-            fresh_values.reshape(token_rows, key_value_width),
-        ],
-        axis=1,
-    )
+    cache_rows = projected[:, query_columns:]
     page_count = page_dest.shape[0]
-    page_blocks = cache_rows.reshape(page_count, token_rows // page_count, 2 * key_value_width)
+    page_blocks = cache_rows.reshape(
+        page_count, token_rows // page_count, cache_rows.shape[1]
+    )
     destination = page_dest[:, 0]
     dest_count = lax.axis_size("group")
     group_iota = jnp.arange(dest_count, dtype=jnp.int32)

time: 251 us -> 191 us (0.76)
  matrix products: 54.2 us -> 19.4 us
  waiting for transfers between devices: 94.1 us -> 72.2 us
  Pallas kernels: 0 us -> 21 us
  local copies, waits for them, and re-layouts: 43 us -> 26.2 us
  other arithmetic: 19.5 us -> 7.78 us
  starting transfers between devices: 36 us -> 40 us
    dot_general x5 -> x0, matrix products: 28.3 us -> none  [the longest x2 11.6 us: attend_update(): jnp.einsum('rkgn,nkd->rkgd', weights.astype(jnp.bfloat16), value_head_row...]
    pallas_call x0 -> x2, Pallas kernels: none -> 21 us  [the longest x1 12.2 us: attend(): pl.pallas_call(functools.partial(attention_kernel, len(pieces)), in_specs...]
    ppermute x15 -> x20, waiting for transfers between devices: 42 us -> 28.4 us  [group_xor(): lax.ppermute(value, 'group', [(g, g ^ bits) for g in range(group_count)])]
    slice x8 -> x3, local copies, waits for them, and re-layouts: 11.7 us -> 0.08 us  [the longest x1 0.05 us: on_device(): cache_rows = projected[:, query_columns:]]
    reduce_sum x3 -> x0, other arithmetic: 9.83 us -> none  [the longest x2 9.6 us: attend_update(): row_total = jnp.sum(weights, axis=-1)]
    dot_general x16, matrix products: 18.9 us -> 12.2 us  [expand_with(): both = jnp.dot(token_block, gate_and_up, preferred_element_type=jnp.float32)]
    ppermute x7, waiting for transfers between devices: 32.3 us -> 26.9 us  [tensor_xor(): return lax.ppermute(value, 'tensor', pairs)]
    concatenate x3 -> x0, local copies, waits for them, and re-layouts: 3.48 us -> none  [the longest x1 2.12 us: gather_prefix(): own_rows = jnp.concatenate([plane, across])]
  transfers between devices with their start and end apart: 30 -> 36, of which waited for: 9 -> 9; matrix products, arithmetic and copies ran while one was open for 43% -> 23% of each run, Pallas kernels for 0% -> 11%
where the time goes in v2:
time: 191 us; the launch traced here: 190 us
  waiting for transfers between devices  72.2 us (38%)
  starting transfers between devices  40 us (21%)
  local copies, waits for them, and re-layouts  26.2 us (14%)
  Pallas kernels  21 us (11%)
  matrix products  19.4 us (10%)
  other arithmetic  7.78 us (4%)
  between operations  3.4 us (2%)
    ppermute x20, waiting for transfers between devices, group_xor(): lax.ppermute(value, 'group', [(g, g ^ bits) for g in range(group_count)])  28.4 us
    ppermute x7, waiting for transfers between devices, tensor_xor(): return lax.ppermute(value, 'tensor', pairs)  26.9 us
    unnamed x53, local copies, waits for them, and re-layouts  19 us
    ppermute x8, waiting for transfers between devices, tensor_turn(): return lax.ppermute(value, 'tensor', pairs)  16.9 us
    ppermute x20, starting transfers between devices, group_xor(): lax.ppermute(value, 'group', [(g, g ^ bits) for g in range(group_count)])  13.4 us
    ppermute x7, starting transfers between devices, tensor_xor(): return lax.ppermute(value, 'tensor', pairs)  12.2 us
    pallas_call x1, Pallas kernels, attend(): pl.pallas_call(functools.partial(attention_kernel, len(pieces)), in_specs...  12.2 us
    dot_general x16, matrix products, expand_with(): both = jnp.dot(token_block, gate_and_up, preferred_element_type=jnp.float32)  12.2 us
  transfers between devices with their start and end apart: 36, of which 9 were waited for; matrix products, arithmetic and copies ran while one was open for 23% of the time, Pallas kernels for 11%

profile of v2, /device:TPU:0, one launch (start us, length us, event | category | flops | bytes accessed | tf_op | source)
XLA Modules:
  0.0 190.0 jit_solution(6462409522642960567)
XLA Ops:
  0.7 1.9 %constant_dynamic-update-slice_fusion.9 = (bf16[1024,1536]{1,0:T(8,128)(2,1)}, bf16[128,1536]{1,0:T(8,128)(2,1)}) fusion(bf16[512,1536]{1,0:T(8,128)(2,1)} %param.16, s32[]{:T(128)S(6)} %select_n.72), kind=kLoop, calls=%fused_computation.94 | loop fusion | bytes 1179652
  2.6 4.0 %collective-permute-start.25 = (bf16[128,1536]{1,0:T(8,128)(2,1)}, bf16[128,1536]{1,0:T(8,128)(2,1)}, u32[]{:S(2)}, u32[]{:S(2)}) collective-permute-start(bf16[128,1536]{1,0:T(8,128)(2,1)} %get-tuple-element.9), channel_id=1, source_target_pairs={{0,4},{1,5},{2,6},{3,7},{4,0},{5,1},{6,2},{7,3},{8,12},{9,13},{10,... | collective-permute-start | bytes 1179656 | tf_op jit(solution)/shard_map/ppermute | solution.py:31
  6.7 1.5 collective-permute-start.23
  8.2 1.0 dynamic-slice_bitcast_fusion.4
  9.3 1.6 collective-permute-start.1
  14.1 0.6 slice_reduce_fusion
  14.7 0.8 copy.23.row_ids
  15.8 1.8 dynamic-slice_dynamic-update-slice_fusion
  17.6 2.4 %dynamic-slice_bitcast_fusion.1 = (bf16[1536,128]{1,0:T(8,128)(2,1)}, bf16[1536,128]{1,0:T(8,128)(2,1)S(1)}, bf16[1536,128]{1,0:T(8,128)(2,1)}, bf16[1536,128]{1,0:T(8,128)(2,1)S(1)}) fusion(bf16[2,1536,512]{2,1,0:T(8,128)(2,1)} %param.15, s32[]{:T(128)S(6)} %select_n.73, s32[]{:T(128)S(6)} %select_n.72, s32[]{:T(128)S(6)} %add.155), kind=kLoop, calls=%fused_computation.22 | loop fusion | bytes 3145740 | tf_op jit(solution)/shard_map/squeeze | solution.py:82
  20.0 1.1 pad_maximum_fusion.1
  21.5 1.0 fusion.43.rest_0_
  22.5 1.4 collective-permute-start.5
  23.9 1.7 collective-permute-start.4
  25.6 1.3 collective-permute-start.3
  27.1 2.9 %collective-permute-done.5 = bf16[32,1536]{1,0:T(8,128)(2,1)S(1)} collective-permute-done((bf16[32,1536]{1,0:T(8,128)(2,1)S(1)}, bf16[32,1536]{1,0:T(8,128)(2,1)S(1)}, u32[]{:S(2)}, u32[]{:S(2)}) %collective-permute-start.5) | collective-permute-done | bytes 98336 | tf_op jit(solution)/shard_map/ppermute | solution.py:31
  30.1 3.4 %collective-permute-start.18 = (bf16[1536,256]{1,0:T(8,128)(2,1)}, bf16[1536,256]{1,0:T(8,128)(2,1)}, u32[]{:S(2)}, u32[]{:S(2)}) collective-permute-start(bf16[1536,256]{1,0:T(8,128)(2,1)} %pad_maximum_fusion.1), channel_id=1, source_target_pairs={{0,4},{1,5},{2,6},{3,7},{4,0},{5,1},{6,2},{7,3},{8,12},{9,13},{10,... | collective-permute-start | bytes 2359304 | tf_op jit(solution)/shard_map/ppermute | solution.py:31
  33.5 1.9 collective-permute-done.4
  35.6 3.7 %copy-done = bf16[1536,3072]{1,0:T(8,128)(2,1)S(1)} copy-done((bf16[1536,3072]{1,0:T(8,128)(2,1)S(1)}, bf16[1536,3072]{1,0:T(8,128)(2,1)}, u32[]{:S(2)}) %copy-start) | copy-done | bytes 9437208
  39.3 8.8 %shard_map.116.projected = bf16[256,3072]{1,0:T(8,128)(2,1)S(1)} custom-call(bf16[256,1536]{1,0:T(8,128)(2,1)S(1)} %copy-done.1, f32[1,1536]{1,0:T(1,128)S(1)} %get-tuple-element.18.gain, bf16[1536,3072]{1,0:T(8,128)(2,1)S(1)} %copy-done, f32[256,384]{1,0:T(8,128)S(1)} %copy.21.cosine, f32[256,384]{1,0:T(8,128)S(1)} %copy.22.sine, ...), custom_call_target="tpu_custom_call" | custom-call | flops 2415919104 | bytes 9437184 | tf_op jit(solution)/shard_map/pallas_call | solution.py:174
  48.2 1.6 collective-permute-start.6
  49.8 1.9 %collective-permute-start.27 = (bf16[128,1536]{1,0:T(8,128)(2,1)}, bf16[128,1536]{1,0:T(8,128)(2,1)}, u32[]{:S(2)}, u32[]{:S(2)}) collective-permute-start(bf16[128,1536]{1,0:T(8,128)(2,1)} %collective-permute-done.25), channel_id=1, source_target_pairs={{0,1},{1,0},{2,3},{3,2},{4,5},{5,4},{6,7},{7,6},{8,9},{9,8},{10,11... | collective-permute-start | bytes 1179656 | tf_op jit(solution)/shard_map/ppermute | solution.py:41
  51.7 0.7 copy-done.3
  53.0 2.1 %convolution_convert_fusion = bf16[4,8,16,1536]{3,1,2,0:T(8,128)(2,1)} fusion(bf16[16,16,1536]{2,1,0:T(8,128)(2,1)S(1)} %bitcast.64, pred[16,8]{0,1:T(8,128)(4,1)S(1)} %iota_compare_fusion.1, pred[16,4]{0,1:T(4,128)(4,1)S(1)} %copy.24), kind=kOutput, calls=%fused_computation | convolution fusion | flops 25952768 | bytes 2359488 | tf_op jit(solution)/shard_map/pdj,pxc->djxc/dot_general | solution.py:331
  55.1 4.7 %all-to-all-start = ((bf16[4,8,16,1536]{3,1,2,0:T(8,128)(2,1)}), bf16[4,8,16,1536]{3,1,2,0:T(8,128)(2,1)}, u32[]{:S(2)}, u32[]{:S(2)}) async-start(bf16[4,8,16,1536]{3,1,2,0:T(8,128)(2,1)} %convolution_convert_fusion), calls=%async_computation | async-start | bytes 3145728 | tf_op jit(solution)/shard_map/all_to_all | solution.py:334
  59.8 1.8 constant_dynamic-update-slice_fusion.8
  61.6 1.9 collective-permute-start.8
  63.7 0.9 slice.218
  64.8 4.0 %collective-permute-done.24 = bf16[128,1536]{1,0:T(8,128)(2,1)} collective-permute-done((bf16[128,1536]{1,0:T(8,128)(2,1)}, bf16[128,1536]{1,0:T(8,128)(2,1)}, u32[]{:S(2)}, u32[]{:S(2)}) %collective-permute-start.24) | collective-permute-done | bytes 393248 | tf_op jit(solution)/shard_map/ppermute | solution.py:45
  68.7 1.8 constant_dynamic-update-slice_fusion.7
  70.6 18.7 %collective-permute-done.8.rest_3_ = bf16[64,1536]{1,0:T(8,128)(2,1)S(1)} collective-permute-done((bf16[64,1536]{1,0:T(8,128)(2,1)S(1)}, bf16[64,1536]{1,0:T(8,128)(2,1)S(1)}, u32[]{:S(2)}, u32[]{:S(2)}) %collective-permute-start.8) | collective-permute-done | bytes 196640 | tf_op jit(solution)/shard_map/ppermute | solution.py:45
  89.8 1.9 %constant_dynamic-update-slice_fusion.6 = bf16[1024,1536]{1,0:T(8,128)(2,1)} fusion(bf16[1024,1536]{1,0:T(8,128)(2,1)} %constant_dynamic-update-slice_fusion.7, bf16[128,1536]{1,0:T(8,128)(2,1)} %collective-permute-done.25), kind=kLoop, calls=%fused_computation.91 | loop fusion | bytes 786432
  91.7 1.9 %collective-permute-start.16 = (bf16[1536,256]{1,0:T(8,128)(2,1)}, bf16[1536,256]{1,0:T(8,128)(2,1)S(1)}, u32[]{:S(2)}, u32[]{:S(2)}) collective-permute-start(bf16[1536,256]{1,0:T(8,128)(2,1)} %pad_maximum_fusion.1), channel_id=1, source_target_pairs={{0,1},{1,0},{2,3},{3,2},{4,5},{5,4},{6,7},{7,6},{8,9},{9,8},{10,11... | collective-permute-start | bytes 2359304 | tf_op jit(solution)/shard_map/ppermute | solution.py:41
  93.6 1.5 collective-permute-start.26
  95.8 1.5 collective-permute-start.19
  97.2 12.2 %shard_map.117 = bf16[256,1536]{1,0:T(8,128)(2,1)S(1)} custom-call(s32[256,1]{1,0:T(8,128)S(1)} %copy-done.2, s32[1,256]{1,0:T(1,128)S(1)} %copy-done.5, bf16[256,3072]{1,0:T(8,128)(2,1)S(1)} %shard_map.116.projected, bf16[128,1536]{1,0:T(8,128)(2,1)S(1)} %pad_maximum_fusion.5.rest_0_, bf16[128,1536]{1,0:T(8,128)(2,1)S(1)} %collective-permute-done.6.rest_1_, ...), custom_call_target="tpu_custom_call" | custom-call | flops 2013265920 | bytes 3932160 | tf_op jit(solution)/shard_map/pallas_call | solution.py:245
  109.5 1.5 multiply_reduce_fusion
  111.6 1.1 constant_dynamic-update-slice_fusion.4
  112.7 2.0 %collective-permute-start.29 = (bf16[64,1536]{1,0:T(8,128)(2,1)S(1)}, bf16[64,1536]{1,0:T(8,128)(2,1)S(1)}, u32[]{:S(2)}, u32[]{:S(2)}) collective-permute-start(bf16[64,1536]{1,0:T(8,128)(2,1)S(1)} %slice.219), channel_id=1, source_target_pairs={{0,1},{1,0},{2,3},{3,2},{4,5},{5,4},{6,7},{7,6},{8,9},{9,8},{10,11... | collective-permute-start | bytes 589832 | tf_op jit(solution)/shard_map/ppermute | solution.py:41
  114.7 1.1 collective-permute-start.17
  115.8 16.9 %collective-permute-done.29 = bf16[64,1536]{1,0:T(8,128)(2,1)S(1)} collective-permute-done((bf16[64,1536]{1,0:T(8,128)(2,1)S(1)}, bf16[64,1536]{1,0:T(8,128)(2,1)S(1)}, u32[]{:S(2)}, u32[]{:S(2)}) %collective-permute-start.29) | collective-permute-done | bytes 196640 | tf_op jit(solution)/shard_map/ppermute | solution.py:41
  132.7 1.6 collective-permute-start.21
  134.3 1.8 collective-permute-start.22
  136.1 0.6 fusion.53
  136.8 0.6 fusion.9
  137.6 0.6 fusion.59
  138.3 1.8 fusion.57
  140.0 3.8 %collective-permute-done.17 = bf16[1536,256]{1,0:T(8,128)(2,1)S(1)} collective-permute-done((bf16[1536,256]{1,0:T(8,128)(2,1)S(1)}, bf16[1536,256]{1,0:T(8,128)(2,1)S(1)}, u32[]{:S(2)}, u32[]{:S(2)}) %collective-permute-start.17) | collective-permute-done | bytes 786464 | tf_op jit(solution)/shard_map/ppermute | solution.py:45
  144.6 0.6 fusion.55
  145.8 5.6 %collective-permute-done.31 = bf16[256,1536]{1,0:T(8,128)(2,1)S(1)} collective-permute-done((bf16[256,1536]{1,0:T(8,128)(2,1)S(1)}, bf16[256,1536]{1,0:T(8,128)(2,1)S(1)}, u32[]{:S(2)}, u32[]{:S(2)}) %collective-permute-start.31) | collective-permute-done | bytes 786464 | tf_op jit(solution)/shard_map/ppermute | solution.py:31
  151.8 2.0 %collective-permute-done.32 = bf16[256,1536]{1,0:T(8,128)(2,1)S(1)} collective-permute-done((bf16[256,1536]{1,0:T(8,128)(2,1)S(1)}, bf16[256,1536]{1,0:T(8,128)(2,1)S(1)}, u32[]{:S(2)}, u32[]{:S(2)}) %collective-permute-start.32) | collective-permute-done | bytes 786464 | tf_op jit(solution)/shard_map/ppermute | solution.py:45
  153.8 0.6 fusion.8
  154.4 0.6 fusion.52
  155.0 0.6 fusion.66
  155.9 0.6 fusion.61
  156.6 0.6 fusion.62
  157.3 1.7 fusion.63
  159.1 0.6 fusion.64
  159.9 0.6 fusion.65
  160.7 1.9 fusion.67
  163.8 1.9 fusion.60
  166.4 0.9 copy-done.6
  167.6 3.2 %copy.26 = bf16[1,1,4,8,16,1536]{5,4,3,2,1,0:T(8,128)(2,1)} copy(bf16[1,1,4,8,16,1536]{5,3,4,2,1,0:T(8,128)(2,1)} %bitcast.18) | data formatting | bytes 3145728
  170.7 16.4 %collective-permute-done.34 = bf16[256,1536]{1,0:T(8,128)(2,1)} collective-permute-done((bf16[256,1536]{1,0:T(8,128)(2,1)S(1)}, bf16[256,1536]{1,0:T(8,128)(2,1)}, u32[]{:S(2)}, u32[]{:S(2)}) %collective-permute-start.34) | collective-permute-done | bytes 786464 | tf_op jit(solution)/shard_map/ppermute | solution.py:31
  187.2 2.8 %fusion.5 = bf16[256,1536]{1,0:T(8,128)(2,1)} fusion(f32[256,1536]{1,0:T(8,128)S(1)} %get-tuple-element.25, f32[512,1536]{1,0:T(8,128)S(1)} %copy-done.7, bf16[256,1536]{1,0:T(8,128)(2,1)} %collective-permute-done.34, bf16[256,1536]{1,0:T(8,128)(2,1)} %collective-permute-done.30), kind=kLoop, calls=%fused_computation.11 | loop fusion | flops 2359296 | bytes 5505024 | tf_op jit(solution)/shard_map/convert_element_type | solution.py:315
  (138 shorter events, 10.2 us)
Async XLA Ops:
  0.6 10.5 %copy-start.18 = (s32[8]{0:T(128)S(1)}, s32[8]{0:T(128)}, u32[]{:S(2)}) copy-start(s32[8]{0:T(128)} %param.18) | copy-start | bytes 100
  0.6 13.1 %copy-start.5 = (s32[1,256]{1,0:T(1,128)S(1)}, s32[1,256]{1,0:T(1,128)}, u32[]{:S(2)}) copy-start(s32[1,256]{1,0:T(1,128)} %column_ids.1) | copy-start | bytes 3076
  0.7 13.3 %copy-start.17 = (s32[16,1]{0,1:T(1,128)S(1)}, s32[16,1]{0,1:T(1,128)}, u32[]{:S(2)}) copy-start(s32[16,1]{0,1:T(1,128)} %param.19) | copy-start | bytes 196
  0.7 13.5 %copy-start.16 = (f32[2,1536]{1,0:T(2,128)S(1)}, f32[2,1536]{1,0:T(2,128)}, u32[]{:S(2)}) copy-start(f32[2,1536]{1,0:T(2,128)} %param.12) | copy-start | bytes 36868
  2.6 45.6 %collective-permute-start.25 = (bf16[128,1536]{1,0:T(8,128)(2,1)}, bf16[128,1536]{1,0:T(8,128)(2,1)}, u32[]{:S(2)}, u32[]{:S(2)}) collective-permute-start(bf16[128,1536]{1,0:T(8,128)(2,1)} %get-tuple-element.9), channel_id=1, source_target_pairs={{0,4},{1,5},{2,6},{3,7},{4,0},{5,1},{6,2},{7,3},{8,12},{9,13},{10,... | collective-permute-start | bytes 1179656 | tf_op jit(solution)/shard_map/ppermute | solution.py:31
  6.7 43.1 %collective-permute-start.23 = (bf16[128,1536]{1,0:T(8,128)(2,1)}, bf16[128,1536]{1,0:T(8,128)(2,1)}, u32[]{:S(2)}, u32[]{:S(2)}) collective-permute-start(bf16[128,1536]{1,0:T(8,128)(2,1)} %get-tuple-element.9), channel_id=1, source_target_pairs={{0,1},{1,0},{2,3},{3,2},{4,5},{5,4},{6,7},{7,6},{8,9},{9,8},{10,11... | collective-permute-start | bytes 1179656 | tf_op jit(solution)/shard_map/ppermute | solution.py:41
  9.2 12.3 %collective-permute-start.2 = (bf16[32,1536]{1,0:T(8,128)(2,1)S(1)}, bf16[32,1536]{1,0:T(8,128)(2,1)S(1)}, u32[]{:S(2)}, u32[]{:S(2)}) collective-permute-start(bf16[32,1536]{1,0:T(8,128)(2,1)S(1)} %get-tuple-element.14), channel_id=1, source_target_pairs={{0,8},{8,0},{16,24},{24,16},{1,9},{9,1},{17,25},{25,17},{2,10},{10... | collective-permute-start | bytes 294920 | tf_op jit(solution)/shard_map/ppermute | solution.py:45
  9.3 12.2 %collective-permute-start.1 = (bf16[32,1536]{1,0:T(8,128)(2,1)S(1)}, bf16[32,1536]{1,0:T(8,128)(2,1)S(1)}, u32[]{:S(2)}, u32[]{:S(2)}) collective-permute-start(bf16[32,1536]{1,0:T(8,128)(2,1)S(1)} %get-tuple-element.15), channel_id=1, source_target_pairs={{0,16},{8,24},{16,0},{24,8},{1,17},{9,25},{17,1},{25,9},{2,18},{10... | collective-permute-start | bytes 294920 | tf_op jit(solution)/shard_map/ppermute | solution.py:45
  10.8 10.7 %collective-permute-start = (bf16[32,1536]{1,0:T(8,128)(2,1)S(1)}, bf16[32,1536]{1,0:T(8,128)(2,1)S(1)}, u32[]{:S(2)}, u32[]{:S(2)}) collective-permute-start(bf16[32,1536]{1,0:T(8,128)(2,1)S(1)} %get-tuple-element.16), channel_id=1, source_target_pairs={{0,24},{8,16},{16,8},{24,0},{1,25},{9,17},{17,9},{25,1},{2,26},{10... | collective-permute-start | bytes 294920 | tf_op jit(solution)/shard_map/ppermute | solution.py:45
  20.0 1.1 copy-start.8
  20.0 1.2 copy-start.10
  21.1 14.4 %copy-start.1 = (bf16[256,1536]{1,0:T(8,128)(2,1)S(1)}, bf16[256,1536]{1,0:T(8,128)(2,1)}, u32[]{:S(2)}) copy-start(bf16[256,1536]{1,0:T(8,128)(2,1)} %hidden.1) | copy-start | bytes 2359300
  22.5 7.6 %collective-permute-start.5 = (bf16[32,1536]{1,0:T(8,128)(2,1)S(1)}, bf16[32,1536]{1,0:T(8,128)(2,1)S(1)}, u32[]{:S(2)}, u32[]{:S(2)}) collective-permute-start(bf16[32,1536]{1,0:T(8,128)(2,1)S(1)} %fusion.43.rest_0_), channel_id=1, source_target_pairs={{0,6},{1,7},{2,4},{3,5},{4,2},{5,3},{6,0},{7,1},{8,14},{9,15},{10,... | collective-permute-start | bytes 294920 | tf_op jit(solution)/shard_map/ppermute | solution.py:31
  23.9 11.5 %collective-permute-start.4 = (bf16[32,1536]{1,0:T(8,128)(2,1)S(1)}, bf16[32,1536]{1,0:T(8,128)(2,1)S(1)}, u32[]{:S(2)}, u32[]{:S(2)}) collective-permute-start(bf16[32,1536]{1,0:T(8,128)(2,1)S(1)} %fusion.43.rest_0_), channel_id=1, source_target_pairs={{0,4},{1,5},{2,6},{3,7},{4,0},{5,1},{6,2},{7,3},{8,12},{9,13},{10,... | collective-permute-start | bytes 294920 | tf_op jit(solution)/shard_map/ppermute | solution.py:31
  25.6 9.8 %collective-permute-start.3 = (bf16[32,1536]{1,0:T(8,128)(2,1)S(1)}, bf16[32,1536]{1,0:T(8,128)(2,1)S(1)}, u32[]{:S(2)}, u32[]{:S(2)}) collective-permute-start(bf16[32,1536]{1,0:T(8,128)(2,1)S(1)} %fusion.43.rest_0_), channel_id=1, source_target_pairs={{0,2},{1,3},{2,0},{3,1},{4,6},{5,7},{6,4},{7,5},{8,10},{9,11},{10,... | collective-permute-start | bytes 294920 | tf_op jit(solution)/shard_map/ppermute | solution.py:31
  30.1 61.6 %collective-permute-start.18 = (bf16[1536,256]{1,0:T(8,128)(2,1)}, bf16[1536,256]{1,0:T(8,128)(2,1)}, u32[]{:S(2)}, u32[]{:S(2)}) collective-permute-start(bf16[1536,256]{1,0:T(8,128)(2,1)} %pad_maximum_fusion.1), channel_id=1, source_target_pairs={{0,4},{1,5},{2,6},{3,7},{4,0},{5,1},{6,2},{7,3},{8,12},{9,13},{10,... | collective-permute-start | bytes 2359304 | tf_op jit(solution)/shard_map/ppermute | solution.py:31
  35.4 16.3 %collective-permute-start.7 = (bf16[128,1536]{1,0:T(8,128)(2,1)S(1)}, bf16[128,1536]{1,0:T(8,128)(2,1)S(1)}, u32[]{:S(2)}, u32[]{:S(2)}) collective-permute-start(bf16[128,1536]{1,0:T(8,128)(2,1)S(1)} %pad_maximum_fusion.5.rest_0_), channel_id=1, source_target_pairs={{0,1},{1,0},{2,3},{3,2},{4,5},{5,4},{6,7},{7,6},{8,9},{9,8},{10,11... | collective-permute-start | bytes 1179656 | tf_op jit(solution)/shard_map/ppermute | solution.py:41
  35.6 3.7 %copy-start = (bf16[1536,3072]{1,0:T(8,128)(2,1)S(1)}, bf16[1536,3072]{1,0:T(8,128)(2,1)}, u32[]{:S(2)}) copy-start(bf16[1536,3072]{1,0:T(8,128)(2,1)} %weight.1) | copy-start | bytes 28311556
  48.1 16.5 %collective-permute-start.10 = (bf16[128,1536]{1,0:T(8,128)(2,1)S(1)}, bf16[128,1536]{1,0:T(8,128)(2,1)}, u32[]{:S(2)}, u32[]{:S(2)}) collective-permute-start(bf16[128,1536]{1,0:T(8,128)(2,1)S(1)} %pad_maximum_fusion.5.rest_0_), channel_id=1, source_target_pairs={{0,8},{8,0},{16,24},{24,16},{1,9},{9,1},{17,25},{25,17},{2,10},{10... | collective-permute-start | bytes 1179656 | tf_op jit(solution)/shard_map/ppermute | solution.py:45
  48.2 13.3 %collective-permute-start.6 = (bf16[128,1536]{1,0:T(8,128)(2,1)S(1)}, bf16[128,1536]{1,0:T(8,128)(2,1)S(1)}, u32[]{:S(2)}, u32[]{:S(2)}) collective-permute-start(bf16[128,1536]{1,0:T(8,128)(2,1)S(1)} %pad_maximum_fusion.5.rest_0_), channel_id=1, source_target_pairs={{0,16},{8,24},{16,0},{24,8},{1,17},{9,25},{17,1},{25,9},{2,18},{10... | collective-permute-start | bytes 1179656 | tf_op jit(solution)/shard_map/ppermute | solution.py:45
  49.8 13.7 %collective-permute-start.27 = (bf16[128,1536]{1,0:T(8,128)(2,1)}, bf16[128,1536]{1,0:T(8,128)(2,1)}, u32[]{:S(2)}, u32[]{:S(2)}) collective-permute-start(bf16[128,1536]{1,0:T(8,128)(2,1)} %collective-permute-done.25), channel_id=1, source_target_pairs={{0,1},{1,0},{2,3},{3,2},{4,5},{5,4},{6,7},{7,6},{8,9},{9,8},{10,11... | collective-permute-start | bytes 1179656 | tf_op jit(solution)/shard_map/ppermute | solution.py:41
  51.7 0.7 copy-start.3
  52.5 16.3 %collective-permute-start.24 = (bf16[128,1536]{1,0:T(8,128)(2,1)}, bf16[128,1536]{1,0:T(8,128)(2,1)}, u32[]{:S(2)}, u32[]{:S(2)}) collective-permute-start(bf16[128,1536]{1,0:T(8,128)(2,1)} %collective-permute-done.23), channel_id=1, source_target_pairs={{0,16},{8,24},{16,0},{24,8},{1,17},{9,25},{17,1},{25,9},{2,18},{10... | collective-permute-start | bytes 1179656 | tf_op jit(solution)/shard_map/ppermute | solution.py:45
  55.1 6.4 %copy-start.4 = (bf16[128,1536]{1,0:T(8,128)(2,1)S(1)}, bf16[128,1536]{1,0:T(8,128)(2,1)}, u32[]{:S(2)}) copy-start(bf16[128,1536]{1,0:T(8,128)(2,1)} %copy-done.3) | copy-start | bytes 1179652
  55.1 112.5 %all-to-all-start = ((bf16[4,8,16,1536]{3,1,2,0:T(8,128)(2,1)}), bf16[4,8,16,1536]{3,1,2,0:T(8,128)(2,1)}, u32[]{:S(2)}, u32[]{:S(2)}) async-start(bf16[4,8,16,1536]{3,1,2,0:T(8,128)(2,1)} %convolution_convert_fusion), calls=%async_computation | async-start | bytes 3145728 | tf_op jit(solution)/shard_map/all_to_all | solution.py:334
  61.5 35.7 %copy-start.2 = (s32[256,1]{1,0:T(8,128)S(1)}, s32[256,1]{1,0:T(8,128)}, u32[]{:S(2)}) copy-start(s32[256,1]{1,0:T(8,128)} %copy.23.row_ids) | copy-start | bytes 3076
  61.6 27.7 %collective-permute-start.8 = (bf16[64,1536]{1,0:T(8,128)(2,1)S(1)}, bf16[64,1536]{1,0:T(8,128)(2,1)S(1)}, u32[]{:S(2)}, u32[]{:S(2)}) collective-permute-start(bf16[64,1536]{1,0:T(8,128)(2,1)S(1)} %slice.198), channel_id=1, source_target_pairs={{0,16},{8,24},{16,0},{24,8},{1,17},{9,25},{17,1},{25,9},{2,18},{10... | collective-permute-start | bytes 589832 | tf_op jit(solution)/shard_map/ppermute | solution.py:45
  63.4 25.8 %collective-permute-start.9 = (bf16[64,1536]{1,0:T(8,128)(2,1)S(1)}, bf16[64,1536]{1,0:T(8,128)(2,1)S(1)}, u32[]{:S(2)}, u32[]{:S(2)}) collective-permute-start(bf16[64,1536]{1,0:T(8,128)(2,1)S(1)} %slice.199), channel_id=1, source_target_pairs={{0,1},{1,0},{2,3},{3,2},{4,5},{5,4},{6,7},{7,6},{8,9},{9,8},{10,11... | collective-permute-start | bytes 589832 | tf_op jit(solution)/shard_map/ppermute | solution.py:41
  64.7 30.4 %collective-permute-start.12 = (bf16[128,1536]{1,0:T(8,128)(2,1)S(1)}, bf16[128,1536]{1,0:T(8,128)(2,1)S(1)}, u32[]{:S(2)}, u32[]{:S(2)}) collective-permute-start(bf16[128,1536]{1,0:T(8,128)(2,1)S(1)} %copy-done.4), channel_id=1, source_target_pairs={{0,8},{8,0},{16,24},{24,16},{1,9},{9,1},{17,25},{25,17},{2,10},{10... | collective-permute-start | bytes 1179656 | tf_op jit(solution)/shard_map/ppermute | solution.py:45
  68.7 27.0 %collective-permute-start.11 = (bf16[128,1536]{1,0:T(8,128)(2,1)S(1)}, bf16[128,1536]{1,0:T(8,128)(2,1)S(1)}, u32[]{:S(2)}, u32[]{:S(2)}) collective-permute-start(bf16[128,1536]{1,0:T(8,128)(2,1)S(1)} %collective-permute-done.6.rest_1_), channel_id=1, source_target_pairs={{0,8},{8,0},{16,24},{24,16},{1,9},{9,1},{17,25},{25,17},{2,10},{10... | collective-permute-start | bytes 1179656 | tf_op jit(solution)/shard_map/ppermute | solution.py:45
  89.2 4.4 %collective-permute-start.13 = (bf16[64,1536]{1,0:T(8,128)(2,1)S(1)}, bf16[64,1536]{1,0:T(8,128)(2,1)S(1)}, u32[]{:S(2)}, u32[]{:S(2)}) collective-permute-start(bf16[64,1536]{1,0:T(8,128)(2,1)S(1)} %collective-permute-done.8.rest_3_), channel_id=1, source_target_pairs={{0,8},{8,0},{16,24},{24,16},{1,9},{9,1},{17,25},{25,17},{2,10},{10... | collective-permute-start | bytes 589832 | tf_op jit(solution)/shard_map/ppermute | solution.py:45
  89.2 6.4 %collective-permute-start.14 = (bf16[64,1536]{1,0:T(8,128)(2,1)S(1)}, bf16[64,1536]{1,0:T(8,128)(2,1)S(1)}, u32[]{:S(2)}, u32[]{:S(2)}) collective-permute-start(bf16[64,1536]{1,0:T(8,128)(2,1)S(1)} %collective-permute-done.9.rest_4_), channel_id=1, source_target_pairs={{0,8},{8,0},{16,24},{24,16},{1,9},{9,1},{17,25},{25,17},{2,10},{10... | collective-permute-start | bytes 589832 | tf_op jit(solution)/shard_map/ppermute | solution.py:45
  89.8 19.7 %slice-start = ((s8[4718592]{0:T(1024)(128)(4,1)}), s8[4194304]{0:T(1024)(128)(4,1)S(1)}, s32[]{:S(2)}) async-start(s8[4718592]{0:T(1024)(128)(4,1)} %bitcast.69), calls=%async_computation.1 | async-start | bytes 8388608
  91.7 17.8 %slice-start.1 = ((s8[4718592]{0:T(1024)(128)(4,1)}), s8[524288]{0:T(1024)(128)(4,1)S(1)}, s32[]{:S(2)}) async-start(s8[4718592]{0:T(1024)(128)(4,1)} %bitcast.69), calls=%async_computation.2 | async-start | bytes 1048576
  91.7 21.0 %collective-permute-start.16 = (bf16[1536,256]{1,0:T(8,128)(2,1)}, bf16[1536,256]{1,0:T(8,128)(2,1)S(1)}, u32[]{:S(2)}, u32[]{:S(2)}) collective-permute-start(bf16[1536,256]{1,0:T(8,128)(2,1)} %pad_maximum_fusion.1), channel_id=1, source_target_pairs={{0,1},{1,0},{2,3},{3,2},{4,5},{5,4},{6,7},{7,6},{8,9},{9,8},{10,11... | collective-permute-start | bytes 2359304 | tf_op jit(solution)/shard_map/ppermute | solution.py:41
  93.6 17.8 %collective-permute-start.26 = (bf16[128,1536]{1,0:T(8,128)(2,1)}, bf16[128,1536]{1,0:T(8,128)(2,1)S(1)}, u32[]{:S(2)}, u32[]{:S(2)}) collective-permute-start(bf16[128,1536]{1,0:T(8,128)(2,1)} %collective-permute-done.25), channel_id=1, source_target_pairs={{0,16},{8,24},{16,0},{24,8},{1,17},{9,25},{17,1},{25,9},{2,18},{10... | collective-permute-start | bytes 1179656 | tf_op jit(solution)/shard_map/ppermute | solution.py:45
  95.1 19.6 %collective-permute-start.28 = (bf16[64,1536]{1,0:T(8,128)(2,1)S(1)}, bf16[64,1536]{1,0:T(8,128)(2,1)S(1)}, u32[]{:S(2)}, u32[]{:S(2)}) collective-permute-start(bf16[64,1536]{1,0:T(8,128)(2,1)S(1)} %slice.218), channel_id=1, source_target_pairs={{0,16},{8,24},{16,0},{24,8},{1,17},{9,25},{17,1},{25,9},{2,18},{10... | collective-permute-start | bytes 589832 | tf_op jit(solution)/shard_map/ppermute | solution.py:45
  95.7 37.0 %collective-permute-start.20 = (bf16[1536,256]{1,0:T(8,128)(2,1)}, bf16[1536,256]{1,0:T(8,128)(2,1)S(1)}, u32[]{:S(2)}, u32[]{:S(2)}) collective-permute-start(bf16[1536,256]{1,0:T(8,128)(2,1)} %collective-permute-done.18), channel_id=1, source_target_pairs={{0,1},{1,0},{2,3},{3,2},{4,5},{5,4},{6,7},{7,6},{8,9},{9,8},{10,11... | collective-permute-start | bytes 2359304 | tf_op jit(solution)/shard_map/ppermute | solution.py:41
  95.8 38.5 %collective-permute-start.19 = (bf16[1536,256]{1,0:T(8,128)(2,1)}, bf16[1536,256]{1,0:T(8,128)(2,1)S(1)}, u32[]{:S(2)}, u32[]{:S(2)}) collective-permute-start(bf16[1536,256]{1,0:T(8,128)(2,1)} %collective-permute-done.18), channel_id=1, source_target_pairs={{0,16},{8,24},{16,0},{24,8},{1,17},{9,25},{17,1},{25,9},{2,18},{10... | collective-permute-start | bytes 2359304 | tf_op jit(solution)/shard_map/ppermute | solution.py:45
  109.5 1.5 copy-start.15
  109.5 2.0 %copy-start.14 = (bf16[1024,1536]{1,0:T(8,128)(2,1)S(1)}, bf16[1024,1536]{1,0:T(8,128)(2,1)}, u32[]{:S(2)}) copy-start(bf16[1024,1536]{1,0:T(8,128)(2,1)} %constant_dynamic-update-slice_fusion.6) | copy-start | bytes 9437188
  111.4 24.7 %collective-permute-start.15 = (bf16[256,1536]{1,0:T(8,128)(2,1)S(1)}, bf16[256,1536]{1,0:T(8,128)(2,1)S(1)}, u32[]{:S(2)}, u32[]{:S(2)}) collective-permute-start(bf16[256,1536]{1,0:T(8,128)(2,1)S(1)} %multiply_convert_fusion), channel_id=1, source_target_pairs={{0,8},{8,0},{16,24},{24,16},{1,9},{9,1},{17,25},{25,17},{2,10},{10... | collective-permute-start | bytes 2359304 | tf_op jit(solution)/shard_map/ppermute | solution.py:45
  111.5 24.6 %copy-start.9 = (bf16[1536,128]{1,0:T(8,128)(2,1)S(1)}, bf16[1536,128]{1,0:T(8,128)(2,1)}, u32[]{:S(2)}) copy-start(bf16[1536,128]{1,0:T(8,128)(2,1)} %copy-done.8) | copy-start | bytes 1179652
  111.6 24.6 %copy-start.11 = (bf16[1536,128]{1,0:T(8,128)(2,1)S(1)}, bf16[1536,128]{1,0:T(8,128)(2,1)}, u32[]{:S(2)}) copy-start(bf16[1536,128]{1,0:T(8,128)(2,1)} %copy-done.10) | copy-start | bytes 1179652
  112.7 19.9 %collective-permute-start.29 = (bf16[64,1536]{1,0:T(8,128)(2,1)S(1)}, bf16[64,1536]{1,0:T(8,128)(2,1)S(1)}, u32[]{:S(2)}, u32[]{:S(2)}) collective-permute-start(bf16[64,1536]{1,0:T(8,128)(2,1)S(1)} %slice.219), channel_id=1, source_target_pairs={{0,1},{1,0},{2,3},{3,2},{4,5},{5,4},{6,7},{7,6},{8,9},{9,8},{10,11... | collective-permute-start | bytes 589832 | tf_op jit(solution)/shard_map/ppermute | solution.py:41
  114.7 29.1 %collective-permute-start.17 = (bf16[1536,256]{1,0:T(8,128)(2,1)S(1)}, bf16[1536,256]{1,0:T(8,128)(2,1)S(1)}, u32[]{:S(2)}, u32[]{:S(2)}) collective-permute-start(bf16[1536,256]{1,0:T(8,128)(2,1)S(1)} %collective-permute-done.16), channel_id=1, source_target_pairs={{0,16},{8,24},{16,0},{24,8},{1,17},{9,25},{17,1},{25,9},{2,18},{10... | collective-permute-start | bytes 2359304 | tf_op jit(solution)/shard_map/ppermute | solution.py:45
  132.6 18.8 %collective-permute-start.31 = (bf16[256,1536]{1,0:T(8,128)(2,1)S(1)}, bf16[256,1536]{1,0:T(8,128)(2,1)S(1)}, u32[]{:S(2)}, u32[]{:S(2)}) collective-permute-start(bf16[256,1536]{1,0:T(8,128)(2,1)S(1)} %multiply_convert_fusion), channel_id=1, source_target_pairs={{0,2},{1,3},{2,0},{3,1},{4,6},{5,7},{6,4},{7,5},{8,10},{9,11},{10,... | collective-permute-start | bytes 2359304 | tf_op jit(solution)/shard_map/ppermute | solution.py:31
  132.7 19.0 %collective-permute-start.21 = (bf16[768,256]{1,0:T(8,128)(2,1)S(1)}, bf16[768,256]{1,0:T(8,128)(2,1)S(1)}, u32[]{:S(2)}, u32[]{:S(2)}) collective-permute-start(bf16[768,256]{1,0:T(8,128)(2,1)S(1)} %slice.214), channel_id=1, source_target_pairs={{0,16},{8,24},{16,0},{24,8},{1,17},{9,25},{17,1},{25,9},{2,18},{10... | collective-permute-start | bytes 1179656 | tf_op jit(solution)/shard_map/ppermute | solution.py:45
  134.3 2.6 %copy-start.12 = (bf16[1536,128]{1,0:T(8,128)(2,1)S(1)}, bf16[1536,128]{1,0:T(8,128)(2,1)}, u32[]{:S(2)}) copy-start(bf16[1536,128]{1,0:T(8,128)(2,1)} %get-tuple-element.10) | copy-start | bytes 1179652
  134.3 2.6 %copy-start.13 = (bf16[1536,128]{1,0:T(8,128)(2,1)S(1)}, bf16[1536,128]{1,0:T(8,128)(2,1)}, u32[]{:S(2)}) copy-start(bf16[1536,128]{1,0:T(8,128)(2,1)} %get-tuple-element.12) | copy-start | bytes 1179652
  134.3 17.4 %collective-permute-start.22 = (bf16[768,256]{1,0:T(8,128)(2,1)S(1)}, bf16[768,256]{1,0:T(8,128)(2,1)S(1)}, u32[]{:S(2)}, u32[]{:S(2)}) collective-permute-start(bf16[768,256]{1,0:T(8,128)(2,1)S(1)} %slice.215), channel_id=1, source_target_pairs={{0,1},{1,0},{2,3},{3,2},{4,5},{5,4},{6,7},{7,6},{8,9},{9,8},{10,11... | collective-permute-start | bytes 1179656 | tf_op jit(solution)/shard_map/ppermute | solution.py:41
  151.4 2.3 %collective-permute-start.32 = (bf16[256,1536]{1,0:T(8,128)(2,1)S(1)}, bf16[256,1536]{1,0:T(8,128)(2,1)S(1)}, u32[]{:S(2)}, u32[]{:S(2)}) collective-permute-start(bf16[256,1536]{1,0:T(8,128)(2,1)S(1)} %collective-permute-done.31), channel_id=1, source_target_pairs={{0,8},{8,0},{16,24},{24,16},{1,9},{9,1},{17,25},{25,17},{2,10},{10... | collective-permute-start | bytes 2359304 | tf_op jit(solution)/shard_map/ppermute | solution.py:45
  162.6 3.6 %collective-permute-start.33 = (bf16[256,1536]{1,0:T(8,128)(2,1)S(1)}, bf16[256,1536]{1,0:T(8,128)(2,1)S(1)}, u32[]{:S(2)}, u32[]{:S(2)}) collective-permute-start(bf16[256,1536]{1,0:T(8,128)(2,1)S(1)} %slice.382), channel_id=1, source_target_pairs={{0,8},{8,0},{16,24},{24,16},{1,9},{9,1},{17,25},{25,17},{2,10},{10... | collective-permute-start | bytes 2359304 | tf_op jit(solution)/shard_map/ppermute | solution.py:45
  165.6 1.6 copy-start.6
  165.7 5.0 %collective-permute-start.30 = (bf16[256,1536]{1,0:T(8,128)(2,1)S(1)}, bf16[256,1536]{1,0:T(8,128)(2,1)}, u32[]{:S(2)}, u32[]{:S(2)}) collective-permute-start(bf16[256,1536]{1,0:T(8,128)(2,1)S(1)} %slice.383), channel_id=1, source_target_pairs={{0,8},{8,0},{16,24},{24,16},{1,9},{9,1},{17,25},{25,17},{2,10},{10... | collective-permute-start | bytes 2359304 | tf_op jit(solution)/shard_map/ppermute | solution.py:45
  167.2 19.9 %collective-permute-start.34 = (bf16[256,1536]{1,0:T(8,128)(2,1)S(1)}, bf16[256,1536]{1,0:T(8,128)(2,1)}, u32[]{:S(2)}, u32[]{:S(2)}) collective-permute-start(bf16[256,1536]{1,0:T(8,128)(2,1)S(1)} %fusion.2), channel_id=1, source_target_pairs={{0,2},{1,3},{2,0},{3,1},{4,6},{5,7},{6,4},{7,5},{8,10},{9,11},{10,... | collective-permute-start | bytes 2359304 | tf_op jit(solution)/shard_map/ppermute | solution.py:31
  167.6 19.6 %copy-start.7 = (f32[512,1536]{1,0:T(8,128)S(1)}, f32[512,1536]{1,0:T(8,128)}, u32[]{:S(2)}) copy-start(f32[512,1536]{1,0:T(8,128)} %copy-done.6) | copy-start | bytes 9437188

commit v3 on v2

v3 whole, which is shorter than its diff:
```python
import functools

import jax
import jax.numpy as jnp
from jax import lax
from jax.experimental import pallas as pl
from jax.experimental.pallas import tpu as pltpu
from jax.sharding import PartitionSpec as P

QUERY_HEADS = 16
KEY_VALUE_HEADS = 8
HEAD_DIMENSION = 96
PREFIX_TOKENS = 1024
CAP = 8


ROPE_BASE = 100000.0
EPSILON = 1e-05
NEGATIVE_FILLER = -1e30
LOG2_E = 1.4426950408889634


Z_SIZE = 4


def tensor_xor(value, tensor_count, z_bits):
    width = tensor_count // Z_SIZE
    pairs = [
        (z * width + y, (z ^ z_bits) * width + y) for z in range(Z_SIZE) for y in range(width)
    ]
    return lax.ppermute(value, "tensor", pairs)


def tensor_turn(value, tensor_count, step):
    width = tensor_count // Z_SIZE
    pairs = [
        (z * width + y, z * width + (y + step) % width)
        for z in range(Z_SIZE)
        for y in range(width)
    ]
    return lax.ppermute(value, "tensor", pairs)


def group_xor(value, group_count, bits):
    return lax.ppermute(value, "group", [(g, g ^ bits) for g in range(group_count)])


def own_quarter(block, prefix_owner, group_count):
    group = lax.axis_index("group")
    owner = prefix_owner[lax.axis_index("tensor")]
    rows = block.shape[0] // group_count
    quarter = block[:rows]
    for bits in range(1, group_count):
        came = group_xor(block[bits * rows : (bits + 1) * rows], group_count, bits)
        quarter = jnp.where(owner == (group ^ bits), came, quarter)
    return quarter


HBM = pl.BlockSpec(memory_space=pltpu.HBM)
ANYWHERE = pl.BlockSpec(memory_space=pl.ANY)


def whole(array):
    return pl.BlockSpec(array.shape, lambda *_: (0,) * len(array.shape))


def wholes(arrays):
    return [whole(array) for array in arrays]


def after(value, *earlier):
    return lax.optimization_barrier((value, *earlier))[0]


def swap_in_plane(value, x_core, group_count, tensor_count):
    pairs = []
    for group in range(group_count):
        for place in range(tensor_count):
            over_x = group % 2 == x_core
            target = (group ^ 2, place) if over_x else (group, place ^ 1)
            pairs.append((group * tensor_count + place, target[0] * tensor_count + target[1]))
    return lax.ppermute(value, ("group", "tensor"), pairs)


def plane_pair(value, group_count, tensor_count):
    if tensor_count != 2 * Z_SIZE:
        return [value, group_xor(value, group_count, 2)]
    return [value, swap_in_plane(value, 0, group_count, tensor_count)]


def plane_rest(pair, group_count, tensor_count):
    width = tensor_count // Z_SIZE
    if width != 2:
        return [tensor_turn(v, tensor_count, step) for step in range(1, width) for v in pair]
    return [swap_in_plane(v, 1, group_count, tensor_count) for v in pair]


def pack_kernel(side, w_in, w_down, inward, down):
    part = w_in.shape[2] // 2
    columns = pl.ds(pl.multiple_of(side[0] * part, part), part)
    for half in range(2):
        inward[:, half * part : (half + 1) * part] = w_in[half, :, columns]
    for block in range(down.shape[0] // part):
        down[block * part : (block + 1) * part, :] = w_down[
            columns, block * 2 * part : (block + 1) * 2 * part
        ]


def join_piece(gate, up, down):
    width = 2 * gate.shape[1]
    blocks = [down[:, at : at + width] for at in range(0, down.shape[1], width)]
    return jnp.concatenate([gate, up], axis=1), jnp.concatenate(blocks)


def split_piece(piece):
    inward, down = piece
    part = inward.shape[1] // 2
    blocks = [down[at : at + part] for at in range(0, down.shape[0], part)]
    return inward[:, :part], inward[:, part:], jnp.concatenate(blocks, axis=1)


def own_piece(w_in, w_down, side):
    core = lax.axis_index("group") % 2
    depth, part = w_in.shape[1], w_in.shape[2] // 4
    if part % 128:
        start = (core * 2 + side) * part
        return join_piece(
            lax.dynamic_slice_in_dim(w_in[0], start, part, 1),
            lax.dynamic_slice_in_dim(w_in[1], start, part, 1),
            lax.dynamic_slice_in_dim(w_down, start, part, 0),
        )
    steps = depth // (4 * part)
    shapes = [(depth, 2 * part), (depth // 2, 2 * part)]
    return pl.pallas_call(
        pack_kernel,
        grid_spec=pltpu.PrefetchScalarGridSpec(
            num_scalar_prefetch=1,
            grid=(steps,),
            in_specs=[
                pl.BlockSpec((2, depth // steps, 2 * part), lambda i, at: (0, i, at[1])),
                pl.BlockSpec((2 * part, depth // steps), lambda i, at: (at[1], i)),
            ],
            out_specs=[
                pl.BlockSpec((rows // steps, columns), lambda i, at: (i, 0))
                for rows, columns in shapes
            ],
        ),
        out_shape=[jax.ShapeDtypeStruct(shape, w_in.dtype) for shape in shapes],
        compiler_params=pltpu.CompilerParams(vmem_limit_bytes=60 << 20),
    )(jnp.stack([side, core]).astype(jnp.int32), w_in, w_down)


def merge_pieces(pieces):
    count = max(1, 128 // (pieces[0][0].shape[1] // 2))
    if count == 1:
        return pieces
    merged = []
    for at in range(0, len(pieces), count):
        gates, ups, downs = zip(*[split_piece(p) for p in pieces[at : at + count]])
        merged.append(
            join_piece(
                jnp.concatenate(gates, axis=1),
                jnp.concatenate(ups, axis=1),
                jnp.concatenate(downs),
            )
        )
    return merged


def rms_norm(inputs, gain_row):
    floated = inputs.astype(jnp.float32)
    return (
        floated
        * lax.rsqrt(jnp.mean(floated * floated, axis=-1, keepdims=True) + EPSILON)
        * gain_row
    )


def positions(segment):
    row_number = segment.shape[0]
    row_index = jnp.arange(row_number, dtype=jnp.int32)
    same_request = segment[:, None] == segment[None, :]
    first_row = jnp.min(jnp.where(same_request, row_index[None, :], row_number), axis=1)
    return PREFIX_TOKENS + row_index - first_row


def rotary_tables(locate_position, width):
    half_dim = HEAD_DIMENSION // 2
    frequency = ROPE_BASE ** (-jnp.arange(half_dim, dtype=jnp.float32) / half_dim)
    angles = locate_position.astype(jnp.float32)[:, None] * frequency[None, :]
    cosine, sine = jnp.cos(angles), jnp.sin(angles)
    heads = width // HEAD_DIMENSION
    return jnp.tile(cosine, (1, 2 * heads)), jnp.tile(
        jnp.concatenate([-sine, sine], axis=1), (1, heads)
    )


def project_kernel(hidden, gain, weight, cosine, sine, *rest):
    out, normed = rest[-2:]
    step = pl.program_id(0)
    width = weight.shape[1]
    rotated_steps = (QUERY_HEADS + KEY_VALUE_HEADS) * HEAD_DIMENSION // width

    @pl.when(step == 0)
    def _():
        normed[...] = rms_norm(hidden[...], gain[...]).astype(jnp.bfloat16)

    projected = jnp.dot(normed[...], weight[...], preferred_element_type=jnp.float32)

    @pl.when(step < rotated_steps)
    def _():
        half_dim = HEAD_DIMENSION // 2
        lane = lax.broadcasted_iota(jnp.int32, projected.shape, 1)
        swapped = jnp.where(
            lane % HEAD_DIMENSION < half_dim,
            pltpu.roll(projected, width - half_dim, 1),
            pltpu.roll(projected, half_dim, 1),
        )
        heads = width // HEAD_DIMENSION
        cosines = jnp.concatenate([cosine[...]] * heads, axis=1)
        sines = jnp.concatenate([sine[...]] * heads, axis=1)
        out[...] = (projected * cosines + swapped * sines).astype(jnp.bfloat16)

    @pl.when(step >= rotated_steps)
    def _():
        out[...] = projected.astype(jnp.bfloat16)


def project(hidden_in, gain_row, weight, locate_position, earlier):
    rows, depth = hidden_in.shape
    columns = weight.shape[1]
    width = 8 * HEAD_DIMENSION
    cosine, sine = rotary_tables(locate_position, HEAD_DIMENSION)
    return pl.pallas_call(
        project_kernel,
        grid=(columns // width,),
        in_specs=[
            whole(hidden_in),
            whole(gain_row[None, :]),
            pl.BlockSpec((depth, width), lambda i: (0, i)),
            whole(cosine),
            whole(sine),
        ]
        + [pl.BlockSpec(memory_space=pl.ANY)] * len(earlier),
        out_specs=pl.BlockSpec((rows, width), lambda i: (0, i)),
        out_shape=jax.ShapeDtypeStruct((rows, columns), jnp.bfloat16),
        scratch_shapes=[pltpu.VMEM((rows, depth), jnp.bfloat16)],
        compiler_params=pltpu.CompilerParams(vmem_limit_bytes=60 << 20),
        cost_estimate=pl.CostEstimate(
            flops=2 * rows * depth * columns,
            bytes_accessed=2 * depth * columns,
            transcendentals=0,
        ),
    )(hidden_in, gain_row[None, :], weight, cosine, sine, *earlier)


def head_columns(index):
    return slice(index * HEAD_DIMENSION, (index + 1) * HEAD_DIMENSION)


def attention_kernel(piece_count, heads, row_ids, column_ids, projected, *rest):
    pieces, out, joined, semaphores = rest[:piece_count], *rest[-3:]
    rows = projected.shape[0]
    repeats = QUERY_HEADS // KEY_VALUE_HEADS
    first, count = heads
    width = count * HEAD_DIMENSION
    key_value_width = KEY_VALUE_HEADS * HEAD_DIMENSION
    copies, at = [], 0
    for index, piece in enumerate(pieces):
        for side in range(2):
            start = side * key_value_width + first * HEAD_DIMENSION
            source = piece.at[:, pl.ds(start, width)]
            target = joined.at[pl.ds(at, piece.shape[0]), pl.ds(side * width, width)]
            copies.append(pltpu.make_async_copy(source, target, semaphores.at[2 * index + side]))
        at += piece.shape[0]
    for copy in copies:
        copy.start()
    for side in range(2):
        start = (QUERY_HEADS + side * KEY_VALUE_HEADS + first) * HEAD_DIMENSION
        joined[at : at + rows, side * width : (side + 1) * width] = projected[
            :, start : start + width
        ]
    row_index = lax.broadcasted_iota(jnp.int32, (rows, rows), 0)
    column_index = lax.broadcasted_iota(jnp.int32, (rows, rows), 1)
    allowed = (row_ids[...] == column_ids[...]) & (column_index <= row_index)
    allowed = jnp.concatenate([allowed] * repeats, axis=0)
    scale = HEAD_DIMENSION ** (-0.5) * LOG2_E
    for copy in copies:
        copy.wait()
    for head in range(count):
        queries = jnp.concatenate(
            [projected[:, head_columns((first + head) * repeats + g)] for g in range(repeats)],
            axis=0,
        )
        scores = lax.dot_general(
            queries,
            joined[:, head_columns(head)],
            (((1,), (1,)), ((), ())),
            preferred_element_type=jnp.float32,
        )
        scores = jnp.concatenate(
            [scores[:, :at], jnp.where(allowed, scores[:, at:], NEGATIVE_FILLER)], axis=1
        )
        top = jnp.max(scores, axis=1, keepdims=True)
        weights = jnp.exp2((scores - top) * scale)
        total = jnp.sum(weights, axis=1, keepdims=True)
        summed = jnp.dot(
            weights.astype(jnp.bfloat16),
            joined[:, head_columns(count + head)],
            preferred_element_type=jnp.float32,
        )
        attended = (summed / total).astype(jnp.bfloat16)
        for g in range(repeats):
            out[:, head_columns(head * repeats + g)] = attended[g * rows : (g + 1) * rows]


def last_attention_kernel(
    piece_count, heads, row_ids, column_ids, projected, hidden, gain, *rest
):
    pieces, w_out = rest[:piece_count], rest[piece_count]
    middle, second, joined, semaphores, out, weight, semaphore = rest[-7:]
    fetch = pltpu.make_async_copy(w_out, weight, semaphore)
    fetch.start()
    attention_kernel(
        piece_count, heads, row_ids, column_ids, projected, *pieces, out, joined, semaphores
    )
    fetch.wait()
    added = jnp.dot(out[...], weight[...], preferred_element_type=jnp.float32)
    middle[...] = (hidden[...].astype(jnp.float32) + added).astype(jnp.bfloat16)
    second[...] = rms_norm(middle[...], gain[...]).astype(jnp.bfloat16)


def attend(segment, projected, pieces, heads, rest=None):
    rows = projected.shape[0]
    key_count = rows + sum(piece.shape[0] for piece in pieces)
    width = heads[1] * HEAD_DIMENSION
    columns = width * QUERY_HEADS // KEY_VALUE_HEADS
    resident = [segment[:, None], segment[None, :], projected]
    remote = list(pieces)
    kernel = attention_kernel
    out = [jax.ShapeDtypeStruct((rows, columns), jnp.bfloat16)]
    scratch = [
        pltpu.VMEM((key_count, 2 * width), jnp.bfloat16),
        pltpu.SemaphoreType.DMA((2 * len(pieces),)),
    ]
    if rest is not None:
        hidden_in, gain_row, w_out = rest
        resident += [hidden_in, gain_row[None, :]]
        remote.append(w_out)
        kernel = last_attention_kernel
        out = [jax.ShapeDtypeStruct(hidden_in.shape, jnp.bfloat16)] * 2
        scratch += [
            pltpu.VMEM((rows, columns), jnp.bfloat16),
            pltpu.VMEM(w_out.shape, jnp.bfloat16),
            pltpu.SemaphoreType.DMA,
        ]
    return pl.pallas_call(
        functools.partial(kernel, len(pieces), heads),
        grid=(1,),
        in_specs=wholes(resident) + [HBM] * len(remote),
        out_specs=wholes(out),
        out_shape=out,
        scratch_shapes=scratch,
        compiler_params=pltpu.CompilerParams(vmem_limit_bytes=60 << 20),
    )(*resident, *remote)


def feed_forward_kernel(piece_count, carry_count, left, right, *rest):
    weights = rest[: 2 * piece_count]
    carries = rest[2 * piece_count : 2 * piece_count + carry_count]
    left_out, right_out, tokens, acts = rest[-4:]
    rows, depth = left.shape
    part = weights[0].shape[1] // 2
    tokens[:rows, :] = left[...]
    tokens[rows:, :] = right[...]
    for index in range(piece_count):
        both = jnp.dot(tokens[...], weights[2 * index][...], preferred_element_type=jnp.float32)
        gate, up = both[:, :part], both[:, part:]
        acts[:, index * part : (index + 1) * part] = (gate / (1.0 + jnp.exp(-gate)) * up).astype(
            jnp.bfloat16
        )
    for block in range(depth // (2 * part)):
        columns = slice(block * 2 * part, (block + 1) * 2 * part)
        weight = jnp.concatenate(
            [v[block * part : (block + 1) * part, :] for v in weights[1::2]]
        )
        sums = jnp.dot(acts[...], weight, preferred_element_type=jnp.float32)
        for side, out in enumerate((left_out, right_out)):
            found = sums[side * rows : (side + 1) * rows]
            for carry in carries[side::2]:
                found += carry[:, columns].astype(jnp.float32)
            out[:, columns] = found.astype(out.dtype)


def feed_forward(left, right, pieces, carries, right_dtype, earlier=()):
    rows, depth = left.shape
    part = pieces[0][0].shape[1] // 2
    chunks = [chunk for piece in pieces for chunk in piece]
    out = [jax.ShapeDtypeStruct((rows, depth), dtype) for dtype in (jnp.float32, right_dtype)]
    return pl.pallas_call(
        functools.partial(feed_forward_kernel, len(pieces), len(carries)),
        grid=(1,),
        in_specs=wholes([left, right, *chunks, *carries]) + [ANYWHERE] * len(earlier),
        out_specs=wholes(out),
        out_shape=out,
        scratch_shapes=[
            pltpu.VMEM((2 * rows, depth), jnp.bfloat16),
            pltpu.VMEM((2 * rows, part * len(pieces)), jnp.bfloat16),
        ],
        compiler_params=pltpu.CompilerParams(vmem_limit_bytes=32 << 20),
    )(left, right, *chunks, *carries, *earlier)


def add_rows(first, *others):
    def kernel(*refs):
        refs[-1][...] = sum(ref[...].astype(jnp.float32) for ref in refs[:-1]).astype(jnp.bfloat16)

    return pl.pallas_call(
        kernel,
        grid=(1,),
        in_specs=wholes([first, *others]),
        out_specs=whole(first),
        out_shape=jax.ShapeDtypeStruct(first.shape, jnp.bfloat16),
    )(first, *others)


def select_kernel(group_count, table, projected, *rest):
    outs = rest[-group_count:]
    page_rows = outs[0].shape[0] // CAP
    columns = outs[0].shape[1]
    for index in range(group_count * CAP):
        page = table[index]
        start = pl.multiple_of(jnp.maximum(page, 0) * page_rows, page_rows)
        rows = projected[pl.ds(start, page_rows), columns:]
        slot = index % CAP
        outs[index // CAP][slot * page_rows : (slot + 1) * page_rows, :] = jnp.where(
            page >= 0, rows, jnp.zeros_like(rows)
        )


def select_pages(projected, destination, group_count, earlier):
    page_count = destination.shape[0]
    page_rows = projected.shape[0] // page_count
    group = lax.axis_index("group")
    same = destination[:, None] == destination[None, :]
    page = jnp.arange(page_count, dtype=jnp.int32)
    rank = jnp.sum(same & (page[None, :] < page[:, None]), axis=1, dtype=jnp.int32)
    slot = (destination ^ group) * CAP + rank
    chosen = slot[None, :] == jnp.arange(group_count * CAP, dtype=jnp.int32)[:, None]
    table = jnp.max(jnp.where(chosen, page[None, :], -1), axis=1)
    columns = projected.shape[1] // 2
    out = [jax.ShapeDtypeStruct((CAP * page_rows, columns), projected.dtype)] * group_count
    return pl.pallas_call(
        functools.partial(select_kernel, group_count),
        grid_spec=pltpu.PrefetchScalarGridSpec(
            num_scalar_prefetch=1,
            grid=(1,),
            in_specs=[whole(projected)] + [ANYWHERE] * len(earlier),
            out_specs=wholes(out),
        ),
        out_shape=out,
        compiler_params=pltpu.CompilerParams(vmem_limit_bytes=16 << 20),
    )(table, projected, *earlier)


def place_kernel(group, *rest):
    *received, out = rest
    for bits, block in enumerate(received):
        out[group[0] ^ bits] = block[...]


def place_pages(received):
    out = jax.ShapeDtypeStruct((len(received), *received[0].shape), received[0].dtype)
    return pl.pallas_call(
        place_kernel,
        grid_spec=pltpu.PrefetchScalarGridSpec(
            num_scalar_prefetch=1,
            grid=(1,),
            in_specs=wholes(received),
            out_specs=whole(out),
        ),
        out_shape=out,
    )(lax.axis_index("group")[None].astype(jnp.int32), *received)


def on_device(
    hidden_in,
    request_ids,
    norm_gains,
    query_key_value_weight,
    w_out,
    w_in,
    w_down,
    prefix_cache,
    prefix_owner,
    page_dest,
):
    group_count, tensor_count = lax.axis_size("group"), lax.axis_size("tensor")
    sizes = (group_count, tensor_count)
    turns = range(1, tensor_count // Z_SIZE)
    segment = request_ids[0]
    quarter = own_quarter(prefix_cache[0], prefix_owner, group_count)
    across = lax.axis_index("group") // 2
    mine = own_piece(w_in, w_down, across)
    far_down = tensor_xor(mine[1], tensor_count, 2)
    inward = [tensor_turn(mine[0], tensor_count, step) for step in turns]
    along_z = [tensor_xor(quarter, tensor_count, bits) for bits in range(1, Z_SIZE)]
    projected = project(
        after(hidden_in, mine[0], quarter),
        norm_gains[0],
        query_key_value_weight,
        positions(segment),
        [],
    )
    line = after(jnp.concatenate([quarter] + along_z), projected, far_down)
    other = own_piece(w_in, w_down, after(1 - across, projected))
    far_in = tensor_xor(after(mine[0], line), tensor_count, 2)
    lines = plane_pair(line, *sizes)
    lines = after(jnp.concatenate(lines), inward[0])
    across = [group_xor(after(v, lines), group_count, 2) for v in inward]
    lines = [lines] + plane_rest([lines], *sizes)
    down_pair = plane_pair(far_down, *sizes)
    down = [[tensor_turn(v, tensor_count, step) for v in (mine[1], other[1])] for step in turns]
    near = []
    for step in range(len(turns)):
        near += [(inward[step], down[step][0]), (across[step], down[step][1])]
    lines += [group_xor(v, group_count, 1) for v in lines]
    middle, second = attend(
        segment,
        projected,
        lines,
        (0, KEY_VALUE_HEADS),
        (hidden_in, norm_gains[1], w_out),
    )
    far = after(second, far_in, across[0], *down[0], down_pair[1])
    far = tensor_xor(far, tensor_count, 1)
    in_pair = plane_pair(far_in, *sizes)
    late = [pair + plane_rest(pair, *sizes) for pair in (in_pair, down_pair)]
    late = list(zip(*late))
    beside = group_xor(second, group_count, 1)
    far_beside = group_xor(far, group_count, 1)
    near = merge_pieces([mine, other] + near)
    late = merge_pieces(late)
    own_early = feed_forward(second, beside, near, [], jnp.float32)
    far_early = feed_forward(far, far_beside, near, [], jnp.float32, own_early)
    outgoing = select_pages(projected, page_dest[:, 0], group_count, [far])
    far_sum, far_beside_sum = feed_forward(
        far, far_beside, late, far_early, jnp.bfloat16, [outgoing[0]]
    )
    far_sum = far_sum + group_xor(far_beside_sum, group_count, 1).astype(jnp.float32)
    far_sum = far_sum.astype(jnp.bfloat16)
    returned = tensor_xor(far_sum, tensor_count, 1)
    received = [outgoing[0]] + [
        group_xor(outgoing[bits], group_count, bits) for bits in range(1, group_count)
    ]
    own_sum, beside_sum = feed_forward(
        after(second, far_sum, *received[1:]), beside, late, [*own_early, middle], jnp.bfloat16
    )
    own_beside = group_xor(beside_sum, group_count, 1)
    received = place_pages(received)
    hidden_out = add_rows(own_sum, own_beside, after(returned, received))
    pages = received.reshape(group_count, CAP, -1, received.shape[2])
    return (hidden_out, pages[None, None])


def solution(mesh):
    return jax.shard_map(
        on_device,
        mesh=mesh,
        in_specs=(
            P(("group", "tensor"), None),
            P(("group", "tensor"), None),
            P(),
            P(),
            P(),
            P(None, None, "tensor"),
            P("tensor", None),
            P("group", "tensor", None),
            P(),
            P(("group", "tensor"), None),
        ),
        out_specs=(P(("group", "tensor"), None), P("group", "tensor", None, None, None, None)),
        check_vma=False,
    )
```

time: 191 us -> 182 us (0.953)
  Pallas kernels: 21 us -> 57.2 us
  local copies, waits for them, and re-layouts: 26.2 us -> 6.2 us
  matrix products: 19.4 us -> 0 us
  starting transfers between devices: 40 us -> 32.9 us
  waiting for transfers between devices: 72.2 us -> 77.8 us
  other arithmetic: 7.78 us -> 4.13 us
    pallas_call x1 -> x10, Pallas kernels: 12.2 us -> 48.4 us  [the longest x1 17.8 us: attend(): pl.pallas_call(functools.partial(kernel, len(pieces), heads), grid=(1,),...]
    ppermute x0 -> x8, waiting for transfers between devices: none -> 31.7 us  [swap_in_plane(): return lax.ppermute(value, ('group', 'tensor'), pairs)]
    dot_general x20 -> x0, matrix products: 19.4 us -> none  [the longest x16 12.2 us: expand_with(): both = jnp.dot(token_block, gate_and_up, preferred_element_type=jnp.float32)]
    ppermute x8 -> x3, waiting for transfers between devices: 16.9 us -> 0.01 us  [tensor_turn(): return lax.ppermute(value, 'tensor', pairs)]
    unnamed x53 -> x36, local copies, waits for them, and re-layouts: 19 us -> 2.37 us
    ppermute x20 -> x13, waiting for transfers between devices: 28.4 us -> 16.7 us  [group_xor(): lax.ppermute(value, 'group', [(g, g ^ bits) for g in range(group_count)])]
    ppermute x0 -> x8, starting transfers between devices: none -> 9.8 us  [swap_in_plane(): return lax.ppermute(value, ('group', 'tensor'), pairs)]
    ppermute x8 -> x3, starting transfers between devices: 9.73 us -> 3.61 us  [tensor_turn(): return lax.ppermute(value, 'tensor', pairs)]
  transfers between devices with their start and end apart: 36 -> 31, of which waited for: 9 -> 10; matrix products, arithmetic and copies ran while one was open for 23% -> 4% of each run, Pallas kernels for 11% -> 28%
where the time goes in v3:
time: 182 us; the launch traced here: 181 us
  waiting for transfers between devices  77.8 us (43%)
  Pallas kernels  57.2 us (31%)
  starting transfers between devices  32.9 us (18%)
  local copies, waits for them, and re-layouts  6.2 us (3%)
  other arithmetic  4.13 us (2%)
  between operations  2.9 us (2%)
    ppermute x8, waiting for transfers between devices, swap_in_plane(): return lax.ppermute(value, ('group', 'tensor'), pairs)  31.7 us
    ppermute x7, waiting for transfers between devices, tensor_xor(): return lax.ppermute(value, 'tensor', pairs)  29.4 us
    pallas_call x1, Pallas kernels, attend(): pl.pallas_call(functools.partial(kernel, len(pieces), heads), grid=(1,),...  17.8 us
    ppermute x13, waiting for transfers between devices, group_xor(): lax.ppermute(value, 'group', [(g, g ^ bits) for g in range(group_count)])  16.7 us
    pallas_call x4, Pallas kernels, feed_forward(): pl.pallas_call(functools.partial(feed_forward_kernel, len(pieces), len(ca...  15.9 us
    ppermute x7, starting transfers between devices, tensor_xor(): return lax.ppermute(value, 'tensor', pairs)  12 us
    ppermute x8, starting transfers between devices, swap_in_plane(): return lax.ppermute(value, ('group', 'tensor'), pairs)  9.8 us
    pallas_call x1, Pallas kernels, project(): pl.pallas_call(project_kernel, grid=(columns // width,), in_specs=[whole(...  8.86 us
  transfers between devices with their start and end apart: 31, of which 10 were waited for; matrix products, arithmetic and copies ran while one was open for 4% of the time, Pallas kernels for 28%

profile of v3, /device:TPU:0, one launch (start us, length us, event | category | flops | bytes accessed | tf_op | source)
XLA Modules:
  0.0 181.1 jit_solution(4065937148539696639)
XLA Ops:
  0.6 1.0 slice_bitcast_fusion
  1.6 2.4 %collective-permute-start = (bf16[32,1536]{1,0:T(8,128)(2,1)S(1)}, bf16[32,1536]{1,0:T(8,128)(2,1)S(1)}, u32[]{:S(2)}, u32[]{:S(2)}) collective-permute-start(bf16[32,1536]{1,0:T(8,128)(2,1)S(1)} %get-tuple-element.58), channel_id=1, source_target_pairs={{0,24},{8,16},{16,8},{24,0},{1,25},{9,17},{17,9},{25,1},{2,26},{10... | collective-permute-start | bytes 294920 | tf_op jit(solution)/shard_map/ppermute | solution.py:45
  4.1 0.6 collective-permute-start.1
  4.8 0.6 pad_add_fusion.side
  5.4 4.3 %shard_map.113 = (bf16[1536,256]{1,0:T(8,128)(2,1)}, bf16[768,256]{1,0:T(8,128)(2,1)}) custom-call(s32[2]{0:T(128)} %pad_add_fusion.side, bf16[2,1536,512]{2,1,0:T(8,128)(2,1)} %w_in.3, bf16[512,1536]{1,0:T(8,128)(2,1)} %w_down.3), custom_call_target="tpu_custom_call" | custom-call | tf_op jit(solution)/shard_map/pallas_call | solution.py:134
  9.6 2.8 %collective-permute-start.6 = (bf16[768,256]{1,0:T(8,128)(2,1)}, bf16[768,256]{1,0:T(8,128)(2,1)}, u32[]{:S(2)}, u32[]{:S(2)}) collective-permute-start(bf16[768,256]{1,0:T(8,128)(2,1)} %get-tuple-element.31.rest_1_), channel_id=1, source_target_pairs={{0,4},{1,5},{2,6},{3,7},{4,0},{5,1},{6,2},{7,3},{8,12},{9,13},{10,... | collective-permute-start | bytes 1179656 | tf_op jit(solution)/shard_map/ppermute | solution.py:31
  12.5 1.5 collective-permute-start.8
  14.0 0.6 dynamic_slice.3
  16.5 0.2 select_reduce_fusion
  16.7 0.5 fusion.2
  17.3 0.1 copy.19
  17.4 0.8 copy.20.cosine
  18.1 0.6 fusion.4
  18.7 0.8 pad_maximum_fusion.2.sine
  19.5 0.9 fusion.1
  20.4 1.6 collective-permute-start.3
  22.1 0.3 collective-permute-start.4
  22.4 2.5 %collective-permute-start.5 = (bf16[32,1536]{1,0:T(8,128)(2,1)S(1)}, bf16[32,1536]{1,0:T(8,128)(2,1)S(1)}, u32[]{:S(2)}, u32[]{:S(2)}) collective-permute-start(bf16[32,1536]{1,0:T(8,128)(2,1)S(1)} %fusion.1), channel_id=1, source_target_pairs={{0,6},{1,7},{2,4},{3,5},{4,2},{5,3},{6,0},{7,1},{8,14},{9,15},{10,... | collective-permute-start | bytes 294920 | tf_op jit(solution)/shard_map/ppermute | solution.py:31
  24.9 8.9 %shard_map.114.projected = bf16[256,3072]{1,0:T(8,128)(2,1)} custom-call(bf16[256,1536]{1,0:T(8,128)(2,1)} %hidden.2, f32[1,1536]{1,0:T(1,128)} %get-tuple-element.60.gain, bf16[1536,3072]{1,0:T(8,128)(2,1)} %weight.1, f32[256,96]{1,0:T(8,128)} %copy.20.cosine, f32[256,96]{1,0:T(8,128)} %pad_maximum_fusion.2.sine), custom_call_target="tpu_custom_call" | custom-call | flops 2415919104 | bytes 9437184 | tf_op jit(solution)/shard_map/pallas_call | solution.py:234
  33.8 3.6 %collective-permute-done.4 = bf16[32,1536]{1,0:T(8,128)(2,1)S(1)} collective-permute-done((bf16[32,1536]{1,0:T(8,128)(2,1)S(1)}, bf16[32,1536]{1,0:T(8,128)(2,1)S(1)}, u32[]{:S(2)}, u32[]{:S(2)}) %collective-permute-start.4) | collective-permute-done | bytes 98336 | tf_op jit(solution)/shard_map/ppermute | solution.py:31
  37.4 1.9 %collective-permute-start.7 = (bf16[128,1536]{1,0:T(8,128)(2,1)S(1)}, bf16[128,1536]{1,0:T(8,128)(2,1)S(1)}, u32[]{:S(2)}, u32[]{:S(2)}) collective-permute-start(bf16[128,1536]{1,0:T(8,128)(2,1)S(1)} %pad_maximum_fusion.1), channel_id=1, source_target_pairs={{0,16},{1,17},{2,18},{3,19},{4,20},{5,21},{6,22},{7,23},{8,9},{9,8... | collective-permute-start | bytes 1179656 | tf_op jit(solution)/shard_map/ppermute | solution.py:82
  39.3 6.0 %collective-permute-done.7 = bf16[128,1536]{1,0:T(8,128)(2,1)S(1)} collective-permute-done((bf16[128,1536]{1,0:T(8,128)(2,1)S(1)}, bf16[128,1536]{1,0:T(8,128)(2,1)S(1)}, u32[]{:S(2)}, u32[]{:S(2)}) %collective-permute-start.7) | collective-permute-done | bytes 393248 | tf_op jit(solution)/shard_map/ppermute | solution.py:82
  45.3 0.1 pad_maximum_fusion.rest_0_
  45.4 1.9 %collective-permute-start.9 = (bf16[256,1536]{1,0:T(8,128)(2,1)S(1)}, bf16[256,1536]{1,0:T(8,128)(2,1)}, u32[]{:S(2)}, u32[]{:S(2)}) collective-permute-start(bf16[256,1536]{1,0:T(8,128)(2,1)S(1)} %pad_maximum_fusion.rest_0_), channel_id=1, source_target_pairs={{0,1},{1,0},{2,3},{3,2},{4,5},{5,4},{6,7},{7,6},{8,24},{9,25},{10,... | collective-permute-start | bytes 2359304 | tf_op jit(solution)/shard_map/ppermute | solution.py:82
  47.2 10.3 %collective-permute-done.9.rest_1_ = bf16[256,1536]{1,0:T(8,128)(2,1)} collective-permute-done((bf16[256,1536]{1,0:T(8,128)(2,1)S(1)}, bf16[256,1536]{1,0:T(8,128)(2,1)}, u32[]{:S(2)}, u32[]{:S(2)}) %collective-permute-start.9) | collective-permute-done | bytes 786464 | tf_op jit(solution)/shard_map/ppermute | solution.py:82
  57.5 4.3 %collective-permute-start.12 = (bf16[1536,256]{1,0:T(8,128)(2,1)S(1)}, bf16[1536,256]{1,0:T(8,128)(2,1)S(1)}, u32[]{:S(2)}, u32[]{:S(2)}) collective-permute-start(bf16[1536,256]{1,0:T(8,128)(2,1)S(1)} %copy-done.1), channel_id=1, source_target_pairs={{0,4},{1,5},{2,6},{3,7},{4,0},{5,1},{6,2},{7,3},{8,12},{9,13},{10,... | collective-permute-start | bytes 2359304 | tf_op jit(solution)/shard_map/ppermute | solution.py:31
  61.8 1.4 collective-permute-start.13
  63.2 1.5 collective-permute-start.14
  64.7 0.6 pad_add_fusion.1.side
  65.3 4.1 %shard_map.116 = (bf16[1536,256]{1,0:T(8,128)(2,1)}, bf16[768,256]{1,0:T(8,128)(2,1)}) custom-call(s32[2]{0:T(128)} %pad_add_fusion.1.side, bf16[2,1536,512]{2,1,0:T(8,128)(2,1)} %w_in.3, bf16[512,1536]{1,0:T(8,128)(2,1)} %w_down.3), custom_call_target="tpu_custom_call" | custom-call | tf_op jit(solution)/shard_map/pallas_call | solution.py:134
  69.5 0.6 collective-permute-start.15
  70.1 0.6 collective-permute-start.16
  70.7 0.8 copy.21.row_ids
  71.5 17.8 %shard_map.115 = (bf16[256,1536]{1,0:T(8,128)(2,1)}, bf16[256,1536]{1,0:T(8,128)(2,1)}) custom-call(s32[256,1]{1,0:T(8,128)} %copy.21.row_ids, s32[1,256]{1,0:T(1,128)} %column_ids.1, bf16[256,3072]{1,0:T(8,128)(2,1)} %shard_map.114.projected, bf16[256,1536]{1,0:T(8,128)(2,1)} %hidden.2, f32[1,1536]{1,0:T(1,128)} %get-tuple-element.59.gain, ...), custom_call_target="tpu_custom_call" | custom-call | tf_op jit(solution)/shard_map/pallas_call | solution.py:357
  89.3 7.6 %collective-permute-done.12.rest_0_ = bf16[1536,256]{1,0:T(8,128)(2,1)S(1)} collective-permute-done((bf16[1536,256]{1,0:T(8,128)(2,1)S(1)}, bf16[1536,256]{1,0:T(8,128)(2,1)S(1)}, u32[]{:S(2)}, u32[]{:S(2)}) %collective-permute-start.12) | collective-permute-done | bytes 786464 | tf_op jit(solution)/shard_map/ppermute | solution.py:31
  96.9 1.4 collective-permute-start.19
  98.3 18.2 %collective-permute-done.17.left.rest_0_ = bf16[256,1536]{1,0:T(8,128)(2,1)S(1)} collective-permute-done((bf16[256,1536]{1,0:T(8,128)(2,1)}, bf16[256,1536]{1,0:T(8,128)(2,1)S(1)}, u32[]{:S(2)}, u32[]{:S(2)}) %collective-permute-start.17) | collective-permute-done | bytes 786464 | tf_op jit(solution)/shard_map/ppermute | solution.py:31
  116.5 1.5 collective-permute-start.20
  118.0 0.6 collective-permute-start.22
  118.5 1.5 collective-permute-start.21
  120.0 0.6 collective-permute-start.23
  120.6 0.2 convert_reduce_fusion
  120.8 0.1 select_reduce_fusion.1.table
  120.9 0.8 shard_map.119
  121.7 4.2 %shard_map.117 = (f32[256,1536]{1,0:T(8,128)S(1)}, f32[256,1536]{1,0:T(8,128)S(1)}) custom-call(bf16[256,1536]{1,0:T(8,128)(2,1)S(1)} %copy-done.2, bf16[256,1536]{1,0:T(8,128)(2,1)S(1)} %collective-permute-done.24.right, bf16[1536,256]{1,0:T(8,128)(2,1)S(1)} %copy-done.1, bf16[768,256]{1,0:T(8,128)(2,1)} %get-tuple-element.31.rest_1_, ...), custom_call_target="tpu_custom_call" | custom-call | tf_op jit(solution)/shard_map/pallas_call | solution.py:400
  125.9 4.1 %shard_map.118 = (f32[256,1536]{1,0:T(8,128)S(1)}, f32[256,1536]{1,0:T(8,128)S(1)}) custom-call(bf16[256,1536]{1,0:T(8,128)(2,1)S(1)} %collective-permute-done.17.left.rest_0_, bf16[256,1536]{1,0:T(8,128)(2,1)S(1)} %collective-permute-done.18.right, bf16[1536,256]{1,0:T(8,128)(2,1)S(1)} %copy-done.1, bf16[768,256]{1,0:T(8,128)(2,1)} %get-tuple-element.31.rest_1_, ...), custom_call_target="tpu_custom_call" | custom-call | tf_op jit(solution)/shard_map/pallas_call | solution.py:400
  130.0 11.2 %collective-permute-done.21.rest_5_ = bf16[768,256]{1,0:T(8,128)(2,1)S(1)} collective-permute-done((bf16[768,256]{1,0:T(8,128)(2,1)}, bf16[768,256]{1,0:T(8,128)(2,1)S(1)}, u32[]{:S(2)}, u32[]{:S(2)}) %collective-permute-start.21) | collective-permute-done | bytes 393248 | tf_op jit(solution)/shard_map/ppermute | solution.py:82
  141.1 4.2 %collective-permute-done.23.rest_7_ = bf16[768,256]{1,0:T(8,128)(2,1)S(1)} collective-permute-done((bf16[768,256]{1,0:T(8,128)(2,1)}, bf16[768,256]{1,0:T(8,128)(2,1)S(1)}, u32[]{:S(2)}, u32[]{:S(2)}) %collective-permute-start.23) | collective-permute-done | bytes 393248 | tf_op jit(solution)/shard_map/ppermute | solution.py:82
  145.4 3.7 %shard_map.120 = (f32[256,1536]{1,0:T(8,128)S(1)}, bf16[256,1536]{1,0:T(8,128)(2,1)S(1)}) custom-call(bf16[256,1536]{1,0:T(8,128)(2,1)S(1)} %collective-permute-done.17.left.rest_0_, bf16[256,1536]{1,0:T(8,128)(2,1)S(1)} %collective-permute-done.18.right, bf16[1536,256]{1,0:T(8,128)(2,1)S(1)} %collective-permute-done.12.rest_0_, ...), custom_call_target="tpu_custom_call" | custom-call | tf_op jit(solution)/shard_map/pallas_call | solution.py:400
  149.1 0.1 collective-permute-start.25
  149.2 0.5 collective-permute-start.26
  149.7 1.4 collective-permute-start.27
  151.1 0.3 collective-permute-done.25
  151.5 0.2 add_convert_fusion
  151.6 0.4 collective-permute-start.30
  152.0 9.6 %collective-permute-done.27.rest_2_ = bf16[128,1536]{1,0:T(8,128)(2,1)S(1)} collective-permute-done((bf16[128,1536]{1,0:T(8,128)(2,1)S(1)}, bf16[128,1536]{1,0:T(8,128)(2,1)S(1)}, u32[]{:S(2)}, u32[]{:S(2)}) %collective-permute-start.27) | collective-permute-done | bytes 393248 | tf_op jit(solution)/shard_map/ppermute | solution.py:45
  161.7 6.7 %collective-permute-done.28.rest_3_ = bf16[128,1536]{1,0:T(8,128)(2,1)S(1)} collective-permute-done((bf16[128,1536]{1,0:T(8,128)(2,1)S(1)}, bf16[128,1536]{1,0:T(8,128)(2,1)S(1)}, u32[]{:S(2)}, u32[]{:S(2)}) %collective-permute-start.28) | collective-permute-done | bytes 393248 | tf_op jit(solution)/shard_map/ppermute | solution.py:45
  168.3 3.9 %shard_map.121 = (f32[256,1536]{1,0:T(8,128)S(1)}, bf16[256,1536]{1,0:T(8,128)(2,1)S(1)}) custom-call(bf16[256,1536]{1,0:T(8,128)(2,1)S(1)} %copy-done.2, bf16[256,1536]{1,0:T(8,128)(2,1)S(1)} %collective-permute-done.24.right, bf16[1536,256]{1,0:T(8,128)(2,1)S(1)} %collective-permute-done.12.rest_0_, bf16[768,256]{1,0:T(8,128)(2,1)} %collective-permute-done.6.rest_1_, ...), custom_call_target="tpu_custom_call" | custom-call | tf_op jit(solution)/shard_map/pallas_call | solution.py:400
  172.2 1.2 copy-done.6
  173.4 1.0 collective-permute-start.29
  174.4 2.6 %shard_map.122 = bf16[4,128,1536]{2,1,0:T(8,128)(2,1)} custom-call(s32[1]{0:T(128)} %bitcast.12.group, bf16[128,1536]{1,0:T(8,128)(2,1)} %copy-done.5, bf16[128,1536]{1,0:T(8,128)(2,1)} %copy-done.11, bf16[128,1536]{1,0:T(8,128)(2,1)} %copy-done.12, bf16[128,1536]{1,0:T(8,128)(2,1)} %copy-done.13), custom_call_target="tpu_custom_call" | custom-call | tf_op jit(solution)/shard_map/pallas_call | solution.py:474
  177.0 0.9 copy-done.9
  177.9 0.3 copy-done.10
  178.2 3.0 %shard_map.123 = bf16[256,1536]{1,0:T(8,128)(2,1)} custom-call(f32[256,1536]{1,0:T(8,128)} %copy-done.6, bf16[256,1536]{1,0:T(8,128)(2,1)} %copy-done.10, bf16[256,1536]{1,0:T(8,128)(2,1)} %copy-done.9), custom_call_target="tpu_custom_call" | custom-call | tf_op jit(solution)/shard_map/pallas_call | solution.py:418
  (66 shorter events, 0.3 us)
Async XLA Ops:
  1.6 17.9 %collective-permute-start = (bf16[32,1536]{1,0:T(8,128)(2,1)S(1)}, bf16[32,1536]{1,0:T(8,128)(2,1)S(1)}, u32[]{:S(2)}, u32[]{:S(2)}) collective-permute-start(bf16[32,1536]{1,0:T(8,128)(2,1)S(1)} %get-tuple-element.58), channel_id=1, source_target_pairs={{0,24},{8,16},{16,8},{24,0},{1,25},{9,17},{17,9},{25,1},{2,26},{10... | collective-permute-start | bytes 294920 | tf_op jit(solution)/shard_map/ppermute | solution.py:45
  4.1 15.4 %collective-permute-start.1 = (bf16[32,1536]{1,0:T(8,128)(2,1)S(1)}, bf16[32,1536]{1,0:T(8,128)(2,1)S(1)}, u32[]{:S(2)}, u32[]{:S(2)}) collective-permute-start(bf16[32,1536]{1,0:T(8,128)(2,1)S(1)} %get-tuple-element.57), channel_id=1, source_target_pairs={{0,16},{8,24},{16,0},{24,8},{1,17},{9,25},{17,1},{25,9},{2,18},{10... | collective-permute-start | bytes 294920 | tf_op jit(solution)/shard_map/ppermute | solution.py:45
  4.7 14.8 %collective-permute-start.2 = (bf16[32,1536]{1,0:T(8,128)(2,1)S(1)}, bf16[32,1536]{1,0:T(8,128)(2,1)S(1)}, u32[]{:S(2)}, u32[]{:S(2)}) collective-permute-start(bf16[32,1536]{1,0:T(8,128)(2,1)S(1)} %get-tuple-element.56), channel_id=1, source_target_pairs={{0,8},{8,0},{16,24},{24,16},{1,9},{9,1},{17,25},{25,17},{2,10},{10... | collective-permute-start | bytes 294920 | tf_op jit(solution)/shard_map/ppermute | solution.py:45
  5.4 8.6 %copy-start.17 = (s32[8]{0:T(128)S(1)}, s32[8]{0:T(128)}, u32[]{:S(2)}) copy-start(s32[8]{0:T(128)} %param.18) | copy-start | bytes 100
  5.4 11.2 %copy-start.14 = (s32[1,256]{1,0:T(1,128)S(1)}, s32[1,256]{1,0:T(1,128)}, u32[]{:S(2)}) copy-start(s32[1,256]{1,0:T(1,128)} %column_ids.1) | copy-start | bytes 3076
  5.4 12.8 %copy-start.15 = (f32[2,1536]{1,0:T(2,128)S(1)}, f32[2,1536]{1,0:T(2,128)}, u32[]{:S(2)}) copy-start(f32[2,1536]{1,0:T(2,128)} %param.12) | copy-start | bytes 36868
  9.6 27.8 %collective-permute-start.6 = (bf16[768,256]{1,0:T(8,128)(2,1)}, bf16[768,256]{1,0:T(8,128)(2,1)}, u32[]{:S(2)}, u32[]{:S(2)}) collective-permute-start(bf16[768,256]{1,0:T(8,128)(2,1)} %get-tuple-element.31.rest_1_), channel_id=1, source_target_pairs={{0,4},{1,5},{2,6},{3,7},{4,0},{5,1},{6,2},{7,3},{8,12},{9,13},{10,... | collective-permute-start | bytes 1179656 | tf_op jit(solution)/shard_map/ppermute | solution.py:31
  12.5 32.9 %collective-permute-start.8 = (bf16[1536,256]{1,0:T(8,128)(2,1)}, bf16[1536,256]{1,0:T(8,128)(2,1)S(1)}, u32[]{:S(2)}, u32[]{:S(2)}) collective-permute-start(bf16[1536,256]{1,0:T(8,128)(2,1)} %get-tuple-element.35.rest_0_), channel_id=1, source_target_pairs={{0,1},{1,0},{2,3},{3,2},{4,5},{5,4},{6,7},{7,6},{8,9},{9,8},{10,11... | collective-permute-start | bytes 2359304 | tf_op jit(solution)/shard_map/ppermute | solution.py:41
  20.4 13.3 %collective-permute-start.3 = (bf16[32,1536]{1,0:T(8,128)(2,1)S(1)}, bf16[32,1536]{1,0:T(8,128)(2,1)S(1)}, u32[]{:S(2)}, u32[]{:S(2)}) collective-permute-start(bf16[32,1536]{1,0:T(8,128)(2,1)S(1)} %fusion.1), channel_id=1, source_target_pairs={{0,2},{1,3},{2,0},{3,1},{4,6},{5,7},{6,4},{7,5},{8,10},{9,11},{10,... | collective-permute-start | bytes 294920 | tf_op jit(solution)/shard_map/ppermute | solution.py:31
  22.1 15.3 %collective-permute-start.4 = (bf16[32,1536]{1,0:T(8,128)(2,1)S(1)}, bf16[32,1536]{1,0:T(8,128)(2,1)S(1)}, u32[]{:S(2)}, u32[]{:S(2)}) collective-permute-start(bf16[32,1536]{1,0:T(8,128)(2,1)S(1)} %fusion.1), channel_id=1, source_target_pairs={{0,4},{1,5},{2,6},{3,7},{4,0},{5,1},{6,2},{7,3},{8,12},{9,13},{10,... | collective-permute-start | bytes 294920 | tf_op jit(solution)/shard_map/ppermute | solution.py:31
  22.4 15.0 %collective-permute-start.5 = (bf16[32,1536]{1,0:T(8,128)(2,1)S(1)}, bf16[32,1536]{1,0:T(8,128)(2,1)S(1)}, u32[]{:S(2)}, u32[]{:S(2)}) collective-permute-start(bf16[32,1536]{1,0:T(8,128)(2,1)S(1)} %fusion.1), channel_id=1, source_target_pairs={{0,6},{1,7},{2,4},{3,5},{4,2},{5,3},{6,0},{7,1},{8,14},{9,15},{10,... | collective-permute-start | bytes 294920 | tf_op jit(solution)/shard_map/ppermute | solution.py:31
  33.8 23.8 %copy-start.1 = (bf16[1536,256]{1,0:T(8,128)(2,1)S(1)}, bf16[1536,256]{1,0:T(8,128)(2,1)}, u32[]{:S(2)}) copy-start(bf16[1536,256]{1,0:T(8,128)(2,1)} %get-tuple-element.35.rest_0_) | copy-start | bytes 2359300
  37.4 7.8 %collective-permute-start.7 = (bf16[128,1536]{1,0:T(8,128)(2,1)S(1)}, bf16[128,1536]{1,0:T(8,128)(2,1)S(1)}, u32[]{:S(2)}, u32[]{:S(2)}) collective-permute-start(bf16[128,1536]{1,0:T(8,128)(2,1)S(1)} %pad_maximum_fusion.1), channel_id=1, source_target_pairs={{0,16},{1,17},{2,18},{3,19},{4,20},{5,21},{6,22},{7,23},{8,9},{9,8... | collective-permute-start | bytes 1179656 | tf_op jit(solution)/shard_map/ppermute | solution.py:82
  45.3 24.1 %copy-start.8 = (bf16[256,1536]{1,0:T(8,128)(2,1)}, bf16[256,1536]{1,0:T(8,128)(2,1)S(1)}, u32[]{:S(2)}) copy-start(bf16[256,1536]{1,0:T(8,128)(2,1)S(1)} %pad_maximum_fusion.rest_0_) | copy-start | bytes 2359300
  45.4 12.2 %collective-permute-start.9 = (bf16[256,1536]{1,0:T(8,128)(2,1)S(1)}, bf16[256,1536]{1,0:T(8,128)(2,1)}, u32[]{:S(2)}, u32[]{:S(2)}) collective-permute-start(bf16[256,1536]{1,0:T(8,128)(2,1)S(1)} %pad_maximum_fusion.rest_0_), channel_id=1, source_target_pairs={{0,1},{1,0},{2,3},{3,2},{4,5},{5,4},{6,7},{7,6},{8,24},{9,25},{10,... | collective-permute-start | bytes 2359304 | tf_op jit(solution)/shard_map/ppermute | solution.py:82
  47.2 22.2 %collective-permute-start.10 = (bf16[256,1536]{1,0:T(8,128)(2,1)S(1)}, bf16[256,1536]{1,0:T(8,128)(2,1)}, u32[]{:S(2)}, u32[]{:S(2)}) collective-permute-start(bf16[256,1536]{1,0:T(8,128)(2,1)S(1)} %pad_maximum_fusion.rest_0_), channel_id=1, source_target_pairs={{0,8},{8,0},{16,24},{24,16},{1,9},{9,1},{17,25},{25,17},{2,10},{10... | collective-permute-start | bytes 2359304 | tf_op jit(solution)/shard_map/ppermute | solution.py:45
  57.5 12.6 %collective-permute-start.11 = (bf16[256,1536]{1,0:T(8,128)(2,1)}, bf16[256,1536]{1,0:T(8,128)(2,1)}, u32[]{:S(2)}, u32[]{:S(2)}) collective-permute-start(bf16[256,1536]{1,0:T(8,128)(2,1)} %collective-permute-done.9.rest_1_), channel_id=1, source_target_pairs={{0,8},{8,0},{16,24},{24,16},{1,9},{9,1},{17,25},{25,17},{2,10},{10... | collective-permute-start | bytes 2359304 | tf_op jit(solution)/shard_map/ppermute | solution.py:45
  57.5 39.4 %collective-permute-start.12 = (bf16[1536,256]{1,0:T(8,128)(2,1)S(1)}, bf16[1536,256]{1,0:T(8,128)(2,1)S(1)}, u32[]{:S(2)}, u32[]{:S(2)}) collective-permute-start(bf16[1536,256]{1,0:T(8,128)(2,1)S(1)} %copy-done.1), channel_id=1, source_target_pairs={{0,4},{1,5},{2,6},{3,7},{4,0},{5,1},{6,2},{7,3},{8,12},{9,13},{10,... | collective-permute-start | bytes 2359304 | tf_op jit(solution)/shard_map/ppermute | solution.py:31
  61.8 35.1 %collective-permute-start.13 = (bf16[1536,256]{1,0:T(8,128)(2,1)S(1)}, bf16[1536,256]{1,0:T(8,128)(2,1)}, u32[]{:S(2)}, u32[]{:S(2)}) collective-permute-start(bf16[1536,256]{1,0:T(8,128)(2,1)S(1)} %collective-permute-done.8.rest_4_), channel_id=1, source_target_pairs={{0,16},{8,24},{16,0},{24,8},{1,17},{9,25},{17,1},{25,9},{2,18},{10... | collective-permute-start | bytes 2359304 | tf_op jit(solution)/shard_map/ppermute | solution.py:45
  63.2 26.1 %collective-permute-start.14 = (bf16[768,256]{1,0:T(8,128)(2,1)}, bf16[768,256]{1,0:T(8,128)(2,1)}, u32[]{:S(2)}, u32[]{:S(2)}) collective-permute-start(bf16[768,256]{1,0:T(8,128)(2,1)} %get-tuple-element.31.rest_1_), channel_id=1, source_target_pairs={{0,1},{1,0},{2,3},{3,2},{4,5},{5,4},{6,7},{7,6},{8,9},{9,8},{10,11... | collective-permute-start | bytes 1179656 | tf_op jit(solution)/shard_map/ppermute | solution.py:41
  69.5 19.9 %collective-permute-start.15 = (bf16[768,256]{1,0:T(8,128)(2,1)}, bf16[768,256]{1,0:T(8,128)(2,1)}, u32[]{:S(2)}, u32[]{:S(2)}) collective-permute-start(bf16[768,256]{1,0:T(8,128)(2,1)} %get-tuple-element.38.rest_3_), channel_id=1, source_target_pairs={{0,1},{1,0},{2,3},{3,2},{4,5},{5,4},{6,7},{7,6},{8,9},{9,8},{10,11... | collective-permute-start | bytes 1179656 | tf_op jit(solution)/shard_map/ppermute | solution.py:41
  70.1 19.3 %collective-permute-start.16 = (bf16[768,256]{1,0:T(8,128)(2,1)}, bf16[768,256]{1,0:T(8,128)(2,1)}, u32[]{:S(2)}, u32[]{:S(2)}) collective-permute-start(bf16[768,256]{1,0:T(8,128)(2,1)} %collective-permute-done.6.rest_1_), channel_id=1, source_target_pairs={{0,16},{1,17},{2,18},{3,19},{4,20},{5,21},{6,22},{7,23},{8,9},{9,8... | collective-permute-start | bytes 1179656 | tf_op jit(solution)/shard_map/ppermute | solution.py:82
  71.5 49.1 %copy-start.16 = (s32[16,1]{0,1:T(1,128)S(1)}, s32[16,1]{0,1:T(1,128)}, u32[]{:S(2)}) copy-start(s32[16,1]{0,1:T(1,128)} %param.19) | copy-start | bytes 196
  71.5 49.3 %copy-start = (bf16[256,3072]{1,0:T(8,128)(2,1)S(1)}, bf16[256,3072]{1,0:T(8,128)(2,1)}, u32[]{:S(2)}) copy-start(bf16[256,3072]{1,0:T(8,128)(2,1)} %shard_map.114.projected) | copy-start | bytes 4718596
  89.3 32.3 %copy-start.2 = (bf16[256,1536]{1,0:T(8,128)(2,1)S(1)}, bf16[256,1536]{1,0:T(8,128)(2,1)}, u32[]{:S(2)}) copy-start(bf16[256,1536]{1,0:T(8,128)(2,1)} %get-tuple-element.51.left) | copy-start | bytes 2359300
  89.3 32.3 %copy-start.3 = (bf16[1536,256]{1,0:T(8,128)(2,1)S(1)}, bf16[1536,256]{1,0:T(8,128)(2,1)}, u32[]{:S(2)}) copy-start(bf16[1536,256]{1,0:T(8,128)(2,1)} %get-tuple-element.40.rest_2_) | copy-start | bytes 2359300
  89.3 32.3 %copy-start.4 = (bf16[768,256]{1,0:T(8,128)(2,1)S(1)}, bf16[768,256]{1,0:T(8,128)(2,1)}, u32[]{:S(2)}) copy-start(bf16[768,256]{1,0:T(8,128)(2,1)} %get-tuple-element.38.rest_3_) | copy-start | bytes 1179652
  96.9 19.6 %collective-permute-start.17 = (bf16[256,1536]{1,0:T(8,128)(2,1)}, bf16[256,1536]{1,0:T(8,128)(2,1)S(1)}, u32[]{:S(2)}, u32[]{:S(2)}) collective-permute-start(bf16[256,1536]{1,0:T(8,128)(2,1)} %get-tuple-element.51.left), channel_id=1, source_target_pairs={{0,2},{1,3},{2,0},{3,1},{4,6},{5,7},{6,4},{7,5},{8,10},{9,11},{10,... | collective-permute-start | bytes 2359304 | tf_op jit(solution)/shard_map/ppermute | solution.py:31
  96.9 21.1 %collective-permute-start.19 = (bf16[1536,256]{1,0:T(8,128)(2,1)S(1)}, bf16[1536,256]{1,0:T(8,128)(2,1)S(1)}, u32[]{:S(2)}, u32[]{:S(2)}) collective-permute-start(bf16[1536,256]{1,0:T(8,128)(2,1)S(1)} %collective-permute-done.12.rest_0_), channel_id=1, source_target_pairs={{0,16},{1,17},{2,18},{3,19},{4,20},{5,21},{6,22},{7,23},{8,9},{9,8... | collective-permute-start | bytes 2359304 | tf_op jit(solution)/shard_map/ppermute | solution.py:82
  98.3 21.7 %collective-permute-start.24 = (bf16[256,1536]{1,0:T(8,128)(2,1)}, bf16[256,1536]{1,0:T(8,128)(2,1)S(1)}, u32[]{:S(2)}, u32[]{:S(2)}) collective-permute-start(bf16[256,1536]{1,0:T(8,128)(2,1)} %get-tuple-element.51.left), channel_id=1, source_target_pairs={{0,8},{8,0},{16,24},{24,16},{1,9},{9,1},{17,25},{25,17},{2,10},{10... | collective-permute-start | bytes 2359304 | tf_op jit(solution)/shard_map/ppermute | solution.py:45
  116.5 9.4 %collective-permute-start.18 = (bf16[256,1536]{1,0:T(8,128)(2,1)S(1)}, bf16[256,1536]{1,0:T(8,128)(2,1)S(1)}, u32[]{:S(2)}, u32[]{:S(2)}) collective-permute-start(bf16[256,1536]{1,0:T(8,128)(2,1)S(1)} %collective-permute-done.17.left.rest_0_), channel_id=1, source_target_pairs={{0,8},{8,0},{16,24},{24,16},{1,9},{9,1},{17,25},{25,17},{2,10},{10... | collective-permute-start | bytes 2359304 | tf_op jit(solution)/shard_map/ppermute | solution.py:45
  116.5 28.8 %collective-permute-start.20 = (bf16[1536,256]{1,0:T(8,128)(2,1)S(1)}, bf16[1536,256]{1,0:T(8,128)(2,1)S(1)}, u32[]{:S(2)}, u32[]{:S(2)}) collective-permute-start(bf16[1536,256]{1,0:T(8,128)(2,1)S(1)} %collective-permute-done.12.rest_0_), channel_id=1, source_target_pairs={{0,1},{1,0},{2,3},{3,2},{4,5},{5,4},{6,7},{7,6},{8,24},{9,25},{10,... | collective-permute-start | bytes 2359304 | tf_op jit(solution)/shard_map/ppermute | solution.py:82
  118.0 27.4 %collective-permute-start.22 = (bf16[1536,256]{1,0:T(8,128)(2,1)S(1)}, bf16[1536,256]{1,0:T(8,128)(2,1)S(1)}, u32[]{:S(2)}, u32[]{:S(2)}) collective-permute-start(bf16[1536,256]{1,0:T(8,128)(2,1)S(1)} %collective-permute-done.19.rest_2_), channel_id=1, source_target_pairs={{0,1},{1,0},{2,3},{3,2},{4,5},{5,4},{6,7},{7,6},{8,24},{9,25},{10,... | collective-permute-start | bytes 2359304 | tf_op jit(solution)/shard_map/ppermute | solution.py:82
  118.5 22.6 %collective-permute-start.21 = (bf16[768,256]{1,0:T(8,128)(2,1)}, bf16[768,256]{1,0:T(8,128)(2,1)S(1)}, u32[]{:S(2)}, u32[]{:S(2)}) collective-permute-start(bf16[768,256]{1,0:T(8,128)(2,1)} %collective-permute-done.6.rest_1_), channel_id=1, source_target_pairs={{0,1},{1,0},{2,3},{3,2},{4,5},{5,4},{6,7},{7,6},{8,24},{9,25},{10,... | collective-permute-start | bytes 1179656 | tf_op jit(solution)/shard_map/ppermute | solution.py:82
  120.0 25.3 %collective-permute-start.23 = (bf16[768,256]{1,0:T(8,128)(2,1)}, bf16[768,256]{1,0:T(8,128)(2,1)S(1)}, u32[]{:S(2)}, u32[]{:S(2)}) collective-permute-start(bf16[768,256]{1,0:T(8,128)(2,1)} %collective-permute-done.16.rest_3_), channel_id=1, source_target_pairs={{0,1},{1,0},{2,3},{3,2},{4,5},{5,4},{6,7},{7,6},{8,24},{9,25},{10,... | collective-permute-start | bytes 1179656 | tf_op jit(solution)/shard_map/ppermute | solution.py:82
  121.6 23.7 %copy-start.5 = (bf16[128,1536]{1,0:T(8,128)(2,1)}, bf16[128,1536]{1,0:T(8,128)(2,1)S(1)}, u32[]{:S(2)}) copy-start(bf16[128,1536]{1,0:T(8,128)(2,1)S(1)} %get-tuple-element.45.rest_10_.rest_0_) | copy-start | bytes 1179652
  149.1 2.4 %collective-permute-start.25 = (bf16[256,1536]{1,0:T(8,128)(2,1)S(1)}, bf16[256,1536]{1,0:T(8,128)(2,1)S(1)}, u32[]{:S(2)}, u32[]{:S(2)}) collective-permute-start(bf16[256,1536]{1,0:T(8,128)(2,1)S(1)} %get-tuple-element.47), channel_id=1, source_target_pairs={{0,8},{8,0},{16,24},{24,16},{1,9},{9,1},{17,25},{25,17},{2,10},{10... | collective-permute-start | bytes 2359304 | tf_op jit(solution)/shard_map/ppermute | solution.py:45
  149.2 2.8 %collective-permute-start.26 = (bf16[128,1536]{1,0:T(8,128)(2,1)S(1)}, bf16[128,1536]{1,0:T(8,128)(2,1)S(1)}, u32[]{:S(2)}, u32[]{:S(2)}) collective-permute-start(bf16[128,1536]{1,0:T(8,128)(2,1)S(1)} %get-tuple-element.48), channel_id=1, source_target_pairs={{0,8},{8,0},{16,24},{24,16},{1,9},{9,1},{17,25},{25,17},{2,10},{10... | collective-permute-start | bytes 1179656 | tf_op jit(solution)/shard_map/ppermute | solution.py:45
  149.7 12.0 %collective-permute-start.27 = (bf16[128,1536]{1,0:T(8,128)(2,1)S(1)}, bf16[128,1536]{1,0:T(8,128)(2,1)S(1)}, u32[]{:S(2)}, u32[]{:S(2)}) collective-permute-start(bf16[128,1536]{1,0:T(8,128)(2,1)S(1)} %get-tuple-element.49), channel_id=1, source_target_pairs={{0,16},{8,24},{16,0},{24,8},{1,17},{9,25},{17,1},{25,9},{2,18},{10... | collective-permute-start | bytes 1179656 | tf_op jit(solution)/shard_map/ppermute | solution.py:45
  151.1 17.3 %collective-permute-start.28 = (bf16[128,1536]{1,0:T(8,128)(2,1)S(1)}, bf16[128,1536]{1,0:T(8,128)(2,1)S(1)}, u32[]{:S(2)}, u32[]{:S(2)}) collective-permute-start(bf16[128,1536]{1,0:T(8,128)(2,1)S(1)} %get-tuple-element.50), channel_id=1, source_target_pairs={{0,24},{8,16},{16,8},{24,0},{1,25},{9,17},{17,9},{25,1},{2,26},{10... | collective-permute-start | bytes 1179656 | tf_op jit(solution)/shard_map/ppermute | solution.py:45
  151.5 16.9 %copy-start.7 = (bf16[256,1536]{1,0:T(8,128)(2,1)S(1)}, bf16[256,1536]{1,0:T(8,128)(2,1)}, u32[]{:S(2)}) copy-start(bf16[256,1536]{1,0:T(8,128)(2,1)} %get-tuple-element.52.rest_10_) | copy-start | bytes 2359300
  151.6 25.4 %collective-permute-start.30 = (bf16[256,1536]{1,0:T(8,128)(2,1)S(1)}, bf16[256,1536]{1,0:T(8,128)(2,1)S(1)}, u32[]{:S(2)}, u32[]{:S(2)}) collective-permute-start(bf16[256,1536]{1,0:T(8,128)(2,1)S(1)} %add_convert_fusion), channel_id=1, source_target_pairs={{0,2},{1,3},{2,0},{3,1},{4,6},{5,7},{6,4},{7,5},{8,10},{9,11},{10,... | collective-permute-start | bytes 2359304 | tf_op jit(solution)/shard_map/ppermute | solution.py:31
  152.0 20.2 %copy-start.11 = (bf16[128,1536]{1,0:T(8,128)(2,1)}, bf16[128,1536]{1,0:T(8,128)(2,1)S(1)}, u32[]{:S(2)}) copy-start(bf16[128,1536]{1,0:T(8,128)(2,1)S(1)} %collective-permute-done.26.rest_1_) | copy-start | bytes 1179652
  161.7 10.6 %copy-start.12 = (bf16[128,1536]{1,0:T(8,128)(2,1)}, bf16[128,1536]{1,0:T(8,128)(2,1)S(1)}, u32[]{:S(2)}) copy-start(bf16[128,1536]{1,0:T(8,128)(2,1)S(1)} %collective-permute-done.27.rest_2_) | copy-start | bytes 1179652
  168.3 3.9 %copy-start.13 = (bf16[128,1536]{1,0:T(8,128)(2,1)}, bf16[128,1536]{1,0:T(8,128)(2,1)S(1)}, u32[]{:S(2)}) copy-start(bf16[128,1536]{1,0:T(8,128)(2,1)S(1)} %collective-permute-done.28.rest_3_) | copy-start | bytes 1179652
  172.2 1.2 copy-start.6
  173.4 3.6 %collective-permute-start.29 = (bf16[256,1536]{1,0:T(8,128)(2,1)S(1)}, bf16[256,1536]{1,0:T(8,128)(2,1)S(1)}, u32[]{:S(2)}, u32[]{:S(2)}) collective-permute-start(bf16[256,1536]{1,0:T(8,128)(2,1)S(1)} %get-tuple-element.54), channel_id=1, source_target_pairs={{0,8},{8,0},{16,24},{24,16},{1,9},{9,1},{17,25},{25,17},{2,10},{10... | collective-permute-start | bytes 2359304 | tf_op jit(solution)/shard_map/ppermute | solution.py:45
  177.0 0.9 copy-start.9
  177.0 1.1 copy-start.10

commit v4 on v3

--- a/solution.py
+++ b/solution.py
@@ -95,7 +95,7 @@
     return [swap_in_plane(v, 1, group_count, tensor_count) for v in pair]
 
 
-def pack_kernel(side, w_in, w_down, inward, down):
+def pack_kernel(side, w_in, w_down, inward, down, *halves):
     part = w_in.shape[2] // 2
     columns = pl.ds(pl.multiple_of(side[0] * part, part), part)
     for half in range(2):
@@ -104,6 +104,11 @@
         down[block * part : (block + 1) * part, :] = w_down[
             columns, block * 2 * part : (block + 1) * 2 * part
         ]
+    for step, out in enumerate(halves):
+
+        @pl.when(pl.program_id(0) == step)
+        def _():
+            out[...] = inward[...]
 
 
 def join_piece(gate, up, down):
@@ -119,33 +124,34 @@
     return inward[:, :part], inward[:, part:], jnp.concatenate(blocks, axis=1)
 
 
-def own_piece(w_in, w_down, side):
+def own_piece(w_in, w_down, side, halved):
     core = lax.axis_index("group") % 2
     depth, part = w_in.shape[1], w_in.shape[2] // 4
     if part % 128:
         start = (core * 2 + side) * part
-        return join_piece(
+        inward, down = join_piece(
             lax.dynamic_slice_in_dim(w_in[0], start, part, 1),
             lax.dynamic_slice_in_dim(w_in[1], start, part, 1),
             lax.dynamic_slice_in_dim(w_down, start, part, 0),
         )
-    steps = depth // (4 * part)
+        return [inward, down, inward[: depth // 2], inward[depth // 2 :]]
     shapes = [(depth, 2 * part), (depth // 2, 2 * part)]
+    halves = [(depth // 2, 2 * part)] * (2 if halved else 0)
     return pl.pallas_call(
         pack_kernel,
         grid_spec=pltpu.PrefetchScalarGridSpec(
             num_scalar_prefetch=1,
-            grid=(steps,),
+            grid=(2,),
             in_specs=[
-                pl.BlockSpec((2, depth // steps, 2 * part), lambda i, at: (0, i, at[1])),
-                pl.BlockSpec((2 * part, depth // steps), lambda i, at: (at[1], i)),
+                pl.BlockSpec((2, depth // 2, 2 * part), lambda i, at: (0, i, at[1])),
+                pl.BlockSpec((2 * part, depth // 2), lambda i, at: (at[1], i)),
             ],
             out_specs=[
-                pl.BlockSpec((rows // steps, columns), lambda i, at: (i, 0))
-                for rows, columns in shapes
-            ],
+                pl.BlockSpec((rows // 2, columns), lambda i, at: (i, 0)) for rows, columns in shapes
+            ]
+            + [pl.BlockSpec(shape, lambda i, at: (0, 0)) for shape in halves],
         ),
-        out_shape=[jax.ShapeDtypeStruct(shape, w_in.dtype) for shape in shapes],
+        out_shape=[jax.ShapeDtypeStruct(shape, w_in.dtype) for shape in shapes + halves],
         compiler_params=pltpu.CompilerParams(vmem_limit_bytes=60 << 20),
     )(jnp.stack([side, core]).astype(jnp.int32), w_in, w_down)
 
@@ -156,7 +162,8 @@
         return pieces
     merged = []
     for at in range(0, len(pieces), count):
-        gates, ups, downs = zip(*[split_piece(p) for p in pieces[at : at + count]])
+        joined = [(jnp.concatenate(p[:-1]), p[-1]) for p in pieces[at : at + count]]
+        gates, ups, downs = zip(*[split_piece(p) for p in joined])
         merged.append(
             join_piece(
                 jnp.concatenate(gates, axis=1),
@@ -365,16 +372,22 @@
     )(*resident, *remote)
 
 
-def feed_forward_kernel(piece_count, carry_count, left, right, *rest):
-    weights = rest[: 2 * piece_count]
-    carries = rest[2 * piece_count : 2 * piece_count + carry_count]
+def feed_forward_kernel(chunks, piece_count, carry_count, left, right, *rest):
+    weights = rest[: chunks * piece_count]
+    carries = rest[chunks * piece_count : chunks * piece_count + carry_count]
     left_out, right_out, tokens, acts = rest[-4:]
     rows, depth = left.shape
     part = weights[0].shape[1] // 2
     tokens[:rows, :] = left[...]
     tokens[rows:, :] = right[...]
     for index in range(piece_count):
-        both = jnp.dot(tokens[...], weights[2 * index][...], preferred_element_type=jnp.float32)
+        both, at = 0.0, 0
+        for weight in weights[chunks * index : chunks * (index + 1) - 1]:
+            columns = slice(at, at + weight.shape[0])
+            both += jnp.dot(
+                tokens[:, columns], weight[...], preferred_element_type=jnp.float32
+            )
+            at += weight.shape[0]
         gate, up = both[:, :part], both[:, part:]
         acts[:, index * part : (index + 1) * part] = (gate / (1.0 + jnp.exp(-gate)) * up).astype(
             jnp.bfloat16
@@ -382,7 +395,7 @@
     for block in range(depth // (2 * part)):
         columns = slice(block * 2 * part, (block + 1) * 2 * part)
         weight = jnp.concatenate(
-            [v[block * part : (block + 1) * part, :] for v in weights[1::2]]
+            [v[block * part : (block + 1) * part, :] for v in weights[chunks - 1 :: chunks]]
         )
         sums = jnp.dot(acts[...], weight, preferred_element_type=jnp.float32)
         for side, out in enumerate((left_out, right_out)):
@@ -398,7 +411,7 @@
     chunks = [chunk for piece in pieces for chunk in piece]
     out = [jax.ShapeDtypeStruct((rows, depth), dtype) for dtype in (jnp.float32, right_dtype)]
     return pl.pallas_call(
-        functools.partial(feed_forward_kernel, len(pieces), len(carries)),
+        functools.partial(feed_forward_kernel, len(pieces[0]), len(pieces), len(carries)),
         grid=(1,),
         in_specs=wholes([left, right, *chunks, *carries]) + [ANYWHERE] * len(earlier),
         out_specs=wholes(out),
@@ -412,16 +425,20 @@
 
 
 def add_rows(first, *others):
+    arrays = [first, *others]
+    rows, columns = first.shape
+    block = pl.BlockSpec((rows // 4, columns), lambda i: (i, 0))
+
     def kernel(*refs):
         refs[-1][...] = sum(ref[...].astype(jnp.float32) for ref in refs[:-1]).astype(jnp.bfloat16)
 
     return pl.pallas_call(
         kernel,
-        grid=(1,),
-        in_specs=wholes([first, *others]),
-        out_specs=whole(first),
+        grid=(4,),
+        in_specs=[block] * len(arrays),
+        out_specs=block,
         out_shape=jax.ShapeDtypeStruct(first.shape, jnp.bfloat16),
-    )(first, *others)
+    )(*arrays)
 
 
 def select_kernel(group_count, table, projected, *rest):
@@ -501,30 +518,32 @@
     segment = request_ids[0]
     quarter = own_quarter(prefix_cache[0], prefix_owner, group_count)
     across = lax.axis_index("group") // 2
-    mine = own_piece(w_in, w_down, across)
+    *mine, upper, lower = own_piece(w_in, w_down, across, True)
     far_down = tensor_xor(mine[1], tensor_count, 2)
-    inward = [tensor_turn(mine[0], tensor_count, step) for step in turns]
+    beside = [[tensor_turn(v, tensor_count, step) for v in mine] for step in turns]
     along_z = [tensor_xor(quarter, tensor_count, bits) for bits in range(1, Z_SIZE)]
     projected = project(
         after(hidden_in, mine[0], quarter),
         norm_gains[0],
         query_key_value_weight,
-        positions(segment),
+        positions(after(segment, quarter)),
         [],
     )
     line = after(jnp.concatenate([quarter] + along_z), projected, far_down)
-    other = own_piece(w_in, w_down, after(1 - across, projected))
-    far_in = tensor_xor(after(mine[0], line), tensor_count, 2)
+    other = own_piece(w_in, w_down, after(1 - across, projected), False)[:2]
+    far_upper = tensor_xor(after(upper, line), tensor_count, 2)
     lines = plane_pair(line, *sizes)
-    lines = after(jnp.concatenate(lines), inward[0])
-    across = [group_xor(after(v, lines), group_count, 2) for v in inward]
+    across = [[group_xor(v, group_count, 2) for v in pair] for pair in beside]
+    lines = after(jnp.concatenate(lines), beside[0][1], across[0][0], other[1], far_upper)
     lines = [lines] + plane_rest([lines], *sizes)
     down_pair = plane_pair(far_down, *sizes)
-    down = [[tensor_turn(v, tensor_count, step) for v in (mine[1], other[1])] for step in turns]
-    near = []
-    for step in range(len(turns)):
-        near += [(inward[step], down[step][0]), (across[step], down[step][1])]
-    lines += [group_xor(v, group_count, 1) for v in lines]
+    near = [pair for pairs in zip(beside, across) for pair in pairs]
+    lines += [
+        group_xor(lines[0], group_count, 1),
+        *[group_xor(v, group_count, 1) for v in lines[1:]],
+    ]
+    far_lower = tensor_xor(after(lower, far_upper), tensor_count, 2)
+    upper_pair = plane_pair(far_upper, *sizes)
     middle, second = attend(
         segment,
         projected,
@@ -532,16 +551,20 @@
         (0, KEY_VALUE_HEADS),
         (hidden_in, norm_gains[1], w_out),
     )
-    far = after(second, far_in, across[0], *down[0], down_pair[1])
+    far = after(second, far_lower, upper_pair[1], down_pair[1], across[0][1])
     far = tensor_xor(far, tensor_count, 1)
-    in_pair = plane_pair(far_in, *sizes)
-    late = [pair + plane_rest(pair, *sizes) for pair in (in_pair, down_pair)]
-    late = list(zip(*late))
+    late_down = down_pair + plane_rest(down_pair, *sizes)
+    late_upper = upper_pair + plane_rest(upper_pair, *sizes)
+    lower_pair = plane_pair(far_lower, *sizes)
+    late_lower = lower_pair + plane_rest(lower_pair, *sizes)
+    late = list(zip(late_upper, late_lower, late_down))
     beside = group_xor(second, group_count, 1)
-    far_beside = group_xor(far, group_count, 1)
     near = merge_pieces([mine, other] + near)
     late = merge_pieces(late)
     own_early = feed_forward(second, beside, near, [], jnp.float32)
+    far_beside = group_xor(
+        after(far, own_early[0], lower_pair[1], *late_down[2:], *late_upper[2:]), group_count, 1
+    )
     far_early = feed_forward(far, far_beside, near, [], jnp.float32, own_early)
     outgoing = select_pages(projected, page_dest[:, 0], group_count, [far])
     far_sum, far_beside_sum = feed_forward(
@@ -550,14 +573,15 @@
     far_sum = far_sum + group_xor(far_beside_sum, group_count, 1).astype(jnp.float32)
     far_sum = far_sum.astype(jnp.bfloat16)
     returned = tensor_xor(far_sum, tensor_count, 1)
-    received = [outgoing[0]] + [
-        group_xor(outgoing[bits], group_count, bits) for bits in range(1, group_count)
+    received = [outgoing[0], group_xor(after(outgoing[1], far_sum), group_count, 1)]
+    received += [
+        group_xor(outgoing[bits], group_count, bits) for bits in range(2, group_count)
     ]
     own_sum, beside_sum = feed_forward(
-        after(second, far_sum, *received[1:]), beside, late, [*own_early, middle], jnp.bfloat16
-    )
-    own_beside = group_xor(beside_sum, group_count, 1)
+        after(second, far_sum, received[1]), beside, late, [*own_early, middle], jnp.bfloat16
+    )
     received = place_pages(received)
+    own_beside = group_xor(after(beside_sum, received), group_count, 1)
     hidden_out = add_rows(own_sum, own_beside, after(returned, received))
     pages = received.reshape(group_count, CAP, -1, received.shape[2])
     return (hidden_out, pages[None, None])

time: 182 us -> 169 us (0.929)
  waiting for transfers between devices: 77.8 us -> 52.5 us
  starting transfers between devices: 32.9 us -> 40.3 us
  local copies, waits for them, and re-layouts: 6.2 us -> 10.7 us
  other arithmetic: 4.13 us -> 6.07 us
    ppermute x7 -> x8, waiting for transfers between devices: 29.4 us -> 4.96 us  [tensor_xor(): return lax.ppermute(value, 'tensor', pairs)]
    unnamed x36 -> x46, local copies, waits for them, and re-layouts: 2.37 us -> 6.77 us
    ppermute x8 -> x11, starting transfers between devices: 9.8 us -> 13.2 us  [swap_in_plane(): return lax.ppermute(value, ('group', 'tensor'), pairs)]
    ppermute x7 -> x8, starting transfers between devices: 12 us -> 15.3 us  [tensor_xor(): return lax.ppermute(value, 'tensor', pairs)]
    ppermute x13 -> x14, waiting for transfers between devices: 16.7 us -> 13.9 us  [group_xor(): lax.ppermute(value, 'group', [(g, g ^ bits) for g in range(group_count)])]
    ppermute x8 -> x11, waiting for transfers between devices: 31.7 us -> 33.6 us  [swap_in_plane(): return lax.ppermute(value, ('group', 'tensor'), pairs)]
    concatenate x1, other arithmetic: 0.05 us -> 1.93 us  [on_device(): jnp.concatenate(lines)]
    ppermute x13 -> x14, starting transfers between devices: 7.51 us -> 8.75 us  [group_xor(): lax.ppermute(value, 'group', [(g, g ^ bits) for g in range(group_count)])]
  transfers between devices with their start and end apart: 31 -> 35, of which waited for: 10 -> 13; matrix products, arithmetic and copies ran while one was open for 4% -> 5% of each run, Pallas kernels for 28% -> 29%
where the time goes in v4:
time: 169 us
  Pallas kernels  56.2 us (33%)
  waiting for transfers between devices  52.5 us (31%)
  starting transfers between devices  40.3 us (24%)
  local copies, waits for them, and re-layouts  10.7 us (6%)
  other arithmetic  6.07 us (4%)
  between operations  2.86 us (2%)
    ppermute x11, waiting for transfers between devices, swap_in_plane(): return lax.ppermute(value, ('group', 'tensor'), pairs)  33.6 us
    pallas_call x1, Pallas kernels, attend(): pl.pallas_call(functools.partial(kernel, len(pieces), heads), grid=(1,),...  18 us
    pallas_call x4, Pallas kernels, feed_forward(): pl.pallas_call(functools.partial(feed_forward_kernel, len(pieces[0]), len...  15.4 us
    ppermute x8, starting transfers between devices, tensor_xor(): return lax.ppermute(value, 'tensor', pairs)  15.3 us
    ppermute x14, waiting for transfers between devices, group_xor(): lax.ppermute(value, 'group', [(g, g ^ bits) for g in range(group_count)])  13.9 us
    ppermute x11, starting transfers between devices, swap_in_plane(): return lax.ppermute(value, ('group', 'tensor'), pairs)  13.2 us
    pallas_call x1, Pallas kernels, project(): pl.pallas_call(project_kernel, grid=(columns // width,), in_specs=[whole(...  8.91 us
    ppermute x14, starting transfers between devices, group_xor(): lax.ppermute(value, 'group', [(g, g ^ bits) for g in range(group_count)])  8.75 us
  transfers between devices with their start and end apart: 35, of which 13 were waited for; matrix products, arithmetic and copies ran while one was open for 5% of the time, Pallas kernels for 29%

profile of v4, /device:TPU:0, one launch (start us, length us, event | category | flops | bytes accessed | tf_op | source)
XLA Modules:
  0.0 168.7 jit_solution(16798631857658022048)
XLA Ops:
  0.6 1.0 slice_bitcast_fusion
  1.6 2.4 %collective-permute-start = (bf16[32,1536]{1,0:T(8,128)(2,1)S(1)}, bf16[32,1536]{1,0:T(8,128)(2,1)S(1)}, u32[]{:S(2)}, u32[]{:S(2)}) collective-permute-start(bf16[32,1536]{1,0:T(8,128)(2,1)S(1)} %get-tuple-element.70), channel_id=1, source_target_pairs={{0,24},{8,16},{16,8},{24,0},{1,25},{9,17},{17,9},{25,1},{2,26},{10... | collective-permute-start | bytes 294920 | tf_op jit(solution)/shard_map/ppermute | solution.py:45
  4.1 0.6 collective-permute-start.1
  4.8 0.6 pad_add_fusion.side
  5.4 3.6 %shard_map.113 = (bf16[1536,256]{1,0:T(8,128)(2,1)}, bf16[768,256]{1,0:T(8,128)(2,1)}, bf16[768,256]{1,0:T(8,128)(2,1)}, bf16[768,256]{1,0:T(8,128)(2,1)}) custom-call(s32[2]{0:T(128)} %pad_add_fusion.side, bf16[2,1536,512]{2,1,0:T(8,128)(2,1)} %w_in.3, bf16[512,1536]{1,0:T(8,128)(2,1)} %w_down.3), custom_call_target="tpu_custom_call" | custom-call | tf_op jit(solution)/shard_map/pallas_call | solution.py:140
  9.0 2.9 %collective-permute-start.6 = (bf16[768,256]{1,0:T(8,128)(2,1)}, bf16[768,256]{1,0:T(8,128)(2,1)S(1)}, u32[]{:S(2)}, u32[]{:S(2)}) collective-permute-start(bf16[768,256]{1,0:T(8,128)(2,1)} %get-tuple-element.38.rest_1_), channel_id=1, source_target_pairs={{0,4},{1,5},{2,6},{3,7},{4,0},{5,1},{6,2},{7,3},{8,12},{9,13},{10,... | collective-permute-start | bytes 1179656 | tf_op jit(solution)/shard_map/ppermute | solution.py:31
  11.9 1.5 collective-permute-start.9
  15.9 0.6 fusion.4
  16.6 0.9 fusion.1
  17.5 1.6 collective-permute-start.3
  19.5 2.5 %collective-permute-start.5 = (bf16[32,1536]{1,0:T(8,128)(2,1)S(1)}, bf16[32,1536]{1,0:T(8,128)(2,1)S(1)}, u32[]{:S(2)}, u32[]{:S(2)}) collective-permute-start(bf16[32,1536]{1,0:T(8,128)(2,1)S(1)} %fusion.1), channel_id=1, source_target_pairs={{0,6},{1,7},{2,4},{3,5},{4,2},{5,3},{6,0},{7,1},{8,14},{9,15},{10,... | collective-permute-start | bytes 294920 | tf_op jit(solution)/shard_map/ppermute | solution.py:31
  22.8 0.8 copy.20.cosine
  23.6 0.8 pad_maximum_fusion.2.sine
  24.3 8.9 %shard_map.114.projected = bf16[256,3072]{1,0:T(8,128)(2,1)} custom-call(bf16[256,1536]{1,0:T(8,128)(2,1)} %hidden.2, f32[1,1536]{1,0:T(1,128)} %get-tuple-element.72.gain, bf16[1536,3072]{1,0:T(8,128)(2,1)} %weight.1, f32[256,96]{1,0:T(8,128)} %copy.20.cosine, f32[256,96]{1,0:T(8,128)} %pad_maximum_fusion.2.sine), custom_call_target="tpu_custom_call" | custom-call | flops 2415919104 | bytes 9437184 | tf_op jit(solution)/shard_map/pallas_call | solution.py:241
  33.2 1.5 collective-permute-start.10
  34.7 2.1 %collective-permute-done.4 = bf16[32,1536]{1,0:T(8,128)(2,1)S(1)} collective-permute-done((bf16[32,1536]{1,0:T(8,128)(2,1)S(1)}, bf16[32,1536]{1,0:T(8,128)(2,1)S(1)}, u32[]{:S(2)}, u32[]{:S(2)}) %collective-permute-start.4) | collective-permute-done | bytes 98336 | tf_op jit(solution)/shard_map/ppermute | solution.py:31
  36.9 1.9 %collective-permute-start.7 = (bf16[128,1536]{1,0:T(8,128)(2,1)S(1)}, bf16[128,1536]{1,0:T(8,128)(2,1)}, u32[]{:S(2)}, u32[]{:S(2)}) collective-permute-start(bf16[128,1536]{1,0:T(8,128)(2,1)S(1)} %pad_maximum_fusion.1), channel_id=1, source_target_pairs={{0,16},{1,17},{2,18},{3,19},{4,20},{5,21},{6,22},{7,23},{8,9},{9,8... | collective-permute-start | bytes 1179656 | tf_op jit(solution)/shard_map/ppermute | solution.py:82
  38.7 1.5 collective-permute-start.8
  40.2 3.9 %collective-permute-start.11 = (bf16[768,256]{1,0:T(8,128)(2,1)}, bf16[768,256]{1,0:T(8,128)(2,1)S(1)}, u32[]{:S(2)}, u32[]{:S(2)}) collective-permute-start(bf16[768,256]{1,0:T(8,128)(2,1)} %get-tuple-element.43), channel_id=1, source_target_pairs={{0,4},{1,5},{2,6},{3,7},{4,0},{5,1},{6,2},{7,3},{8,12},{9,13},{10,... | collective-permute-start | bytes 1179656 | tf_op jit(solution)/shard_map/ppermute | solution.py:31
  44.1 0.7 pad_add_fusion.1.side
  44.8 3.2 %shard_map.115 = (bf16[1536,256]{1,0:T(8,128)(2,1)}, bf16[768,256]{1,0:T(8,128)(2,1)}) custom-call(s32[2]{0:T(128)} %pad_add_fusion.1.side, bf16[2,1536,512]{2,1,0:T(8,128)(2,1)} %w_in.3, bf16[512,1536]{1,0:T(8,128)(2,1)} %w_down.3), custom_call_target="tpu_custom_call" | custom-call | tf_op jit(solution)/shard_map/pallas_call | solution.py:140
  48.0 7.9 %collective-permute-done.7 = bf16[128,1536]{1,0:T(8,128)(2,1)} collective-permute-done((bf16[128,1536]{1,0:T(8,128)(2,1)S(1)}, bf16[128,1536]{1,0:T(8,128)(2,1)}, u32[]{:S(2)}, u32[]{:S(2)}) %collective-permute-start.7) | collective-permute-done | bytes 393248 | tf_op jit(solution)/shard_map/ppermute | solution.py:82
  55.8 1.9 %pad_maximum_fusion.rest_0_ = bf16[256,1536]{1,0:T(8,128)(2,1)} fusion(bf16[128,1536]{1,0:T(8,128)(2,1)} %collective-permute-done.7, bf16[128,1536]{1,0:T(8,128)(2,1)S(1)} %pad_maximum_fusion.1), kind=kLoop, calls=%fused_computation.1 | loop fusion | flops 1572864 | bytes 1572864 | tf_op jit(solution)/shard_map/concatenate | solution.py:537
  57.8 2.9 %collective-permute-done.11.rest_0_ = bf16[768,256]{1,0:T(8,128)(2,1)S(1)} collective-permute-done((bf16[768,256]{1,0:T(8,128)(2,1)}, bf16[768,256]{1,0:T(8,128)(2,1)S(1)}, u32[]{:S(2)}, u32[]{:S(2)}) %collective-permute-start.11) | collective-permute-done | bytes 393248 | tf_op jit(solution)/shard_map/ppermute | solution.py:31
  60.6 1.5 collective-permute-start.12
  62.1 10.7 %collective-permute-done.12.rest_1_ = bf16[256,1536]{1,0:T(8,128)(2,1)S(1)} collective-permute-done((bf16[256,1536]{1,0:T(8,128)(2,1)}, bf16[256,1536]{1,0:T(8,128)(2,1)S(1)}, u32[]{:S(2)}, u32[]{:S(2)}) %collective-permute-start.12) | collective-permute-done | bytes 786464 | tf_op jit(solution)/shard_map/ppermute | solution.py:82
  72.8 0.9 copy.21.row_ids
  73.8 1.4 collective-permute-start.18
  75.2 0.7 collective-permute-start.17
  75.8 1.4 collective-permute-start.16
  77.2 18.0 %shard_map.116 = (bf16[256,1536]{1,0:T(8,128)(2,1)}, bf16[256,1536]{1,0:T(8,128)(2,1)}) custom-call(s32[256,1]{1,0:T(8,128)} %copy.21.row_ids, s32[1,256]{1,0:T(1,128)} %column_ids.1, bf16[256,3072]{1,0:T(8,128)(2,1)} %shard_map.114.projected, bf16[256,1536]{1,0:T(8,128)(2,1)} %hidden.2, f32[1,1536]{1,0:T(1,128)} %get-tuple-element.71.gain, ...), custom_call_target="tpu_custom_call" | custom-call | tf_op jit(solution)/shard_map/pallas_call | solution.py:364
  95.3 1.6 collective-permute-start.22
  96.9 2.1 %collective-permute-start.19 = (bf16[256,1536]{1,0:T(8,128)(2,1)}, bf16[256,1536]{1,0:T(8,128)(2,1)S(1)}, u32[]{:S(2)}, u32[]{:S(2)}) collective-permute-start(bf16[256,1536]{1,0:T(8,128)(2,1)} %get-tuple-element.60.left), channel_id=1, source_target_pairs={{0,2},{1,3},{2,0},{3,1},{4,6},{5,7},{6,4},{7,5},{8,10},{9,11},{10,... | collective-permute-start | bytes 2359304 | tf_op jit(solution)/shard_map/ppermute | solution.py:31
  99.5 1.5 collective-permute-start.23
  101.0 2.1 %collective-permute-done.22.rest_8_ = bf16[768,256]{1,0:T(8,128)(2,1)S(1)} collective-permute-done((bf16[768,256]{1,0:T(8,128)(2,1)S(1)}, bf16[768,256]{1,0:T(8,128)(2,1)S(1)}, u32[]{:S(2)}, u32[]{:S(2)}) %collective-permute-start.22) | collective-permute-done | bytes 393248 | tf_op jit(solution)/shard_map/ppermute | solution.py:82
  103.1 0.7 collective-permute-start.21
  103.8 1.5 collective-permute-start.25
  105.3 1.1 copy-done.3
  106.4 1.0 copy-done.6
  107.4 1.0 copy-done.8
  108.4 3.8 %shard_map.117 = (f32[256,1536]{1,0:T(8,128)S(1)}, f32[256,1536]{1,0:T(8,128)S(1)}) custom-call(bf16[256,1536]{1,0:T(8,128)(2,1)S(1)} %copy-done.3, bf16[256,1536]{1,0:T(8,128)(2,1)S(1)} %collective-permute-done.20.right, bf16[1536,256]{1,0:T(8,128)(2,1)S(1)} %copy-done.1, bf16[768,256]{1,0:T(8,128)(2,1)S(1)} %copy-done.6, bf16[1536,256]{1,0:T(8,128)(2,1)S(1)} %copy-done.2, ...), custom_call_target="tpu_custom_call" | custom-call | tf_op jit(solution)/shard_map/pallas_call | solution.py:413
  112.3 3.4 %collective-permute-done.23.rest_11_ = bf16[768,256]{1,0:T(8,128)(2,1)S(1)} collective-permute-done((bf16[768,256]{1,0:T(8,128)(2,1)}, bf16[768,256]{1,0:T(8,128)(2,1)S(1)}, u32[]{:S(2)}, u32[]{:S(2)}) %collective-permute-start.23) | collective-permute-done | bytes 393248 | tf_op jit(solution)/shard_map/ppermute | solution.py:82
  115.8 4.2 %collective-permute-done.25.rest_9_ = bf16[768,256]{1,0:T(8,128)(2,1)S(1)} collective-permute-done((bf16[768,256]{1,0:T(8,128)(2,1)}, bf16[768,256]{1,0:T(8,128)(2,1)S(1)}, u32[]{:S(2)}, u32[]{:S(2)}) %collective-permute-start.25) | collective-permute-done | bytes 393248 | tf_op jit(solution)/shard_map/ppermute | solution.py:82
  120.0 1.5 collective-permute-start.27
  122.3 0.8 shard_map.119
  123.1 3.8 %shard_map.118 = (f32[256,1536]{1,0:T(8,128)S(1)}, f32[256,1536]{1,0:T(8,128)S(1)}) custom-call(bf16[256,1536]{1,0:T(8,128)(2,1)S(1)} %collective-permute-done.19.left.rest_0_, bf16[256,1536]{1,0:T(8,128)(2,1)S(1)} %collective-permute-done.26.right, bf16[1536,256]{1,0:T(8,128)(2,1)S(1)} %copy-done.1, bf16[768,256]{1,0:T(8,128)(2,1)S(1)} %copy-done.7, ...), custom_call_target="tpu_custom_call" | custom-call | tf_op jit(solution)/shard_map/pallas_call | solution.py:413
  127.0 1.0 collective-permute-done.27.rest_7_
  128.0 4.2 %collective-permute-done.28.rest_10_ = bf16[768,256]{1,0:T(8,128)(2,1)S(1)} collective-permute-done((bf16[768,256]{1,0:T(8,128)(2,1)S(1)}, bf16[768,256]{1,0:T(8,128)(2,1)S(1)}, u32[]{:S(2)}, u32[]{:S(2)}) %collective-permute-start.28) | collective-permute-done | bytes 393248 | tf_op jit(solution)/shard_map/ppermute | solution.py:82
  132.2 3.8 %shard_map.120 = (f32[256,1536]{1,0:T(8,128)S(1)}, bf16[256,1536]{1,0:T(8,128)(2,1)S(1)}) custom-call(bf16[256,1536]{1,0:T(8,128)(2,1)S(1)} %collective-permute-done.19.left.rest_0_, bf16[256,1536]{1,0:T(8,128)(2,1)S(1)} %collective-permute-done.26.right, bf16[768,256]{1,0:T(8,128)(2,1)S(1)} %collective-permute-done.11.rest_0_, ...), custom_call_target="tpu_custom_call" | custom-call | tf_op jit(solution)/shard_map/pallas_call | solution.py:413
  136.1 2.3 %collective-permute-done.29 = bf16[256,1536]{1,0:T(8,128)(2,1)S(1)} collective-permute-done((bf16[256,1536]{1,0:T(8,128)(2,1)S(1)}, bf16[256,1536]{1,0:T(8,128)(2,1)S(1)}, u32[]{:S(2)}, u32[]{:S(2)}) %collective-permute-start.29) | collective-permute-done | bytes 786464 | tf_op jit(solution)/shard_map/ppermute | solution.py:45
  138.8 0.7 collective-permute-start.31
  139.5 1.1 collective-permute-start.32
  140.5 2.0 %collective-permute-start.34 = (bf16[256,1536]{1,0:T(8,128)(2,1)S(1)}, bf16[256,1536]{1,0:T(8,128)(2,1)S(1)}, u32[]{:S(2)}, u32[]{:S(2)}) collective-permute-start(bf16[256,1536]{1,0:T(8,128)(2,1)S(1)} %add_convert_fusion), channel_id=1, source_target_pairs={{0,2},{1,3},{2,0},{3,1},{4,6},{5,7},{6,4},{7,5},{8,10},{9,11},{10,... | collective-permute-start | bytes 2359304 | tf_op jit(solution)/shard_map/ppermute | solution.py:31
  142.5 0.8 copy-done.16
  143.3 3.8 %shard_map.121 = (f32[256,1536]{1,0:T(8,128)S(1)}, bf16[256,1536]{1,0:T(8,128)(2,1)S(1)}) custom-call(bf16[256,1536]{1,0:T(8,128)(2,1)S(1)} %copy-done.4, bf16[256,1536]{1,0:T(8,128)(2,1)S(1)} %collective-permute-done.20.right, bf16[768,256]{1,0:T(8,128)(2,1)S(1)} %collective-permute-done.11.rest_0_, bf16[768,256]{1,0:T(8,128)(2,1)} %collective-permute-done.15.rest_1_, ...), custom_call_target="tpu_custom_call" | custom-call | tf_op jit(solution)/shard_map/pallas_call | solution.py:413
  147.1 1.2 copy-done.11
  148.3 2.4 %collective-permute-done.31.rest_2_ = bf16[128,1536]{1,0:T(8,128)(2,1)S(1)} collective-permute-done((bf16[128,1536]{1,0:T(8,128)(2,1)S(1)}, bf16[128,1536]{1,0:T(8,128)(2,1)S(1)}, u32[]{:S(2)}, u32[]{:S(2)}) %collective-permute-start.31) | collective-permute-done | bytes 393248 | tf_op jit(solution)/shard_map/ppermute | solution.py:45
  150.7 7.3 %collective-permute-done.32.rest_3_ = bf16[128,1536]{1,0:T(8,128)(2,1)S(1)} collective-permute-done((bf16[128,1536]{1,0:T(8,128)(2,1)S(1)}, bf16[128,1536]{1,0:T(8,128)(2,1)S(1)}, u32[]{:S(2)}, u32[]{:S(2)}) %collective-permute-start.32) | collective-permute-done | bytes 393248 | tf_op jit(solution)/shard_map/ppermute | solution.py:45
  158.1 0.8 copy-done.18
  158.8 2.6 %shard_map.122 = bf16[4,128,1536]{2,1,0:T(8,128)(2,1)} custom-call(s32[1]{0:T(128)} %bitcast.12.group, bf16[128,1536]{1,0:T(8,128)(2,1)} %copy-done.10, bf16[128,1536]{1,0:T(8,128)(2,1)} %copy-done.16, bf16[128,1536]{1,0:T(8,128)(2,1)} %copy-done.17, bf16[128,1536]{1,0:T(8,128)(2,1)} %copy-done.18), custom_call_target="tpu_custom_call" | custom-call | tf_op jit(solution)/shard_map/pallas_call | solution.py:491
  161.4 0.7 collective-permute-start.33
  162.1 1.9 %collective-permute-done.33.refs_1_ = bf16[256,1536]{1,0:T(8,128)(2,1)S(1)} collective-permute-done((bf16[256,1536]{1,0:T(8,128)(2,1)S(1)}, bf16[256,1536]{1,0:T(8,128)(2,1)S(1)}, u32[]{:S(2)}, u32[]{:S(2)}) %collective-permute-start.33) | collective-permute-done | bytes 786464 | tf_op jit(solution)/shard_map/ppermute | solution.py:45
  164.0 0.9 copy-done.14
  164.9 3.8 %shard_map.123 = bf16[256,1536]{1,0:T(8,128)(2,1)} custom-call(f32[256,1536]{1,0:T(8,128)} %copy-done.11, bf16[256,1536]{1,0:T(8,128)(2,1)} %copy-done.14, bf16[256,1536]{1,0:T(8,128)(2,1)} %copy-done.13), custom_call_target="tpu_custom_call" | custom-call | tf_op jit(solution)/shard_map/pallas_call | solution.py:435
  (84 shorter events, 3.7 us)
Async XLA Ops:
  1.6 14.9 %collective-permute-start = (bf16[32,1536]{1,0:T(8,128)(2,1)S(1)}, bf16[32,1536]{1,0:T(8,128)(2,1)S(1)}, u32[]{:S(2)}, u32[]{:S(2)}) collective-permute-start(bf16[32,1536]{1,0:T(8,128)(2,1)S(1)} %get-tuple-element.70), channel_id=1, source_target_pairs={{0,24},{8,16},{16,8},{24,0},{1,25},{9,17},{17,9},{25,1},{2,26},{10... | collective-permute-start | bytes 294920 | tf_op jit(solution)/shard_map/ppermute | solution.py:45
  4.1 12.5 %collective-permute-start.1 = (bf16[32,1536]{1,0:T(8,128)(2,1)S(1)}, bf16[32,1536]{1,0:T(8,128)(2,1)S(1)}, u32[]{:S(2)}, u32[]{:S(2)}) collective-permute-start(bf16[32,1536]{1,0:T(8,128)(2,1)S(1)} %get-tuple-element.69), channel_id=1, source_target_pairs={{0,16},{8,24},{16,0},{24,8},{1,17},{9,25},{17,1},{25,9},{2,18},{10... | collective-permute-start | bytes 294920 | tf_op jit(solution)/shard_map/ppermute | solution.py:45
  4.7 11.9 %collective-permute-start.2 = (bf16[32,1536]{1,0:T(8,128)(2,1)S(1)}, bf16[32,1536]{1,0:T(8,128)(2,1)S(1)}, u32[]{:S(2)}, u32[]{:S(2)}) collective-permute-start(bf16[32,1536]{1,0:T(8,128)(2,1)S(1)} %get-tuple-element.68), channel_id=1, source_target_pairs={{0,8},{8,0},{16,24},{24,16},{1,9},{9,1},{17,25},{25,17},{2,10},{10... | collective-permute-start | bytes 294920 | tf_op jit(solution)/shard_map/ppermute | solution.py:45
  5.4 8.1 %copy-start.22 = (s32[8]{0:T(128)S(1)}, s32[8]{0:T(128)}, u32[]{:S(2)}) copy-start(s32[8]{0:T(128)} %param.18) | copy-start | bytes 100
  5.4 10.6 %copy-start.20 = (f32[2,1536]{1,0:T(2,128)S(1)}, f32[2,1536]{1,0:T(2,128)}, u32[]{:S(2)}) copy-start(f32[2,1536]{1,0:T(2,128)} %param.12) | copy-start | bytes 36868
  5.4 16.6 %copy-start.19 = (s32[1,256]{1,0:T(1,128)S(1)}, s32[1,256]{1,0:T(1,128)}, u32[]{:S(2)}) copy-start(s32[1,256]{1,0:T(1,128)} %column_ids.1) | copy-start | bytes 3076
  9.0 27.9 %collective-permute-start.6 = (bf16[768,256]{1,0:T(8,128)(2,1)}, bf16[768,256]{1,0:T(8,128)(2,1)S(1)}, u32[]{:S(2)}, u32[]{:S(2)}) collective-permute-start(bf16[768,256]{1,0:T(8,128)(2,1)} %get-tuple-element.38.rest_1_), channel_id=1, source_target_pairs={{0,4},{1,5},{2,6},{3,7},{4,0},{5,1},{6,2},{7,3},{8,12},{9,13},{10,... | collective-permute-start | bytes 1179656 | tf_op jit(solution)/shard_map/ppermute | solution.py:31
  11.9 21.4 %collective-permute-start.9 = (bf16[1536,256]{1,0:T(8,128)(2,1)}, bf16[1536,256]{1,0:T(8,128)(2,1)S(1)}, u32[]{:S(2)}, u32[]{:S(2)}) collective-permute-start(bf16[1536,256]{1,0:T(8,128)(2,1)} %get-tuple-element.35.rest_0_), channel_id=1, source_target_pairs={{0,1},{1,0},{2,3},{3,2},{4,5},{5,4},{6,7},{7,6},{8,9},{9,8},{10,11... | collective-permute-start | bytes 2359304 | tf_op jit(solution)/shard_map/ppermute | solution.py:41
  17.5 17.2 %collective-permute-start.3 = (bf16[32,1536]{1,0:T(8,128)(2,1)S(1)}, bf16[32,1536]{1,0:T(8,128)(2,1)S(1)}, u32[]{:S(2)}, u32[]{:S(2)}) collective-permute-start(bf16[32,1536]{1,0:T(8,128)(2,1)S(1)} %fusion.1), channel_id=1, source_target_pairs={{0,2},{1,3},{2,0},{3,1},{4,6},{5,7},{6,4},{7,5},{8,10},{9,11},{10,... | collective-permute-start | bytes 294920 | tf_op jit(solution)/shard_map/ppermute | solution.py:31
  19.2 17.6 %collective-permute-start.4 = (bf16[32,1536]{1,0:T(8,128)(2,1)S(1)}, bf16[32,1536]{1,0:T(8,128)(2,1)S(1)}, u32[]{:S(2)}, u32[]{:S(2)}) collective-permute-start(bf16[32,1536]{1,0:T(8,128)(2,1)S(1)} %fusion.1), channel_id=1, source_target_pairs={{0,4},{1,5},{2,6},{3,7},{4,0},{5,1},{6,2},{7,3},{8,12},{9,13},{10,... | collective-permute-start | bytes 294920 | tf_op jit(solution)/shard_map/ppermute | solution.py:31
  19.5 17.3 %collective-permute-start.5 = (bf16[32,1536]{1,0:T(8,128)(2,1)S(1)}, bf16[32,1536]{1,0:T(8,128)(2,1)S(1)}, u32[]{:S(2)}, u32[]{:S(2)}) collective-permute-start(bf16[32,1536]{1,0:T(8,128)(2,1)S(1)} %fusion.1), channel_id=1, source_target_pairs={{0,6},{1,7},{2,4},{3,5},{4,2},{5,3},{6,0},{7,1},{8,14},{9,15},{10,... | collective-permute-start | bytes 294920 | tf_op jit(solution)/shard_map/ppermute | solution.py:31
  24.3 14.4 %copy-start.5 = (bf16[768,256]{1,0:T(8,128)(2,1)S(1)}, bf16[768,256]{1,0:T(8,128)(2,1)}, u32[]{:S(2)}) copy-start(bf16[768,256]{1,0:T(8,128)(2,1)} %get-tuple-element.38.rest_1_) | copy-start | bytes 1179652
  33.2 27.4 %collective-permute-start.10 = (bf16[1536,256]{1,0:T(8,128)(2,1)S(1)}, bf16[1536,256]{1,0:T(8,128)(2,1)S(1)}, u32[]{:S(2)}, u32[]{:S(2)}) collective-permute-start(bf16[1536,256]{1,0:T(8,128)(2,1)S(1)} %collective-permute-done.9.rest_4_), channel_id=1, source_target_pairs={{0,16},{8,24},{16,0},{24,8},{1,17},{9,25},{17,1},{25,9},{2,18},{10... | collective-permute-start | bytes 2359304 | tf_op jit(solution)/shard_map/ppermute | solution.py:45
  36.9 19.0 %collective-permute-start.7 = (bf16[128,1536]{1,0:T(8,128)(2,1)S(1)}, bf16[128,1536]{1,0:T(8,128)(2,1)}, u32[]{:S(2)}, u32[]{:S(2)}) collective-permute-start(bf16[128,1536]{1,0:T(8,128)(2,1)S(1)} %pad_maximum_fusion.1), channel_id=1, source_target_pairs={{0,16},{1,17},{2,18},{3,19},{4,20},{5,21},{6,22},{7,23},{8,9},{9,8... | collective-permute-start | bytes 1179656 | tf_op jit(solution)/shard_map/ppermute | solution.py:82
  38.7 19.0 %collective-permute-start.8 = (bf16[768,256]{1,0:T(8,128)(2,1)S(1)}, bf16[768,256]{1,0:T(8,128)(2,1)}, u32[]{:S(2)}, u32[]{:S(2)}) collective-permute-start(bf16[768,256]{1,0:T(8,128)(2,1)S(1)} %copy-done.5), channel_id=1, source_target_pairs={{0,1},{1,0},{2,3},{3,2},{4,5},{5,4},{6,7},{7,6},{8,9},{9,8},{10,11... | collective-permute-start | bytes 1179656 | tf_op jit(solution)/shard_map/ppermute | solution.py:41
  40.2 20.4 %collective-permute-start.11 = (bf16[768,256]{1,0:T(8,128)(2,1)}, bf16[768,256]{1,0:T(8,128)(2,1)S(1)}, u32[]{:S(2)}, u32[]{:S(2)}) collective-permute-start(bf16[768,256]{1,0:T(8,128)(2,1)} %get-tuple-element.43), channel_id=1, source_target_pairs={{0,4},{1,5},{2,6},{3,7},{4,0},{5,1},{6,2},{7,3},{8,12},{9,13},{10,... | collective-permute-start | bytes 1179656 | tf_op jit(solution)/shard_map/ppermute | solution.py:31
  60.6 12.2 %collective-permute-start.12 = (bf16[256,1536]{1,0:T(8,128)(2,1)}, bf16[256,1536]{1,0:T(8,128)(2,1)S(1)}, u32[]{:S(2)}, u32[]{:S(2)}) collective-permute-start(bf16[256,1536]{1,0:T(8,128)(2,1)} %pad_maximum_fusion.rest_0_), channel_id=1, source_target_pairs={{0,1},{1,0},{2,3},{3,2},{4,5},{5,4},{6,7},{7,6},{8,24},{9,25},{10,... | collective-permute-start | bytes 2359304 | tf_op jit(solution)/shard_map/ppermute | solution.py:82
  62.1 13.7 %collective-permute-start.13 = (bf16[256,1536]{1,0:T(8,128)(2,1)}, bf16[256,1536]{1,0:T(8,128)(2,1)}, u32[]{:S(2)}, u32[]{:S(2)}) collective-permute-start(bf16[256,1536]{1,0:T(8,128)(2,1)} %pad_maximum_fusion.rest_0_), channel_id=1, source_target_pairs={{0,8},{8,0},{16,24},{24,16},{1,9},{9,1},{17,25},{25,17},{2,10},{10... | collective-permute-start | bytes 2359304 | tf_op jit(solution)/shard_map/ppermute | solution.py:45
  72.8 4.4 %copy-start.15 = (bf16[256,1536]{1,0:T(8,128)(2,1)}, bf16[256,1536]{1,0:T(8,128)(2,1)S(1)}, u32[]{:S(2)}) copy-start(bf16[256,1536]{1,0:T(8,128)(2,1)S(1)} %collective-permute-done.12.rest_1_) | copy-start | bytes 2359300
  72.8 4.4 %collective-permute-start.14 = (bf16[256,1536]{1,0:T(8,128)(2,1)S(1)}, bf16[256,1536]{1,0:T(8,128)(2,1)}, u32[]{:S(2)}, u32[]{:S(2)}) collective-permute-start(bf16[256,1536]{1,0:T(8,128)(2,1)S(1)} %collective-permute-done.12.rest_1_), channel_id=1, source_target_pairs={{0,8},{8,0},{16,24},{24,16},{1,9},{9,1},{17,25},{25,17},{2,10},{10... | collective-permute-start | bytes 2359304 | tf_op jit(solution)/shard_map/ppermute | solution.py:45
  73.8 21.5 %collective-permute-start.18 = (bf16[768,256]{1,0:T(8,128)(2,1)}, bf16[768,256]{1,0:T(8,128)(2,1)}, u32[]{:S(2)}, u32[]{:S(2)}) collective-permute-start(bf16[768,256]{1,0:T(8,128)(2,1)} %collective-permute-done.8.rest_5_), channel_id=1, source_target_pairs={{0,16},{8,24},{16,0},{24,8},{1,17},{9,25},{17,1},{25,9},{2,18},{10... | collective-permute-start | bytes 1179656 | tf_op jit(solution)/shard_map/ppermute | solution.py:45
  75.2 21.7 %collective-permute-start.17 = (bf16[768,256]{1,0:T(8,128)(2,1)S(1)}, bf16[768,256]{1,0:T(8,128)(2,1)}, u32[]{:S(2)}, u32[]{:S(2)}) collective-permute-start(bf16[768,256]{1,0:T(8,128)(2,1)S(1)} %collective-permute-done.6.rest_2_), channel_id=1, source_target_pairs={{0,16},{1,17},{2,18},{3,19},{4,20},{5,21},{6,22},{7,23},{8,9},{9,8... | collective-permute-start | bytes 1179656 | tf_op jit(solution)/shard_map/ppermute | solution.py:82
  75.8 21.1 %collective-permute-start.15 = (bf16[768,256]{1,0:T(8,128)(2,1)}, bf16[768,256]{1,0:T(8,128)(2,1)}, u32[]{:S(2)}, u32[]{:S(2)}) collective-permute-start(bf16[768,256]{1,0:T(8,128)(2,1)} %get-tuple-element.47), channel_id=1, source_target_pairs={{0,4},{1,5},{2,6},{3,7},{4,0},{5,1},{6,2},{7,3},{8,12},{9,13},{10,... | collective-permute-start | bytes 1179656 | tf_op jit(solution)/shard_map/ppermute | solution.py:31
  75.8 21.1 %collective-permute-start.16 = (bf16[768,256]{1,0:T(8,128)(2,1)S(1)}, bf16[768,256]{1,0:T(8,128)(2,1)}, u32[]{:S(2)}, u32[]{:S(2)}) collective-permute-start(bf16[768,256]{1,0:T(8,128)(2,1)S(1)} %collective-permute-done.11.rest_0_), channel_id=1, source_target_pairs={{0,16},{1,17},{2,18},{3,19},{4,20},{5,21},{6,22},{7,23},{8,9},{9,8... | collective-permute-start | bytes 1179656 | tf_op jit(solution)/shard_map/ppermute | solution.py:82
  77.2 28.1 %copy-start.1 = (bf16[1536,256]{1,0:T(8,128)(2,1)S(1)}, bf16[1536,256]{1,0:T(8,128)(2,1)}, u32[]{:S(2)}) copy-start(bf16[1536,256]{1,0:T(8,128)(2,1)} %get-tuple-element.35.rest_0_) | copy-start | bytes 2359300
  77.2 28.1 %copy-start.2 = (bf16[1536,256]{1,0:T(8,128)(2,1)S(1)}, bf16[1536,256]{1,0:T(8,128)(2,1)}, u32[]{:S(2)}) copy-start(bf16[1536,256]{1,0:T(8,128)(2,1)} %get-tuple-element.49.rest_2_) | copy-start | bytes 2359300
  95.2 8.6 %collective-permute-start.20 = (bf16[256,1536]{1,0:T(8,128)(2,1)}, bf16[256,1536]{1,0:T(8,128)(2,1)S(1)}, u32[]{:S(2)}, u32[]{:S(2)}) collective-permute-start(bf16[256,1536]{1,0:T(8,128)(2,1)} %get-tuple-element.60.left), channel_id=1, source_target_pairs={{0,8},{8,0},{16,24},{24,16},{1,9},{9,1},{17,25},{25,17},{2,10},{10... | collective-permute-start | bytes 2359304 | tf_op jit(solution)/shard_map/ppermute | solution.py:45
  95.3 7.8 %collective-permute-start.22 = (bf16[768,256]{1,0:T(8,128)(2,1)S(1)}, bf16[768,256]{1,0:T(8,128)(2,1)S(1)}, u32[]{:S(2)}, u32[]{:S(2)}) collective-permute-start(bf16[768,256]{1,0:T(8,128)(2,1)S(1)} %collective-permute-done.6.rest_2_), channel_id=1, source_target_pairs={{0,1},{1,0},{2,3},{3,2},{4,5},{5,4},{6,7},{7,6},{8,24},{9,25},{10,... | collective-permute-start | bytes 1179656 | tf_op jit(solution)/shard_map/ppermute | solution.py:82
  96.9 23.1 %collective-permute-start.19 = (bf16[256,1536]{1,0:T(8,128)(2,1)}, bf16[256,1536]{1,0:T(8,128)(2,1)S(1)}, u32[]{:S(2)}, u32[]{:S(2)}) collective-permute-start(bf16[256,1536]{1,0:T(8,128)(2,1)} %get-tuple-element.60.left), channel_id=1, source_target_pairs={{0,2},{1,3},{2,0},{3,1},{4,6},{5,7},{6,4},{7,5},{8,10},{9,11},{10,... | collective-permute-start | bytes 2359304 | tf_op jit(solution)/shard_map/ppermute | solution.py:31
  98.9 13.4 %collective-permute-start.24 = (bf16[768,256]{1,0:T(8,128)(2,1)S(1)}, bf16[768,256]{1,0:T(8,128)(2,1)S(1)}, u32[]{:S(2)}, u32[]{:S(2)}) collective-permute-start(bf16[768,256]{1,0:T(8,128)(2,1)S(1)} %collective-permute-done.11.rest_0_), channel_id=1, source_target_pairs={{0,1},{1,0},{2,3},{3,2},{4,5},{5,4},{6,7},{7,6},{8,24},{9,25},{10,... | collective-permute-start | bytes 1179656 | tf_op jit(solution)/shard_map/ppermute | solution.py:82
  99.5 16.3 %collective-permute-start.23 = (bf16[768,256]{1,0:T(8,128)(2,1)}, bf16[768,256]{1,0:T(8,128)(2,1)S(1)}, u32[]{:S(2)}, u32[]{:S(2)}) collective-permute-start(bf16[768,256]{1,0:T(8,128)(2,1)} %collective-permute-done.17.rest_5_), channel_id=1, source_target_pairs={{0,1},{1,0},{2,3},{3,2},{4,5},{5,4},{6,7},{7,6},{8,24},{9,25},{10,... | collective-permute-start | bytes 1179656 | tf_op jit(solution)/shard_map/ppermute | solution.py:82
  103.1 12.6 %collective-permute-start.21 = (bf16[768,256]{1,0:T(8,128)(2,1)}, bf16[768,256]{1,0:T(8,128)(2,1)S(1)}, u32[]{:S(2)}, u32[]{:S(2)}) collective-permute-start(bf16[768,256]{1,0:T(8,128)(2,1)} %collective-permute-done.15.rest_1_), channel_id=1, source_target_pairs={{0,16},{1,17},{2,18},{3,19},{4,20},{5,21},{6,22},{7,23},{8,9},{9,8... | collective-permute-start | bytes 1179656 | tf_op jit(solution)/shard_map/ppermute | solution.py:82
  103.8 16.2 %collective-permute-start.25 = (bf16[768,256]{1,0:T(8,128)(2,1)}, bf16[768,256]{1,0:T(8,128)(2,1)S(1)}, u32[]{:S(2)}, u32[]{:S(2)}) collective-permute-start(bf16[768,256]{1,0:T(8,128)(2,1)} %collective-permute-done.16.rest_3_), channel_id=1, source_target_pairs={{0,1},{1,0},{2,3},{3,2},{4,5},{5,4},{6,7},{7,6},{8,24},{9,25},{10,... | collective-permute-start | bytes 1179656 | tf_op jit(solution)/shard_map/ppermute | solution.py:82
  105.3 1.1 copy-start.3
  106.4 1.0 copy-start.6
  107.4 1.0 copy-start.8
  108.4 13.6 %copy-start.21 = (s32[16,1]{0,1:T(1,128)S(1)}, s32[16,1]{0,1:T(1,128)}, u32[]{:S(2)}) copy-start(s32[16,1]{0,1:T(1,128)} %param.19) | copy-start | bytes 196
  108.4 13.9 %copy-start = (bf16[256,3072]{1,0:T(8,128)(2,1)S(1)}, bf16[256,3072]{1,0:T(8,128)(2,1)}, u32[]{:S(2)}) copy-start(bf16[256,3072]{1,0:T(8,128)(2,1)} %shard_map.114.projected) | copy-start | bytes 4718596
  112.3 10.8 %copy-start.7 = (bf16[768,256]{1,0:T(8,128)(2,1)S(1)}, bf16[768,256]{1,0:T(8,128)(2,1)}, u32[]{:S(2)}) copy-start(bf16[768,256]{1,0:T(8,128)(2,1)} %get-tuple-element.38.rest_1_) | copy-start | bytes 1179652
  112.3 10.8 %copy-start.9 = (bf16[768,256]{1,0:T(8,128)(2,1)S(1)}, bf16[768,256]{1,0:T(8,128)(2,1)}, u32[]{:S(2)}) copy-start(bf16[768,256]{1,0:T(8,128)(2,1)} %get-tuple-element.41.rest_3_) | copy-start | bytes 1179652
  120.0 3.1 %collective-permute-start.26 = (bf16[256,1536]{1,0:T(8,128)(2,1)S(1)}, bf16[256,1536]{1,0:T(8,128)(2,1)S(1)}, u32[]{:S(2)}, u32[]{:S(2)}) collective-permute-start(bf16[256,1536]{1,0:T(8,128)(2,1)S(1)} %collective-permute-done.19.left.rest_0_), channel_id=1, source_target_pairs={{0,8},{8,0},{16,24},{24,16},{1,9},{9,1},{17,25},{25,17},{2,10},{10... | collective-permute-start | bytes 2359304 | tf_op jit(solution)/shard_map/ppermute | solution.py:45
  120.0 8.0 %collective-permute-start.27 = (bf16[768,256]{1,0:T(8,128)(2,1)}, bf16[768,256]{1,0:T(8,128)(2,1)S(1)}, u32[]{:S(2)}, u32[]{:S(2)}) collective-permute-start(bf16[768,256]{1,0:T(8,128)(2,1)} %collective-permute-done.15.rest_1_), channel_id=1, source_target_pairs={{0,1},{1,0},{2,3},{3,2},{4,5},{5,4},{6,7},{7,6},{8,24},{9,25},{10,... | collective-permute-start | bytes 1179656 | tf_op jit(solution)/shard_map/ppermute | solution.py:82
  121.5 10.7 %collective-permute-start.28 = (bf16[768,256]{1,0:T(8,128)(2,1)S(1)}, bf16[768,256]{1,0:T(8,128)(2,1)S(1)}, u32[]{:S(2)}, u32[]{:S(2)}) collective-permute-start(bf16[768,256]{1,0:T(8,128)(2,1)S(1)} %collective-permute-done.21.rest_4_), channel_id=1, source_target_pairs={{0,1},{1,0},{2,3},{3,2},{4,5},{5,4},{6,7},{7,6},{8,24},{9,25},{10,... | collective-permute-start | bytes 1179656 | tf_op jit(solution)/shard_map/ppermute | solution.py:82
  123.1 9.1 %copy-start.10 = (bf16[128,1536]{1,0:T(8,128)(2,1)}, bf16[128,1536]{1,0:T(8,128)(2,1)S(1)}, u32[]{:S(2)}) copy-start(bf16[128,1536]{1,0:T(8,128)(2,1)S(1)} %get-tuple-element.55.rest_14_.rest_0_) | copy-start | bytes 1179652
  136.0 2.4 %collective-permute-start.29 = (bf16[256,1536]{1,0:T(8,128)(2,1)S(1)}, bf16[256,1536]{1,0:T(8,128)(2,1)S(1)}, u32[]{:S(2)}, u32[]{:S(2)}) collective-permute-start(bf16[256,1536]{1,0:T(8,128)(2,1)S(1)} %get-tuple-element.57), channel_id=1, source_target_pairs={{0,8},{8,0},{16,24},{24,16},{1,9},{9,1},{17,25},{25,17},{2,10},{10... | collective-permute-start | bytes 2359304 | tf_op jit(solution)/shard_map/ppermute | solution.py:45
  138.4 4.9 %copy-start.4 = (bf16[256,1536]{1,0:T(8,128)(2,1)S(1)}, bf16[256,1536]{1,0:T(8,128)(2,1)}, u32[]{:S(2)}) copy-start(bf16[256,1536]{1,0:T(8,128)(2,1)} %get-tuple-element.60.left) | copy-start | bytes 2359300
  138.4 4.9 %copy-start.12 = (bf16[256,1536]{1,0:T(8,128)(2,1)S(1)}, bf16[256,1536]{1,0:T(8,128)(2,1)}, u32[]{:S(2)}) copy-start(bf16[256,1536]{1,0:T(8,128)(2,1)} %get-tuple-element.61.rest_14_) | copy-start | bytes 2359300
  138.6 3.9 %collective-permute-start.30 = (bf16[128,1536]{1,0:T(8,128)(2,1)S(1)}, bf16[128,1536]{1,0:T(8,128)(2,1)S(1)}, u32[]{:S(2)}, u32[]{:S(2)}) collective-permute-start(bf16[128,1536]{1,0:T(8,128)(2,1)S(1)} %get-tuple-element.59), channel_id=1, source_target_pairs={{0,8},{8,0},{16,24},{24,16},{1,9},{9,1},{17,25},{25,17},{2,10},{10... | collective-permute-start | bytes 1179656 | tf_op jit(solution)/shard_map/ppermute | solution.py:45
  138.8 11.9 %collective-permute-start.31 = (bf16[128,1536]{1,0:T(8,128)(2,1)S(1)}, bf16[128,1536]{1,0:T(8,128)(2,1)S(1)}, u32[]{:S(2)}, u32[]{:S(2)}) collective-permute-start(bf16[128,1536]{1,0:T(8,128)(2,1)S(1)} %get-tuple-element.64), channel_id=1, source_target_pairs={{0,16},{8,24},{16,0},{24,8},{1,17},{9,25},{17,1},{25,9},{2,18},{10... | collective-permute-start | bytes 1179656 | tf_op jit(solution)/shard_map/ppermute | solution.py:45
  139.5 18.6 %collective-permute-start.32 = (bf16[128,1536]{1,0:T(8,128)(2,1)S(1)}, bf16[128,1536]{1,0:T(8,128)(2,1)S(1)}, u32[]{:S(2)}, u32[]{:S(2)}) collective-permute-start(bf16[128,1536]{1,0:T(8,128)(2,1)S(1)} %get-tuple-element.65), channel_id=1, source_target_pairs={{0,24},{8,16},{16,8},{24,0},{1,25},{9,17},{17,9},{25,1},{2,26},{10... | collective-permute-start | bytes 1179656 | tf_op jit(solution)/shard_map/ppermute | solution.py:45
  140.5 21.6 %collective-permute-start.34 = (bf16[256,1536]{1,0:T(8,128)(2,1)S(1)}, bf16[256,1536]{1,0:T(8,128)(2,1)S(1)}, u32[]{:S(2)}, u32[]{:S(2)}) collective-permute-start(bf16[256,1536]{1,0:T(8,128)(2,1)S(1)} %add_convert_fusion), channel_id=1, source_target_pairs={{0,2},{1,3},{2,0},{3,1},{4,6},{5,7},{6,4},{7,5},{8,10},{9,11},{10,... | collective-permute-start | bytes 2359304 | tf_op jit(solution)/shard_map/ppermute | solution.py:31
  142.5 0.8 copy-start.16
  147.1 1.2 copy-start.11
  150.7 7.3 %copy-start.17 = (bf16[128,1536]{1,0:T(8,128)(2,1)}, bf16[128,1536]{1,0:T(8,128)(2,1)S(1)}, u32[]{:S(2)}) copy-start(bf16[128,1536]{1,0:T(8,128)(2,1)S(1)} %collective-permute-done.31.rest_2_) | copy-start | bytes 1179652
  158.0 0.8 copy-start.18
  161.4 2.6 %collective-permute-start.33 = (bf16[256,1536]{1,0:T(8,128)(2,1)S(1)}, bf16[256,1536]{1,0:T(8,128)(2,1)S(1)}, u32[]{:S(2)}, u32[]{:S(2)}) collective-permute-start(bf16[256,1536]{1,0:T(8,128)(2,1)S(1)} %get-tuple-element.66), channel_id=1, source_target_pairs={{0,8},{8,0},{16,24},{24,16},{1,9},{9,1},{17,25},{25,17},{2,10},{10... | collective-permute-start | bytes 2359304 | tf_op jit(solution)/shard_map/ppermute | solution.py:45
  162.1 1.9 %copy-start.13 = (bf16[256,1536]{1,0:T(8,128)(2,1)}, bf16[256,1536]{1,0:T(8,128)(2,1)S(1)}, u32[]{:S(2)}) copy-start(bf16[256,1536]{1,0:T(8,128)(2,1)S(1)} %collective-permute-done.34.refs_2_) | copy-start | bytes 2359300
  164.0 0.9 copy-start.14

commit v5 on v4

--- a/solution.py
+++ b/solution.py
@@ -156,13 +156,32 @@
     )(jnp.stack([side, core]).astype(jnp.int32), w_in, w_down)
 
 
+def halves_of(arrays):
+    return [(array, half) for array in arrays for half in range(2)]
+
+
+def block_of(chunk):
+    if not isinstance(chunk, tuple):
+        return whole(chunk)
+    array, half = chunk
+    return pl.BlockSpec((array.shape[0] // 2, array.shape[1]), lambda *_: (half, 0))
+
+
+def rows_of(chunk):
+    if not isinstance(chunk, tuple):
+        return chunk
+    array, half = chunk
+    return jnp.split(array, 2)[half]
+
+
 def merge_pieces(pieces):
     count = max(1, 128 // (pieces[0][0].shape[1] // 2))
     if count == 1:
         return pieces
     merged = []
     for at in range(0, len(pieces), count):
-        joined = [(jnp.concatenate(p[:-1]), p[-1]) for p in pieces[at : at + count]]
+        taken = [[rows_of(chunk) for chunk in p] for p in pieces[at : at + count]]
+        joined = [(jnp.concatenate(p[:-1]), p[-1]) for p in taken]
         gates, ups, downs = zip(*[split_piece(p) for p in joined])
         merged.append(
             join_piece(
@@ -409,11 +428,18 @@
     rows, depth = left.shape
     part = pieces[0][0].shape[1] // 2
     chunks = [chunk for piece in pieces for chunk in piece]
+    blocks = [block_of(chunk) for chunk in chunks]
+    chunks = [chunk[0] if isinstance(chunk, tuple) else chunk for chunk in chunks]
     out = [jax.ShapeDtypeStruct((rows, depth), dtype) for dtype in (jnp.float32, right_dtype)]
     return pl.pallas_call(
         functools.partial(feed_forward_kernel, len(pieces[0]), len(pieces), len(carries)),
         grid=(1,),
-        in_specs=wholes([left, right, *chunks, *carries]) + [ANYWHERE] * len(earlier),
+        in_specs=[
+            *wholes([left, right]),
+            *blocks,
+            *wholes(carries),
+            *[ANYWHERE] * len(earlier),
+        ],
         out_specs=wholes(out),
         out_shape=out,
         scratch_shapes=[
@@ -426,17 +452,14 @@
 
 def add_rows(first, *others):
     arrays = [first, *others]
-    rows, columns = first.shape
-    block = pl.BlockSpec((rows // 4, columns), lambda i: (i, 0))
-
     def kernel(*refs):
         refs[-1][...] = sum(ref[...].astype(jnp.float32) for ref in refs[:-1]).astype(jnp.bfloat16)
 
     return pl.pallas_call(
         kernel,
-        grid=(4,),
-        in_specs=[block] * len(arrays),
-        out_specs=block,
+        grid=(1,),
+        in_specs=wholes(arrays),
+        out_specs=whole(first),
         out_shape=jax.ShapeDtypeStruct(first.shape, jnp.bfloat16),
     )(*arrays)
 
@@ -534,14 +557,17 @@
     far_upper = tensor_xor(after(upper, line), tensor_count, 2)
     lines = plane_pair(line, *sizes)
     across = [[group_xor(v, group_count, 2) for v in pair] for pair in beside]
-    lines = after(jnp.concatenate(lines), beside[0][1], across[0][0], other[1], far_upper)
+    down_pair = plane_pair(far_down, *sizes)
+    lines = after(
+        jnp.concatenate(lines), beside[0][1], across[0][0], other[1], far_upper, down_pair[1]
+    )
     lines = [lines] + plane_rest([lines], *sizes)
-    down_pair = plane_pair(far_down, *sizes)
     near = [pair for pairs in zip(beside, across) for pair in pairs]
     lines += [
         group_xor(lines[0], group_count, 1),
         *[group_xor(v, group_count, 1) for v in lines[1:]],
     ]
+    down_rest = plane_rest([jnp.concatenate(down_pair)], *sizes)
     far_lower = tensor_xor(after(lower, far_upper), tensor_count, 2)
     upper_pair = plane_pair(far_upper, *sizes)
     middle, second = attend(
@@ -551,21 +577,27 @@
         (0, KEY_VALUE_HEADS),
         (hidden_in, norm_gains[1], w_out),
     )
-    far = after(second, far_lower, upper_pair[1], down_pair[1], across[0][1])
+    far = after(second, far_lower, upper_pair[1], *down_rest, across[0][1])
     far = tensor_xor(far, tensor_count, 1)
-    late_down = down_pair + plane_rest(down_pair, *sizes)
-    late_upper = upper_pair + plane_rest(upper_pair, *sizes)
+    upper_rest = plane_rest([jnp.concatenate([after(v, second) for v in upper_pair])], *sizes)
     lower_pair = plane_pair(far_lower, *sizes)
-    late_lower = lower_pair + plane_rest(lower_pair, *sizes)
-    late = list(zip(late_upper, late_lower, late_down))
+    lower_rest = plane_rest([jnp.concatenate(lower_pair)], *sizes)
+    late = zip(
+        upper_pair + halves_of(upper_rest),
+        lower_pair + halves_of(lower_rest),
+        down_pair + halves_of(down_rest),
+    )
+    late = list(late)
     beside = group_xor(second, group_count, 1)
     near = merge_pieces([mine, other] + near)
     late = merge_pieces(late)
     own_early = feed_forward(second, beside, near, [], jnp.float32)
     far_beside = group_xor(
-        after(far, own_early[0], lower_pair[1], *late_down[2:], *late_upper[2:]), group_count, 1
-    )
-    far_early = feed_forward(far, far_beside, near, [], jnp.float32, own_early)
+        after(far, own_early[0], lower_pair[1], *upper_rest), group_count, 1
+    )
+    far_early = feed_forward(
+        far, far_beside, near, [], jnp.float32, [*own_early, *lower_rest]
+    )
     outgoing = select_pages(projected, page_dest[:, 0], group_count, [far])
     far_sum, far_beside_sum = feed_forward(
         far, far_beside, late, far_early, jnp.bfloat16, [outgoing[0]]

time: 169 us -> 167 us (0.988)
  starting transfers between devices: 40.3 us -> 30 us
  waiting for transfers between devices: 52.5 us -> 62 us
  Pallas kernels: 56.2 us -> 53 us
  other arithmetic: 6.07 us -> 8 us
    ppermute x8, starting transfers between devices: 15.3 us -> 9.87 us  [tensor_xor(): return lax.ppermute(value, 'tensor', pairs)]
    ppermute x11 -> x8, starting transfers between devices: 13.2 us -> 8.69 us  [swap_in_plane(): return lax.ppermute(value, ('group', 'tensor'), pairs)]
    ppermute x11 -> x8, waiting for transfers between devices: 33.6 us -> 38 us  [swap_in_plane(): return lax.ppermute(value, ('group', 'tensor'), pairs)]
    ppermute x14, waiting for transfers between devices: 13.9 us -> 17 us  [group_xor(): lax.ppermute(value, 'group', [(g, g ^ bits) for g in range(group_count)])]
    pallas_call x4, Pallas kernels: 15.4 us -> 12.8 us  [feed_forward(): pl.pallas_call(functools.partial(feed_forward_kernel, len(pieces[0]), len...]
    ppermute x8, waiting for transfers between devices: 4.96 us -> 6.91 us  [tensor_xor(): return lax.ppermute(value, 'tensor', pairs)]
    unnamed x46 -> x50, local copies, waits for them, and re-layouts: 6.77 us -> 6.52 us
  transfers between devices with their start and end apart: 35 -> 32, of which waited for: 13 -> 13; matrix products, arithmetic and copies ran while one was open for 5% -> 6% of each run, Pallas kernels for 29% -> 26%
where the time goes in v5:
time: 167 us; the launch traced here: 166 us
  waiting for transfers between devices  62 us (37%)
  Pallas kernels  53 us (32%)
  starting transfers between devices  30 us (18%)
  local copies, waits for them, and re-layouts  10.4 us (6%)
  other arithmetic  8 us (5%)
  between operations  2.93 us (2%)
    ppermute x8, waiting for transfers between devices, swap_in_plane(): return lax.ppermute(value, ('group', 'tensor'), pairs)  38 us
    pallas_call x1, Pallas kernels, attend(): pl.pallas_call(functools.partial(kernel, len(pieces), heads), grid=(1,),...  17.9 us
    ppermute x14, waiting for transfers between devices, group_xor(): lax.ppermute(value, 'group', [(g, g ^ bits) for g in range(group_count)])  17 us
    pallas_call x4, Pallas kernels, feed_forward(): pl.pallas_call(functools.partial(feed_forward_kernel, len(pieces[0]), len...  12.8 us
    ppermute x8, starting transfers between devices, tensor_xor(): return lax.ppermute(value, 'tensor', pairs)  9.87 us
    pallas_call x1, Pallas kernels, project(): pl.pallas_call(project_kernel, grid=(columns // width,), in_specs=[whole(...  8.91 us
    ppermute x8, starting transfers between devices, swap_in_plane(): return lax.ppermute(value, ('group', 'tensor'), pairs)  8.69 us
    ppermute x14, starting transfers between devices, group_xor(): lax.ppermute(value, 'group', [(g, g ^ bits) for g in range(group_count)])  8.42 us
  transfers between devices with their start and end apart: 32, of which 13 were waited for; matrix products, arithmetic and copies ran while one was open for 6% of the time, Pallas kernels for 26%

profile of v5, /device:TPU:0, one launch (start us, length us, event | category | flops | bytes accessed | tf_op | source)
XLA Modules:
  0.0 166.2 jit_solution(17679249515951334656)
XLA Ops:
  0.6 1.0 slice_bitcast_fusion
  1.6 0.5 collective-permute-start.2
  2.2 2.6 %collective-permute-start.1 = (bf16[32,1536]{1,0:T(8,128)(2,1)S(1)}, bf16[32,1536]{1,0:T(8,128)(2,1)S(1)}, u32[]{:S(2)}, u32[]{:S(2)}) collective-permute-start(bf16[32,1536]{1,0:T(8,128)(2,1)S(1)} %get-tuple-element.73), channel_id=1, source_target_pairs={{0,16},{8,24},{16,0},{24,8},{1,17},{9,25},{17,1},{25,9},{2,18},{10... | collective-permute-start | bytes 294920 | tf_op jit(solution)/shard_map/ppermute | solution.py:45
  4.8 0.6 pad_add_fusion.side
  5.4 3.7 %shard_map.113 = (bf16[1536,256]{1,0:T(8,128)(2,1)}, bf16[768,256]{1,0:T(8,128)(2,1)}, bf16[768,256]{1,0:T(8,128)(2,1)}, bf16[768,256]{1,0:T(8,128)(2,1)}) custom-call(s32[2]{0:T(128)} %pad_add_fusion.side, bf16[2,1536,512]{2,1,0:T(8,128)(2,1)} %w_in.3, bf16[512,1536]{1,0:T(8,128)(2,1)} %w_down.3), custom_call_target="tpu_custom_call" | custom-call | tf_op jit(solution)/shard_map/pallas_call | solution.py:140
  9.1 2.9 %collective-permute-start.6 = (bf16[768,256]{1,0:T(8,128)(2,1)}, bf16[768,256]{1,0:T(8,128)(2,1)S(1)}, u32[]{:S(2)}, u32[]{:S(2)}) collective-permute-start(bf16[768,256]{1,0:T(8,128)(2,1)} %get-tuple-element.40.rest_1_), channel_id=1, source_target_pairs={{0,4},{1,5},{2,6},{3,7},{4,0},{5,1},{6,2},{7,3},{8,12},{9,13},{10,... | collective-permute-start | bytes 1179656 | tf_op jit(solution)/shard_map/ppermute | solution.py:31
  12.0 1.5 collective-permute-start.9
  13.5 0.6 dynamic_slice.3
  16.1 0.6 fusion.4
  16.7 0.9 fusion.1
  17.7 1.4 collective-permute-start.5
  19.1 1.7 %collective-permute-start.4 = (bf16[32,1536]{1,0:T(8,128)(2,1)S(1)}, bf16[32,1536]{1,0:T(8,128)(2,1)S(1)}, u32[]{:S(2)}, u32[]{:S(2)}) collective-permute-start(bf16[32,1536]{1,0:T(8,128)(2,1)S(1)} %fusion.1), channel_id=1, source_target_pairs={{0,4},{1,5},{2,6},{3,7},{4,0},{5,1},{6,2},{7,3},{8,12},{9,13},{10,... | collective-permute-start | bytes 294920 | tf_op jit(solution)/shard_map/ppermute | solution.py:31
  20.8 1.3 collective-permute-start.3
  22.3 0.5 fusion.2
  22.9 0.8 copy.20.cosine
  23.7 0.8 pad_maximum_fusion.5.sine
  24.5 8.9 %shard_map.114.projected = bf16[256,3072]{1,0:T(8,128)(2,1)} custom-call(bf16[256,1536]{1,0:T(8,128)(2,1)} %hidden.2, f32[1,1536]{1,0:T(1,128)} %get-tuple-element.76.gain, bf16[1536,3072]{1,0:T(8,128)(2,1)} %weight.1, f32[256,96]{1,0:T(8,128)} %copy.20.cosine, f32[256,96]{1,0:T(8,128)} %pad_maximum_fusion.5.sine), custom_call_target="tpu_custom_call" | custom-call | flops 2415919104 | bytes 9437184 | tf_op jit(solution)/shard_map/pallas_call | solution.py:260
  33.4 1.5 collective-permute-start.10
  34.9 3.8 %collective-permute-done.4 = bf16[32,1536]{1,0:T(8,128)(2,1)S(1)} collective-permute-done((bf16[32,1536]{1,0:T(8,128)(2,1)S(1)}, bf16[32,1536]{1,0:T(8,128)(2,1)S(1)}, u32[]{:S(2)}, u32[]{:S(2)}) %collective-permute-start.4) | collective-permute-done | bytes 98336 | tf_op jit(solution)/shard_map/ppermute | solution.py:31
  38.7 0.9 pad_maximum_fusion.4
  39.7 1.6 collective-permute-start.7
  41.3 1.5 collective-permute-start.8
  42.8 0.5 collective-permute-start.12
  43.8 0.7 pad_add_fusion.1.side
  44.5 3.2 %shard_map.115 = (bf16[1536,256]{1,0:T(8,128)(2,1)}, bf16[768,256]{1,0:T(8,128)(2,1)}) custom-call(s32[2]{0:T(128)} %pad_add_fusion.1.side, bf16[2,1536,512]{2,1,0:T(8,128)(2,1)} %w_in.3, bf16[512,1536]{1,0:T(8,128)(2,1)} %w_down.3), custom_call_target="tpu_custom_call" | custom-call | tf_op jit(solution)/shard_map/pallas_call | solution.py:140
  47.7 8.4 %collective-permute-done.7 = bf16[128,1536]{1,0:T(8,128)(2,1)} collective-permute-done((bf16[128,1536]{1,0:T(8,128)(2,1)S(1)}, bf16[128,1536]{1,0:T(8,128)(2,1)}, u32[]{:S(2)}, u32[]{:S(2)}) %collective-permute-start.7) | collective-permute-done | bytes 393248 | tf_op jit(solution)/shard_map/ppermute | solution.py:82
  56.1 1.0 pad_maximum_fusion.rest_0_
  57.2 3.0 %collective-permute-done.12.rest_5_ = bf16[768,256]{1,0:T(8,128)(2,1)S(1)} collective-permute-done((bf16[768,256]{1,0:T(8,128)(2,1)S(1)}, bf16[768,256]{1,0:T(8,128)(2,1)S(1)}, u32[]{:S(2)}, u32[]{:S(2)}) %collective-permute-start.12) | collective-permute-done | bytes 393248 | tf_op jit(solution)/shard_map/ppermute | solution.py:82
  60.2 2.4 %collective-permute-done.11.rest_0_ = bf16[768,256]{1,0:T(8,128)(2,1)S(1)} collective-permute-done((bf16[768,256]{1,0:T(8,128)(2,1)}, bf16[768,256]{1,0:T(8,128)(2,1)S(1)}, u32[]{:S(2)}, u32[]{:S(2)}) %collective-permute-start.11) | collective-permute-done | bytes 393248 | tf_op jit(solution)/shard_map/ppermute | solution.py:31
  62.6 0.9 copy-done.2
  63.5 0.7 collective-permute-start.13
  64.2 11.4 %collective-permute-done.13.rest_1_ = bf16[256,1536]{1,0:T(8,128)(2,1)} collective-permute-done((bf16[256,1536]{1,0:T(8,128)(2,1)S(1)}, bf16[256,1536]{1,0:T(8,128)(2,1)}, u32[]{:S(2)}, u32[]{:S(2)}) %collective-permute-start.13) | collective-permute-done | bytes 786464 | tf_op jit(solution)/shard_map/ppermute | solution.py:82
  75.6 0.9 pad_maximum_fusion.1
  76.5 0.7 collective-permute-start.18
  77.2 1.3 collective-permute-start.17
  78.5 0.7 collective-permute-start.19
  79.2 0.9 copy-done.17
  80.1 0.8 copy.21.row_ids
  80.9 17.9 %shard_map.116 = (bf16[256,1536]{1,0:T(8,128)(2,1)}, bf16[256,1536]{1,0:T(8,128)(2,1)}) custom-call(s32[256,1]{1,0:T(8,128)} %copy.21.row_ids, s32[1,256]{1,0:T(1,128)} %column_ids.1, bf16[256,3072]{1,0:T(8,128)(2,1)} %shard_map.114.projected, bf16[256,1536]{1,0:T(8,128)(2,1)} %hidden.2, f32[1,1536]{1,0:T(1,128)} %get-tuple-element.75.gain, ...), custom_call_target="tpu_custom_call" | custom-call | tf_op jit(solution)/shard_map/pallas_call | solution.py:383
  99.4 1.5 collective-permute-start.23
  100.9 2.0 %collective-permute-start.20 = (bf16[256,1536]{1,0:T(8,128)(2,1)S(1)}, bf16[256,1536]{1,0:T(8,128)(2,1)S(1)}, u32[]{:S(2)}, u32[]{:S(2)}) collective-permute-start(bf16[256,1536]{1,0:T(8,128)(2,1)S(1)} %copy-done.5), channel_id=1, source_target_pairs={{0,2},{1,3},{2,0},{3,1},{4,6},{5,7},{6,4},{7,5},{8,10},{9,11},{10,... | collective-permute-start | bytes 2359304 | tf_op jit(solution)/shard_map/ppermute | solution.py:31
  102.9 1.5 collective-permute-start.22
  104.4 10.6 %collective-permute-done.22.rest_4_ = bf16[768,256]{1,0:T(8,128)(2,1)S(1)} collective-permute-done((bf16[768,256]{1,0:T(8,128)(2,1)S(1)}, bf16[768,256]{1,0:T(8,128)(2,1)S(1)}, u32[]{:S(2)}, u32[]{:S(2)}) %collective-permute-start.22) | collective-permute-done | bytes 393248 | tf_op jit(solution)/shard_map/ppermute | solution.py:82
  115.0 0.9 collective-permute-start.25
  116.0 1.0 copy-done.8
  117.0 3.8 %shard_map.117 = (f32[256,1536]{1,0:T(8,128)S(1)}, f32[256,1536]{1,0:T(8,128)S(1)}) custom-call(bf16[256,1536]{1,0:T(8,128)(2,1)S(1)} %copy-done.5, bf16[256,1536]{1,0:T(8,128)(2,1)S(1)} %collective-permute-done.21.right, bf16[1536,256]{1,0:T(8,128)(2,1)S(1)} %copy-done.1, bf16[768,256]{1,0:T(8,128)(2,1)S(1)} %copy-done.7, bf16[1536,256]{1,0:T(8,128)(2,1)S(1)} %copy-done.4, ...), custom_call_target="tpu_custom_call" | custom-call | tf_op jit(solution)/shard_map/pallas_call | solution.py:434
  121.7 0.8 shard_map.119
  122.5 4.6 %collective-permute-done.25.rest_10_.rest_7_ = bf16[1536,256]{1,0:T(8,128)(2,1)S(1)} collective-permute-done((bf16[1536,256]{1,0:T(8,128)(2,1)S(1)}, bf16[1536,256]{1,0:T(8,128)(2,1)S(1)}, u32[]{:S(2)}, u32[]{:S(2)}) %collective-permute-start.25) | collective-permute-done | bytes 786464 | tf_op jit(solution)/shard_map/ppermute | solution.py:82
  127.1 3.7 %shard_map.118 = (f32[256,1536]{1,0:T(8,128)S(1)}, f32[256,1536]{1,0:T(8,128)S(1)}) custom-call(bf16[256,1536]{1,0:T(8,128)(2,1)S(1)} %collective-permute-done.20.left.rest_0_, bf16[256,1536]{1,0:T(8,128)(2,1)S(1)} %collective-permute-done.24.right, bf16[1536,256]{1,0:T(8,128)(2,1)S(1)} %copy-done.1, bf16[768,256]{1,0:T(8,128)(2,1)S(1)} %copy-done.7, ...), custom_call_target="tpu_custom_call" | custom-call | tf_op jit(solution)/shard_map/pallas_call | solution.py:434
  130.8 2.6 %shard_map.120 = (f32[256,1536]{1,0:T(8,128)S(1)}, bf16[256,1536]{1,0:T(8,128)(2,1)S(1)}) custom-call(bf16[256,1536]{1,0:T(8,128)(2,1)S(1)} %collective-permute-done.20.left.rest_0_, bf16[256,1536]{1,0:T(8,128)(2,1)S(1)} %collective-permute-done.24.right, bf16[768,256]{1,0:T(8,128)(2,1)S(1)} %collective-permute-done.11.rest_0_, ...), custom_call_target="tpu_custom_call" | custom-call | tf_op jit(solution)/shard_map/pallas_call | solution.py:434
  133.5 2.3 %collective-permute-done.26 = bf16[256,1536]{1,0:T(8,128)(2,1)S(1)} collective-permute-done((bf16[256,1536]{1,0:T(8,128)(2,1)S(1)}, bf16[256,1536]{1,0:T(8,128)(2,1)S(1)}, u32[]{:S(2)}, u32[]{:S(2)}) %collective-permute-start.26) | collective-permute-done | bytes 786464 | tf_op jit(solution)/shard_map/ppermute | solution.py:45
  135.8 1.1 add_convert_fusion
  137.0 1.5 collective-permute-start.28
  138.8 2.6 %shard_map.121 = (f32[256,1536]{1,0:T(8,128)S(1)}, bf16[256,1536]{1,0:T(8,128)(2,1)S(1)}) custom-call(bf16[256,1536]{1,0:T(8,128)(2,1)S(1)} %copy-done.5, bf16[256,1536]{1,0:T(8,128)(2,1)S(1)} %collective-permute-done.21.right, bf16[768,256]{1,0:T(8,128)(2,1)S(1)} %collective-permute-done.11.rest_0_, bf16[768,256]{1,0:T(8,128)(2,1)S(1)} %collective-permute-done.16.rest_1_, ...), custom_call_target="tpu_custom_call" | custom-call | tf_op jit(solution)/shard_map/pallas_call | solution.py:434
  141.4 1.2 copy-done.11
  142.6 0.9 copy-done.13
  143.4 5.5 %collective-permute-done.28.rest_2_ = bf16[128,1536]{1,0:T(8,128)(2,1)S(1)} collective-permute-done((bf16[128,1536]{1,0:T(8,128)(2,1)S(1)}, bf16[128,1536]{1,0:T(8,128)(2,1)S(1)}, u32[]{:S(2)}, u32[]{:S(2)}) %collective-permute-start.28) | collective-permute-done | bytes 393248 | tf_op jit(solution)/shard_map/ppermute | solution.py:45
  149.0 7.3 %collective-permute-done.29.rest_3_ = bf16[128,1536]{1,0:T(8,128)(2,1)S(1)} collective-permute-done((bf16[128,1536]{1,0:T(8,128)(2,1)S(1)}, bf16[128,1536]{1,0:T(8,128)(2,1)S(1)}, u32[]{:S(2)}, u32[]{:S(2)}) %collective-permute-start.29) | collective-permute-done | bytes 393248 | tf_op jit(solution)/shard_map/ppermute | solution.py:45
  156.3 0.8 copy-done.20
  157.0 2.7 %shard_map.122 = bf16[4,128,1536]{2,1,0:T(8,128)(2,1)} custom-call(s32[1]{0:T(128)} %bitcast.12.group, bf16[128,1536]{1,0:T(8,128)(2,1)} %copy-done.10, bf16[128,1536]{1,0:T(8,128)(2,1)} %copy-done.18, bf16[128,1536]{1,0:T(8,128)(2,1)} %copy-done.19, bf16[128,1536]{1,0:T(8,128)(2,1)} %copy-done.20), custom_call_target="tpu_custom_call" | custom-call | tf_op jit(solution)/shard_map/pallas_call | solution.py:514
  159.7 0.8 collective-permute-start.30
  160.5 1.9 %collective-permute-done.30.refs_1_ = bf16[256,1536]{1,0:T(8,128)(2,1)S(1)} collective-permute-done((bf16[256,1536]{1,0:T(8,128)(2,1)S(1)}, bf16[256,1536]{1,0:T(8,128)(2,1)S(1)}, u32[]{:S(2)}, u32[]{:S(2)}) %collective-permute-start.30) | collective-permute-done | bytes 786464 | tf_op jit(solution)/shard_map/ppermute | solution.py:45
  162.4 0.9 copy-done.16
  163.3 3.0 %shard_map.123 = bf16[256,1536]{1,0:T(8,128)(2,1)} custom-call(f32[256,1536]{1,0:T(8,128)} %copy-done.11, bf16[256,1536]{1,0:T(8,128)(2,1)} %copy-done.16, bf16[256,1536]{1,0:T(8,128)(2,1)} %collective-permute-done.31.refs_2_), custom_call_target="tpu_custom_call" | custom-call | tf_op jit(solution)/shard_map/pallas_call | solution.py:458
  (85 shorter events, 2.8 us)
Async XLA Ops:
  1.6 15.1 %collective-permute-start.2 = (bf16[32,1536]{1,0:T(8,128)(2,1)S(1)}, bf16[32,1536]{1,0:T(8,128)(2,1)S(1)}, u32[]{:S(2)}, u32[]{:S(2)}) collective-permute-start(bf16[32,1536]{1,0:T(8,128)(2,1)S(1)} %get-tuple-element.72), channel_id=1, source_target_pairs={{0,8},{8,0},{16,24},{24,16},{1,9},{9,1},{17,25},{25,17},{2,10},{10... | collective-permute-start | bytes 294920 | tf_op jit(solution)/shard_map/ppermute | solution.py:45
  2.2 14.5 %collective-permute-start.1 = (bf16[32,1536]{1,0:T(8,128)(2,1)S(1)}, bf16[32,1536]{1,0:T(8,128)(2,1)S(1)}, u32[]{:S(2)}, u32[]{:S(2)}) collective-permute-start(bf16[32,1536]{1,0:T(8,128)(2,1)S(1)} %get-tuple-element.73), channel_id=1, source_target_pairs={{0,16},{8,24},{16,0},{24,8},{1,17},{9,25},{17,1},{25,9},{2,18},{10... | collective-permute-start | bytes 294920 | tf_op jit(solution)/shard_map/ppermute | solution.py:45
  4.7 12.0 %collective-permute-start = (bf16[32,1536]{1,0:T(8,128)(2,1)S(1)}, bf16[32,1536]{1,0:T(8,128)(2,1)S(1)}, u32[]{:S(2)}, u32[]{:S(2)}) collective-permute-start(bf16[32,1536]{1,0:T(8,128)(2,1)S(1)} %get-tuple-element.74), channel_id=1, source_target_pairs={{0,24},{8,16},{16,8},{24,0},{1,25},{9,17},{17,9},{25,1},{2,26},{10... | collective-permute-start | bytes 294920 | tf_op jit(solution)/shard_map/ppermute | solution.py:45
  5.4 8.1 %copy-start.24 = (s32[8]{0:T(128)S(1)}, s32[8]{0:T(128)}, u32[]{:S(2)}) copy-start(s32[8]{0:T(128)} %param.18) | copy-start | bytes 100
  5.4 10.7 %copy-start.22 = (f32[2,1536]{1,0:T(2,128)S(1)}, f32[2,1536]{1,0:T(2,128)}, u32[]{:S(2)}) copy-start(f32[2,1536]{1,0:T(2,128)} %param.12) | copy-start | bytes 36868
  5.4 16.7 %copy-start.21 = (s32[1,256]{1,0:T(1,128)S(1)}, s32[1,256]{1,0:T(1,128)}, u32[]{:S(2)}) copy-start(s32[1,256]{1,0:T(1,128)} %column_ids.1) | copy-start | bytes 3076
  9.1 30.6 %collective-permute-start.6 = (bf16[768,256]{1,0:T(8,128)(2,1)}, bf16[768,256]{1,0:T(8,128)(2,1)S(1)}, u32[]{:S(2)}, u32[]{:S(2)}) collective-permute-start(bf16[768,256]{1,0:T(8,128)(2,1)} %get-tuple-element.40.rest_1_), channel_id=1, source_target_pairs={{0,4},{1,5},{2,6},{3,7},{4,0},{5,1},{6,2},{7,3},{8,12},{9,13},{10,... | collective-permute-start | bytes 1179656 | tf_op jit(solution)/shard_map/ppermute | solution.py:31
  12.0 21.4 %collective-permute-start.9 = (bf16[1536,256]{1,0:T(8,128)(2,1)}, bf16[1536,256]{1,0:T(8,128)(2,1)S(1)}, u32[]{:S(2)}, u32[]{:S(2)}) collective-permute-start(bf16[1536,256]{1,0:T(8,128)(2,1)} %get-tuple-element.37.rest_0_), channel_id=1, source_target_pairs={{0,1},{1,0},{2,3},{3,2},{4,5},{5,4},{6,7},{7,6},{8,9},{9,8},{10,11... | collective-permute-start | bytes 2359304 | tf_op jit(solution)/shard_map/ppermute | solution.py:41
  17.7 17.2 %collective-permute-start.5 = (bf16[32,1536]{1,0:T(8,128)(2,1)S(1)}, bf16[32,1536]{1,0:T(8,128)(2,1)S(1)}, u32[]{:S(2)}, u32[]{:S(2)}) collective-permute-start(bf16[32,1536]{1,0:T(8,128)(2,1)S(1)} %fusion.1), channel_id=1, source_target_pairs={{0,6},{1,7},{2,4},{3,5},{4,2},{5,3},{6,0},{7,1},{8,14},{9,15},{10,... | collective-permute-start | bytes 294920 | tf_op jit(solution)/shard_map/ppermute | solution.py:31
  19.1 19.7 %collective-permute-start.4 = (bf16[32,1536]{1,0:T(8,128)(2,1)S(1)}, bf16[32,1536]{1,0:T(8,128)(2,1)S(1)}, u32[]{:S(2)}, u32[]{:S(2)}) collective-permute-start(bf16[32,1536]{1,0:T(8,128)(2,1)S(1)} %fusion.1), channel_id=1, source_target_pairs={{0,4},{1,5},{2,6},{3,7},{4,0},{5,1},{6,2},{7,3},{8,12},{9,13},{10,... | collective-permute-start | bytes 294920 | tf_op jit(solution)/shard_map/ppermute | solution.py:31
  20.8 18.0 %collective-permute-start.3 = (bf16[32,1536]{1,0:T(8,128)(2,1)S(1)}, bf16[32,1536]{1,0:T(8,128)(2,1)}, u32[]{:S(2)}, u32[]{:S(2)}) collective-permute-start(bf16[32,1536]{1,0:T(8,128)(2,1)S(1)} %fusion.1), channel_id=1, source_target_pairs={{0,2},{1,3},{2,0},{3,1},{4,6},{5,7},{6,4},{7,5},{8,10},{9,11},{10,... | collective-permute-start | bytes 294920 | tf_op jit(solution)/shard_map/ppermute | solution.py:31
  24.5 16.8 %copy-start.6 = (bf16[768,256]{1,0:T(8,128)(2,1)S(1)}, bf16[768,256]{1,0:T(8,128)(2,1)}, u32[]{:S(2)}) copy-start(bf16[768,256]{1,0:T(8,128)(2,1)} %get-tuple-element.40.rest_1_) | copy-start | bytes 1179652
  33.4 29.2 %collective-permute-start.10 = (bf16[1536,256]{1,0:T(8,128)(2,1)S(1)}, bf16[1536,256]{1,0:T(8,128)(2,1)S(1)}, u32[]{:S(2)}, u32[]{:S(2)}) collective-permute-start(bf16[1536,256]{1,0:T(8,128)(2,1)S(1)} %collective-permute-done.9.rest_4_), channel_id=1, source_target_pairs={{0,16},{8,24},{16,0},{24,8},{1,17},{9,25},{17,1},{25,9},{2,18},{10... | collective-permute-start | bytes 2359304 | tf_op jit(solution)/shard_map/ppermute | solution.py:45
  39.7 16.4 %collective-permute-start.7 = (bf16[128,1536]{1,0:T(8,128)(2,1)S(1)}, bf16[128,1536]{1,0:T(8,128)(2,1)}, u32[]{:S(2)}, u32[]{:S(2)}) collective-permute-start(bf16[128,1536]{1,0:T(8,128)(2,1)S(1)} %pad_maximum_fusion.4), channel_id=1, source_target_pairs={{0,16},{1,17},{2,18},{3,19},{4,20},{5,21},{6,22},{7,23},{8,9},{9,8... | collective-permute-start | bytes 1179656 | tf_op jit(solution)/shard_map/ppermute | solution.py:82
  41.3 15.9 %collective-permute-start.8 = (bf16[768,256]{1,0:T(8,128)(2,1)S(1)}, bf16[768,256]{1,0:T(8,128)(2,1)}, u32[]{:S(2)}, u32[]{:S(2)}) collective-permute-start(bf16[768,256]{1,0:T(8,128)(2,1)S(1)} %copy-done.6), channel_id=1, source_target_pairs={{0,1},{1,0},{2,3},{3,2},{4,5},{5,4},{6,7},{7,6},{8,9},{9,8},{10,11... | collective-permute-start | bytes 1179656 | tf_op jit(solution)/shard_map/ppermute | solution.py:41
  42.8 17.4 %collective-permute-start.12 = (bf16[768,256]{1,0:T(8,128)(2,1)S(1)}, bf16[768,256]{1,0:T(8,128)(2,1)S(1)}, u32[]{:S(2)}, u32[]{:S(2)}) collective-permute-start(bf16[768,256]{1,0:T(8,128)(2,1)S(1)} %collective-permute-done.6.rest_2_), channel_id=1, source_target_pairs={{0,16},{1,17},{2,18},{3,19},{4,20},{5,21},{6,22},{7,23},{8,9},{9,8... | collective-permute-start | bytes 1179656 | tf_op jit(solution)/shard_map/ppermute | solution.py:82
  43.3 19.3 %collective-permute-start.11 = (bf16[768,256]{1,0:T(8,128)(2,1)}, bf16[768,256]{1,0:T(8,128)(2,1)S(1)}, u32[]{:S(2)}, u32[]{:S(2)}) collective-permute-start(bf16[768,256]{1,0:T(8,128)(2,1)} %get-tuple-element.45), channel_id=1, source_target_pairs={{0,4},{1,5},{2,6},{3,7},{4,0},{5,1},{6,2},{7,3},{8,12},{9,13},{10,... | collective-permute-start | bytes 1179656 | tf_op jit(solution)/shard_map/ppermute | solution.py:31
  57.1 22.1 %copy-start.15 = (bf16[256,1536]{1,0:T(8,128)(2,1)}, bf16[256,1536]{1,0:T(8,128)(2,1)S(1)}, u32[]{:S(2)}) copy-start(bf16[256,1536]{1,0:T(8,128)(2,1)S(1)} %pad_maximum_fusion.rest_0_) | copy-start | bytes 2359300
  62.6 0.9 copy-start.2
  63.5 12.1 %collective-permute-start.13 = (bf16[256,1536]{1,0:T(8,128)(2,1)S(1)}, bf16[256,1536]{1,0:T(8,128)(2,1)}, u32[]{:S(2)}, u32[]{:S(2)}) collective-permute-start(bf16[256,1536]{1,0:T(8,128)(2,1)S(1)} %pad_maximum_fusion.rest_0_), channel_id=1, source_target_pairs={{0,1},{1,0},{2,3},{3,2},{4,5},{5,4},{6,7},{7,6},{8,24},{9,25},{10,... | collective-permute-start | bytes 2359304 | tf_op jit(solution)/shard_map/ppermute | solution.py:82
  64.2 15.1 %collective-permute-start.14 = (bf16[256,1536]{1,0:T(8,128)(2,1)S(1)}, bf16[256,1536]{1,0:T(8,128)(2,1)S(1)}, u32[]{:S(2)}, u32[]{:S(2)}) collective-permute-start(bf16[256,1536]{1,0:T(8,128)(2,1)S(1)} %pad_maximum_fusion.rest_0_), channel_id=1, source_target_pairs={{0,8},{8,0},{16,24},{24,16},{1,9},{9,1},{17,25},{25,17},{2,10},{10... | collective-permute-start | bytes 2359304 | tf_op jit(solution)/shard_map/ppermute | solution.py:45
  75.6 5.3 %collective-permute-start.15 = (bf16[256,1536]{1,0:T(8,128)(2,1)}, bf16[256,1536]{1,0:T(8,128)(2,1)}, u32[]{:S(2)}, u32[]{:S(2)}) collective-permute-start(bf16[256,1536]{1,0:T(8,128)(2,1)} %collective-permute-done.13.rest_1_), channel_id=1, source_target_pairs={{0,8},{8,0},{16,24},{24,16},{1,9},{9,1},{17,25},{25,17},{2,10},{10... | collective-permute-start | bytes 2359304 | tf_op jit(solution)/shard_map/ppermute | solution.py:45
  76.5 22.9 %collective-permute-start.18 = (bf16[1536,256]{1,0:T(8,128)(2,1)}, bf16[1536,256]{1,0:T(8,128)(2,1)S(1)}, u32[]{:S(2)}, u32[]{:S(2)}) collective-permute-start(bf16[1536,256]{1,0:T(8,128)(2,1)} %pad_maximum_fusion.1), channel_id=1, source_target_pairs={{0,1},{1,0},{2,3},{3,2},{4,5},{5,4},{6,7},{7,6},{8,24},{9,25},{10,... | collective-permute-start | bytes 2359304 | tf_op jit(solution)/shard_map/ppermute | solution.py:82
  77.2 21.8 %collective-permute-start.17 = (bf16[768,256]{1,0:T(8,128)(2,1)S(1)}, bf16[768,256]{1,0:T(8,128)(2,1)S(1)}, u32[]{:S(2)}, u32[]{:S(2)}) collective-permute-start(bf16[768,256]{1,0:T(8,128)(2,1)S(1)} %collective-permute-done.11.rest_0_), channel_id=1, source_target_pairs={{0,16},{1,17},{2,18},{3,19},{4,20},{5,21},{6,22},{7,23},{8,9},{9,8... | collective-permute-start | bytes 1179656 | tf_op jit(solution)/shard_map/ppermute | solution.py:82
  78.5 20.5 %collective-permute-start.19 = (bf16[768,256]{1,0:T(8,128)(2,1)}, bf16[768,256]{1,0:T(8,128)(2,1)}, u32[]{:S(2)}, u32[]{:S(2)}) collective-permute-start(bf16[768,256]{1,0:T(8,128)(2,1)} %collective-permute-done.8.rest_5_), channel_id=1, source_target_pairs={{0,16},{8,24},{16,0},{24,8},{1,17},{9,25},{17,1},{25,9},{2,18},{10... | collective-permute-start | bytes 1179656 | tf_op jit(solution)/shard_map/ppermute | solution.py:45
  79.2 0.9 copy-start.17
  80.1 19.3 %collective-permute-start.16 = (bf16[768,256]{1,0:T(8,128)(2,1)}, bf16[768,256]{1,0:T(8,128)(2,1)S(1)}, u32[]{:S(2)}, u32[]{:S(2)}) collective-permute-start(bf16[768,256]{1,0:T(8,128)(2,1)} %get-tuple-element.49), channel_id=1, source_target_pairs={{0,4},{1,5},{2,6},{3,7},{4,0},{5,1},{6,2},{7,3},{8,12},{9,13},{10,... | collective-permute-start | bytes 1179656 | tf_op jit(solution)/shard_map/ppermute | solution.py:31
  80.9 35.0 %copy-start.7 = (bf16[768,256]{1,0:T(8,128)(2,1)S(1)}, bf16[768,256]{1,0:T(8,128)(2,1)}, u32[]{:S(2)}) copy-start(bf16[768,256]{1,0:T(8,128)(2,1)} %get-tuple-element.40.rest_1_) | copy-start | bytes 1179652
  98.9 2.0 %copy-start.5 = (bf16[256,1536]{1,0:T(8,128)(2,1)S(1)}, bf16[256,1536]{1,0:T(8,128)(2,1)}, u32[]{:S(2)}) copy-start(bf16[256,1536]{1,0:T(8,128)(2,1)} %get-tuple-element.64.left) | copy-start | bytes 2359300
  98.9 17.1 %copy-start.1 = (bf16[1536,256]{1,0:T(8,128)(2,1)S(1)}, bf16[1536,256]{1,0:T(8,128)(2,1)}, u32[]{:S(2)}) copy-start(bf16[1536,256]{1,0:T(8,128)(2,1)} %get-tuple-element.37.rest_0_) | copy-start | bytes 2359300
  98.9 17.1 %copy-start.3 = (bf16[1536,256]{1,0:T(8,128)(2,1)S(1)}, bf16[1536,256]{1,0:T(8,128)(2,1)}, u32[]{:S(2)}) copy-start(bf16[1536,256]{1,0:T(8,128)(2,1)} %copy-done.2) | copy-start | bytes 2359300
  98.9 17.1 %copy-start.4 = (bf16[1536,256]{1,0:T(8,128)(2,1)S(1)}, bf16[1536,256]{1,0:T(8,128)(2,1)}, u32[]{:S(2)}) copy-start(bf16[1536,256]{1,0:T(8,128)(2,1)} %get-tuple-element.51.rest_2_) | copy-start | bytes 2359300
  98.9 17.0 %collective-permute-start.21 = (bf16[256,1536]{1,0:T(8,128)(2,1)}, bf16[256,1536]{1,0:T(8,128)(2,1)S(1)}, u32[]{:S(2)}, u32[]{:S(2)}) collective-permute-start(bf16[256,1536]{1,0:T(8,128)(2,1)} %get-tuple-element.64.left), channel_id=1, source_target_pairs={{0,8},{8,0},{16,24},{24,16},{1,9},{9,1},{17,25},{25,17},{2,10},{10... | collective-permute-start | bytes 2359304 | tf_op jit(solution)/shard_map/ppermute | solution.py:45
  99.4 21.4 %collective-permute-start.23 = (bf16[1536,256]{1,0:T(8,128)(2,1)S(1)}, bf16[1536,256]{1,0:T(8,128)(2,1)S(1)}, u32[]{:S(2)}, u32[]{:S(2)}) collective-permute-start(bf16[1536,256]{1,0:T(8,128)(2,1)S(1)} %pad_maximum_fusion.2), channel_id=1, source_target_pairs={{0,1},{1,0},{2,3},{3,2},{4,5},{5,4},{6,7},{7,6},{8,24},{9,25},{10,... | collective-permute-start | bytes 2359304 | tf_op jit(solution)/shard_map/ppermute | solution.py:82
  100.9 20.2 %collective-permute-start.20 = (bf16[256,1536]{1,0:T(8,128)(2,1)S(1)}, bf16[256,1536]{1,0:T(8,128)(2,1)S(1)}, u32[]{:S(2)}, u32[]{:S(2)}) collective-permute-start(bf16[256,1536]{1,0:T(8,128)(2,1)S(1)} %copy-done.5), channel_id=1, source_target_pairs={{0,2},{1,3},{2,0},{3,1},{4,6},{5,7},{6,4},{7,5},{8,10},{9,11},{10,... | collective-permute-start | bytes 2359304 | tf_op jit(solution)/shard_map/ppermute | solution.py:31
  102.9 12.1 %collective-permute-start.22 = (bf16[768,256]{1,0:T(8,128)(2,1)S(1)}, bf16[768,256]{1,0:T(8,128)(2,1)S(1)}, u32[]{:S(2)}, u32[]{:S(2)}) collective-permute-start(bf16[768,256]{1,0:T(8,128)(2,1)S(1)} %collective-permute-done.16.rest_1_), channel_id=1, source_target_pairs={{0,16},{1,17},{2,18},{3,19},{4,20},{5,21},{6,22},{7,23},{8,9},{9,8... | collective-permute-start | bytes 1179656 | tf_op jit(solution)/shard_map/ppermute | solution.py:82
  115.0 12.1 %collective-permute-start.25 = (bf16[1536,256]{1,0:T(8,128)(2,1)S(1)}, bf16[1536,256]{1,0:T(8,128)(2,1)S(1)}, u32[]{:S(2)}, u32[]{:S(2)}) collective-permute-start(bf16[1536,256]{1,0:T(8,128)(2,1)S(1)} %pad_maximum_fusion.3), channel_id=1, source_target_pairs={{0,1},{1,0},{2,3},{3,2},{4,5},{5,4},{6,7},{7,6},{8,24},{9,25},{10,... | collective-permute-start | bytes 2359304 | tf_op jit(solution)/shard_map/ppermute | solution.py:82
  116.0 1.0 copy-start.8
  117.0 4.5 %copy-start.23 = (s32[16,1]{0,1:T(1,128)S(1)}, s32[16,1]{0,1:T(1,128)}, u32[]{:S(2)}) copy-start(s32[16,1]{0,1:T(1,128)} %param.19) | copy-start | bytes 196
  117.0 4.8 %copy-start = (bf16[256,3072]{1,0:T(8,128)(2,1)S(1)}, bf16[256,3072]{1,0:T(8,128)(2,1)}, u32[]{:S(2)}) copy-start(bf16[256,3072]{1,0:T(8,128)(2,1)} %shard_map.114.projected) | copy-start | bytes 4718596
  120.8 6.3 %copy-start.9 = (bf16[768,256]{1,0:T(8,128)(2,1)S(1)}, bf16[768,256]{1,0:T(8,128)(2,1)}, u32[]{:S(2)}) copy-start(bf16[768,256]{1,0:T(8,128)(2,1)} %get-tuple-element.43.rest_3_) | copy-start | bytes 1179652
  121.1 5.9 %collective-permute-start.24 = (bf16[256,1536]{1,0:T(8,128)(2,1)S(1)}, bf16[256,1536]{1,0:T(8,128)(2,1)S(1)}, u32[]{:S(2)}, u32[]{:S(2)}) collective-permute-start(bf16[256,1536]{1,0:T(8,128)(2,1)S(1)} %collective-permute-done.20.left.rest_0_), channel_id=1, source_target_pairs={{0,8},{8,0},{16,24},{24,16},{1,9},{9,1},{17,25},{25,17},{2,10},{10... | collective-permute-start | bytes 2359304 | tf_op jit(solution)/shard_map/ppermute | solution.py:45
  122.5 8.3 %copy-start.10 = (bf16[128,1536]{1,0:T(8,128)(2,1)}, bf16[128,1536]{1,0:T(8,128)(2,1)S(1)}, u32[]{:S(2)}) copy-start(bf16[128,1536]{1,0:T(8,128)(2,1)S(1)} %get-tuple-element.59.rest_14_.rest_0_) | copy-start | bytes 1179652
  133.4 2.4 %collective-permute-start.26 = (bf16[256,1536]{1,0:T(8,128)(2,1)S(1)}, bf16[256,1536]{1,0:T(8,128)(2,1)S(1)}, u32[]{:S(2)}, u32[]{:S(2)}) collective-permute-start(bf16[256,1536]{1,0:T(8,128)(2,1)S(1)} %get-tuple-element.61), channel_id=1, source_target_pairs={{0,8},{8,0},{16,24},{24,16},{1,9},{9,1},{17,25},{25,17},{2,10},{10... | collective-permute-start | bytes 2359304 | tf_op jit(solution)/shard_map/ppermute | solution.py:45
  135.8 3.0 %copy-start.12 = (bf16[256,1536]{1,0:T(8,128)(2,1)S(1)}, bf16[256,1536]{1,0:T(8,128)(2,1)}, u32[]{:S(2)}) copy-start(bf16[256,1536]{1,0:T(8,128)(2,1)} %get-tuple-element.65.rest_14_) | copy-start | bytes 2359300
  136.9 1.9 %collective-permute-start.27 = (bf16[128,1536]{1,0:T(8,128)(2,1)S(1)}, bf16[128,1536]{1,0:T(8,128)(2,1)S(1)}, u32[]{:S(2)}, u32[]{:S(2)}) collective-permute-start(bf16[128,1536]{1,0:T(8,128)(2,1)S(1)} %get-tuple-element.63), channel_id=1, source_target_pairs={{0,8},{8,0},{16,24},{24,16},{1,9},{9,1},{17,25},{25,17},{2,10},{10... | collective-permute-start | bytes 1179656 | tf_op jit(solution)/shard_map/ppermute | solution.py:45
  137.0 11.9 %collective-permute-start.28 = (bf16[128,1536]{1,0:T(8,128)(2,1)S(1)}, bf16[128,1536]{1,0:T(8,128)(2,1)S(1)}, u32[]{:S(2)}, u32[]{:S(2)}) collective-permute-start(bf16[128,1536]{1,0:T(8,128)(2,1)S(1)} %get-tuple-element.68), channel_id=1, source_target_pairs={{0,16},{8,24},{16,0},{24,8},{1,17},{9,25},{17,1},{25,9},{2,18},{10... | collective-permute-start | bytes 1179656 | tf_op jit(solution)/shard_map/ppermute | solution.py:45
  138.5 17.8 %collective-permute-start.29 = (bf16[128,1536]{1,0:T(8,128)(2,1)S(1)}, bf16[128,1536]{1,0:T(8,128)(2,1)S(1)}, u32[]{:S(2)}, u32[]{:S(2)}) collective-permute-start(bf16[128,1536]{1,0:T(8,128)(2,1)S(1)} %get-tuple-element.69), channel_id=1, source_target_pairs={{0,24},{8,16},{16,8},{24,0},{1,25},{9,17},{17,9},{25,1},{2,26},{10... | collective-permute-start | bytes 1179656 | tf_op jit(solution)/shard_map/ppermute | solution.py:45
  138.7 21.8 %collective-permute-start.31 = (bf16[256,1536]{1,0:T(8,128)(2,1)}, bf16[256,1536]{1,0:T(8,128)(2,1)}, u32[]{:S(2)}, u32[]{:S(2)}) collective-permute-start(bf16[256,1536]{1,0:T(8,128)(2,1)} %add_convert_fusion), channel_id=1, source_target_pairs={{0,2},{1,3},{2,0},{3,1},{4,6},{5,7},{6,4},{7,5},{8,10},{9,11},{10,... | collective-permute-start | bytes 2359304 | tf_op jit(solution)/shard_map/ppermute | solution.py:31
  138.7 2.6 %copy-start.18 = (bf16[128,1536]{1,0:T(8,128)(2,1)}, bf16[128,1536]{1,0:T(8,128)(2,1)S(1)}, u32[]{:S(2)}) copy-start(bf16[128,1536]{1,0:T(8,128)(2,1)S(1)} %collective-permute-done.27.rest_1_) | copy-start | bytes 1179652
  141.4 1.2 copy-start.11
  142.6 0.9 copy-start.13
  149.0 7.3 %copy-start.19 = (bf16[128,1536]{1,0:T(8,128)(2,1)}, bf16[128,1536]{1,0:T(8,128)(2,1)S(1)}, u32[]{:S(2)}) copy-start(bf16[128,1536]{1,0:T(8,128)(2,1)S(1)} %collective-permute-done.28.rest_2_) | copy-start | bytes 1179652
  156.3 0.8 copy-start.20
  157.0 2.7 %copy-start.14 = (bf16[256,1536]{1,0:T(8,128)(2,1)S(1)}, bf16[256,1536]{1,0:T(8,128)(2,1)}, u32[]{:S(2)}) copy-start(bf16[256,1536]{1,0:T(8,128)(2,1)} %copy-done.13) | copy-start | bytes 2359300
  159.7 2.7 %collective-permute-start.30 = (bf16[256,1536]{1,0:T(8,128)(2,1)S(1)}, bf16[256,1536]{1,0:T(8,128)(2,1)S(1)}, u32[]{:S(2)}, u32[]{:S(2)}) collective-permute-start(bf16[256,1536]{1,0:T(8,128)(2,1)S(1)} %copy-done.14), channel_id=1, source_target_pairs={{0,8},{8,0},{16,24},{24,16},{1,9},{9,1},{17,25},{25,17},{2,10},{10... | collective-permute-start | bytes 2359304 | tf_op jit(solution)/shard_map/ppermute | solution.py:45
  162.4 0.9 copy-start.16

commit v6 on v5

--- a/solution.py
+++ b/solution.py
@@ -612,8 +612,8 @@
     own_sum, beside_sum = feed_forward(
         after(second, far_sum, received[1]), beside, late, [*own_early, middle], jnp.bfloat16
     )
+    own_beside = group_xor(after(beside_sum, *received[2:]), group_count, 1)
     received = place_pages(received)
-    own_beside = group_xor(after(beside_sum, received), group_count, 1)
     hidden_out = add_rows(own_sum, own_beside, after(returned, received))
     pages = received.reshape(group_count, CAP, -1, received.shape[2])
     return (hidden_out, pages[None, None])

time: 167 us -> 165 us (0.988)
  waiting for transfers between devices: 62 us -> 60.2 us
    ppermute x14, waiting for transfers between devices: 17 us -> 15.1 us  [group_xor(): lax.ppermute(value, 'group', [(g, g ^ bits) for g in range(group_count)])]
    unnamed x50 -> x46, local copies, waits for them, and re-layouts: 6.52 us -> 5.64 us
  transfers between devices with their start and end apart: 32 -> 32, of which waited for: 13 -> 12; matrix products, arithmetic and copies ran while one was open for 6% -> 6% of each run, Pallas kernels for 26% -> 27%
where the time goes in v6:
time: 165 us; the launch traced here: 164 us
  waiting for transfers between devices  60.2 us (36%)
  Pallas kernels  53.8 us (33%)
  starting transfers between devices  30 us (18%)
  local copies, waits for them, and re-layouts  9.47 us (6%)
  other arithmetic  7.96 us (5%)
  between operations  2.91 us (2%)
    ppermute x8, waiting for transfers between devices, swap_in_plane(): return lax.ppermute(value, ('group', 'tensor'), pairs)  38 us
    pallas_call x1, Pallas kernels, attend(): pl.pallas_call(functools.partial(kernel, len(pieces), heads), grid=(1,),...  17.9 us
    ppermute x14, waiting for transfers between devices, group_xor(): lax.ppermute(value, 'group', [(g, g ^ bits) for g in range(group_count)])  15.1 us
    pallas_call x4, Pallas kernels, feed_forward(): pl.pallas_call(functools.partial(feed_forward_kernel, len(pieces[0]), len...  13.7 us
    ppermute x8, starting transfers between devices, tensor_xor(): return lax.ppermute(value, 'tensor', pairs)  9.86 us
    pallas_call x1, Pallas kernels, project(): pl.pallas_call(project_kernel, grid=(columns // width,), in_specs=[whole(...  8.91 us
    ppermute x8, starting transfers between devices, swap_in_plane(): return lax.ppermute(value, ('group', 'tensor'), pairs)  8.69 us
    ppermute x14, starting transfers between devices, group_xor(): lax.ppermute(value, 'group', [(g, g ^ bits) for g in range(group_count)])  8.41 us
  transfers between devices with their start and end apart: 32, of which 12 were waited for; matrix products, arithmetic and copies ran while one was open for 6% of the time, Pallas kernels for 27%

profile of v6, /device:TPU:0, one launch (start us, length us, event | category | flops | bytes accessed | tf_op | source)
XLA Modules:
  0.0 164.3 jit_solution(17690769878916534528)
XLA Ops:
  0.6 1.0 slice_bitcast_fusion
  1.6 0.5 collective-permute-start.2
  2.2 2.6 %collective-permute-start.1 = (bf16[32,1536]{1,0:T(8,128)(2,1)S(1)}, bf16[32,1536]{1,0:T(8,128)(2,1)S(1)}, u32[]{:S(2)}, u32[]{:S(2)}) collective-permute-start(bf16[32,1536]{1,0:T(8,128)(2,1)S(1)} %get-tuple-element.73), channel_id=1, source_target_pairs={{0,16},{8,24},{16,0},{24,8},{1,17},{9,25},{17,1},{25,9},{2,18},{10... | collective-permute-start | bytes 294920 | tf_op jit(solution)/shard_map/ppermute | solution.py:45
  4.8 0.6 pad_add_fusion.side
  5.4 3.7 %shard_map.113 = (bf16[1536,256]{1,0:T(8,128)(2,1)}, bf16[768,256]{1,0:T(8,128)(2,1)}, bf16[768,256]{1,0:T(8,128)(2,1)}, bf16[768,256]{1,0:T(8,128)(2,1)}) custom-call(s32[2]{0:T(128)} %pad_add_fusion.side, bf16[2,1536,512]{2,1,0:T(8,128)(2,1)} %w_in.3, bf16[512,1536]{1,0:T(8,128)(2,1)} %w_down.3), custom_call_target="tpu_custom_call" | custom-call | tf_op jit(solution)/shard_map/pallas_call | solution.py:140
  9.1 2.9 %collective-permute-start.6 = (bf16[768,256]{1,0:T(8,128)(2,1)}, bf16[768,256]{1,0:T(8,128)(2,1)S(1)}, u32[]{:S(2)}, u32[]{:S(2)}) collective-permute-start(bf16[768,256]{1,0:T(8,128)(2,1)} %get-tuple-element.40.rest_1_), channel_id=1, source_target_pairs={{0,4},{1,5},{2,6},{3,7},{4,0},{5,1},{6,2},{7,3},{8,12},{9,13},{10,... | collective-permute-start | bytes 1179656 | tf_op jit(solution)/shard_map/ppermute | solution.py:31
  12.0 1.5 collective-permute-start.9
  13.5 0.6 dynamic_slice.3
  16.1 0.6 fusion.4
  16.7 0.9 fusion.1
  17.6 1.4 collective-permute-start.5
  19.0 1.7 %collective-permute-start.4 = (bf16[32,1536]{1,0:T(8,128)(2,1)S(1)}, bf16[32,1536]{1,0:T(8,128)(2,1)S(1)}, u32[]{:S(2)}, u32[]{:S(2)}) collective-permute-start(bf16[32,1536]{1,0:T(8,128)(2,1)S(1)} %fusion.1), channel_id=1, source_target_pairs={{0,4},{1,5},{2,6},{3,7},{4,0},{5,1},{6,2},{7,3},{8,12},{9,13},{10,... | collective-permute-start | bytes 294920 | tf_op jit(solution)/shard_map/ppermute | solution.py:31
  20.7 1.3 collective-permute-start.3
  22.3 0.5 fusion.2
  22.9 0.8 copy.20.cosine
  23.7 0.8 pad_maximum_fusion.5.sine
  24.4 8.9 %shard_map.114.projected = bf16[256,3072]{1,0:T(8,128)(2,1)} custom-call(bf16[256,1536]{1,0:T(8,128)(2,1)} %hidden.2, f32[1,1536]{1,0:T(1,128)} %get-tuple-element.76.gain, bf16[1536,3072]{1,0:T(8,128)(2,1)} %weight.1, f32[256,96]{1,0:T(8,128)} %copy.20.cosine, f32[256,96]{1,0:T(8,128)} %pad_maximum_fusion.5.sine), custom_call_target="tpu_custom_call" | custom-call | flops 2415919104 | bytes 9437184 | tf_op jit(solution)/shard_map/pallas_call | solution.py:260
  33.4 1.5 collective-permute-start.10
  34.8 3.9 %collective-permute-done.4 = bf16[32,1536]{1,0:T(8,128)(2,1)S(1)} collective-permute-done((bf16[32,1536]{1,0:T(8,128)(2,1)S(1)}, bf16[32,1536]{1,0:T(8,128)(2,1)S(1)}, u32[]{:S(2)}, u32[]{:S(2)}) %collective-permute-start.4) | collective-permute-done | bytes 98336 | tf_op jit(solution)/shard_map/ppermute | solution.py:31
  38.7 0.9 pad_maximum_fusion.4
  39.7 1.6 collective-permute-start.7
  41.3 1.5 collective-permute-start.8
  42.8 0.5 collective-permute-start.12
  43.3 0.5 collective-permute-start.11
  43.8 0.6 pad_add_fusion.1.side
  44.4 3.2 %shard_map.115 = (bf16[1536,256]{1,0:T(8,128)(2,1)}, bf16[768,256]{1,0:T(8,128)(2,1)}) custom-call(s32[2]{0:T(128)} %pad_add_fusion.1.side, bf16[2,1536,512]{2,1,0:T(8,128)(2,1)} %w_in.3, bf16[512,1536]{1,0:T(8,128)(2,1)} %w_down.3), custom_call_target="tpu_custom_call" | custom-call | tf_op jit(solution)/shard_map/pallas_call | solution.py:140
  47.6 8.4 %collective-permute-done.7 = bf16[128,1536]{1,0:T(8,128)(2,1)} collective-permute-done((bf16[128,1536]{1,0:T(8,128)(2,1)S(1)}, bf16[128,1536]{1,0:T(8,128)(2,1)}, u32[]{:S(2)}, u32[]{:S(2)}) %collective-permute-start.7) | collective-permute-done | bytes 393248 | tf_op jit(solution)/shard_map/ppermute | solution.py:82
  56.1 1.0 pad_maximum_fusion.rest_0_
  57.1 3.0 %collective-permute-done.12.rest_5_ = bf16[768,256]{1,0:T(8,128)(2,1)S(1)} collective-permute-done((bf16[768,256]{1,0:T(8,128)(2,1)S(1)}, bf16[768,256]{1,0:T(8,128)(2,1)S(1)}, u32[]{:S(2)}, u32[]{:S(2)}) %collective-permute-start.12) | collective-permute-done | bytes 393248 | tf_op jit(solution)/shard_map/ppermute | solution.py:82
  60.2 2.4 %collective-permute-done.11.rest_0_ = bf16[768,256]{1,0:T(8,128)(2,1)S(1)} collective-permute-done((bf16[768,256]{1,0:T(8,128)(2,1)}, bf16[768,256]{1,0:T(8,128)(2,1)S(1)}, u32[]{:S(2)}, u32[]{:S(2)}) %collective-permute-start.11) | collective-permute-done | bytes 393248 | tf_op jit(solution)/shard_map/ppermute | solution.py:31
  62.6 0.9 copy-done.2
  63.5 0.7 collective-permute-start.13
  64.1 11.4 %collective-permute-done.13.rest_1_ = bf16[256,1536]{1,0:T(8,128)(2,1)} collective-permute-done((bf16[256,1536]{1,0:T(8,128)(2,1)S(1)}, bf16[256,1536]{1,0:T(8,128)(2,1)}, u32[]{:S(2)}, u32[]{:S(2)}) %collective-permute-start.13) | collective-permute-done | bytes 786464 | tf_op jit(solution)/shard_map/ppermute | solution.py:82
  75.6 0.9 pad_maximum_fusion.1
  76.5 0.7 collective-permute-start.18
  77.2 1.3 collective-permute-start.17
  78.5 0.7 collective-permute-start.19
  79.2 0.9 copy-done.15
  80.1 0.8 copy.21.row_ids
  80.9 17.9 %shard_map.116 = (bf16[256,1536]{1,0:T(8,128)(2,1)}, bf16[256,1536]{1,0:T(8,128)(2,1)}) custom-call(s32[256,1]{1,0:T(8,128)} %copy.21.row_ids, s32[1,256]{1,0:T(1,128)} %column_ids.1, bf16[256,3072]{1,0:T(8,128)(2,1)} %shard_map.114.projected, bf16[256,1536]{1,0:T(8,128)(2,1)} %hidden.2, f32[1,1536]{1,0:T(1,128)} %get-tuple-element.75.gain, ...), custom_call_target="tpu_custom_call" | custom-call | tf_op jit(solution)/shard_map/pallas_call | solution.py:383
  99.0 0.4 collective-permute-done.16.rest_1_
  99.4 1.5 collective-permute-start.23
  100.9 2.0 %collective-permute-start.20 = (bf16[256,1536]{1,0:T(8,128)(2,1)S(1)}, bf16[256,1536]{1,0:T(8,128)(2,1)S(1)}, u32[]{:S(2)}, u32[]{:S(2)}) collective-permute-start(bf16[256,1536]{1,0:T(8,128)(2,1)S(1)} %copy-done.5), channel_id=1, source_target_pairs={{0,2},{1,3},{2,0},{3,1},{4,6},{5,7},{6,4},{7,5},{8,10},{9,11},{10,... | collective-permute-start | bytes 2359304 | tf_op jit(solution)/shard_map/ppermute | solution.py:31
  102.9 1.5 collective-permute-start.22
  104.4 10.6 %collective-permute-done.22.rest_4_ = bf16[768,256]{1,0:T(8,128)(2,1)S(1)} collective-permute-done((bf16[768,256]{1,0:T(8,128)(2,1)S(1)}, bf16[768,256]{1,0:T(8,128)(2,1)S(1)}, u32[]{:S(2)}, u32[]{:S(2)}) %collective-permute-start.22) | collective-permute-done | bytes 393248 | tf_op jit(solution)/shard_map/ppermute | solution.py:82
  115.0 0.9 collective-permute-start.25
  116.0 1.0 copy-done.8
  117.0 3.8 %shard_map.117 = (f32[256,1536]{1,0:T(8,128)S(1)}, f32[256,1536]{1,0:T(8,128)S(1)}) custom-call(bf16[256,1536]{1,0:T(8,128)(2,1)S(1)} %copy-done.5, bf16[256,1536]{1,0:T(8,128)(2,1)S(1)} %collective-permute-done.21.right, bf16[1536,256]{1,0:T(8,128)(2,1)S(1)} %copy-done.1, bf16[768,256]{1,0:T(8,128)(2,1)S(1)} %copy-done.7, bf16[1536,256]{1,0:T(8,128)(2,1)S(1)} %copy-done.4, ...), custom_call_target="tpu_custom_call" | custom-call | tf_op jit(solution)/shard_map/pallas_call | solution.py:434
  121.7 0.8 shard_map.119
  122.5 4.6 %collective-permute-done.25.rest_10_.rest_7_ = bf16[1536,256]{1,0:T(8,128)(2,1)S(1)} collective-permute-done((bf16[1536,256]{1,0:T(8,128)(2,1)S(1)}, bf16[1536,256]{1,0:T(8,128)(2,1)S(1)}, u32[]{:S(2)}, u32[]{:S(2)}) %collective-permute-start.25) | collective-permute-done | bytes 786464 | tf_op jit(solution)/shard_map/ppermute | solution.py:82
  127.1 3.7 %shard_map.118 = (f32[256,1536]{1,0:T(8,128)S(1)}, f32[256,1536]{1,0:T(8,128)S(1)}) custom-call(bf16[256,1536]{1,0:T(8,128)(2,1)S(1)} %collective-permute-done.20.left.rest_0_, bf16[256,1536]{1,0:T(8,128)(2,1)S(1)} %collective-permute-done.24.right, bf16[1536,256]{1,0:T(8,128)(2,1)S(1)} %copy-done.1, bf16[768,256]{1,0:T(8,128)(2,1)S(1)} %copy-done.7, ...), custom_call_target="tpu_custom_call" | custom-call | tf_op jit(solution)/shard_map/pallas_call | solution.py:434
  130.8 2.6 %shard_map.120 = (f32[256,1536]{1,0:T(8,128)S(1)}, bf16[256,1536]{1,0:T(8,128)(2,1)S(1)}) custom-call(bf16[256,1536]{1,0:T(8,128)(2,1)S(1)} %collective-permute-done.20.left.rest_0_, bf16[256,1536]{1,0:T(8,128)(2,1)S(1)} %collective-permute-done.24.right, bf16[768,256]{1,0:T(8,128)(2,1)S(1)} %collective-permute-done.11.rest_0_, ...), custom_call_target="tpu_custom_call" | custom-call | tf_op jit(solution)/shard_map/pallas_call | solution.py:434
  133.5 2.3 %collective-permute-done.26 = bf16[256,1536]{1,0:T(8,128)(2,1)S(1)} collective-permute-done((bf16[256,1536]{1,0:T(8,128)(2,1)S(1)}, bf16[256,1536]{1,0:T(8,128)(2,1)S(1)}, u32[]{:S(2)}, u32[]{:S(2)}) %collective-permute-start.26) | collective-permute-done | bytes 786464 | tf_op jit(solution)/shard_map/ppermute | solution.py:45
  135.8 1.1 add_convert_fusion
  137.0 1.5 collective-permute-start.28
  138.8 3.5 %shard_map.121 = (f32[256,1536]{1,0:T(8,128)S(1)}, bf16[256,1536]{1,0:T(8,128)(2,1)}) custom-call(bf16[256,1536]{1,0:T(8,128)(2,1)S(1)} %copy-done.5, bf16[256,1536]{1,0:T(8,128)(2,1)S(1)} %collective-permute-done.21.right, bf16[768,256]{1,0:T(8,128)(2,1)S(1)} %collective-permute-done.11.rest_0_, bf16[768,256]{1,0:T(8,128)(2,1)S(1)} %collective-permute-done.16.rest_1_, ...), custom_call_target="tpu_custom_call" | custom-call | tf_op jit(solution)/shard_map/pallas_call | solution.py:434
  142.3 1.2 copy-done.11
  143.4 5.5 %collective-permute-done.28.rest_2_ = bf16[128,1536]{1,0:T(8,128)(2,1)S(1)} collective-permute-done((bf16[128,1536]{1,0:T(8,128)(2,1)S(1)}, bf16[128,1536]{1,0:T(8,128)(2,1)S(1)}, u32[]{:S(2)}, u32[]{:S(2)}) %collective-permute-start.28) | collective-permute-done | bytes 393248 | tf_op jit(solution)/shard_map/ppermute | solution.py:45
  149.0 7.3 %collective-permute-done.29.rest_3_ = bf16[128,1536]{1,0:T(8,128)(2,1)S(1)} collective-permute-done((bf16[128,1536]{1,0:T(8,128)(2,1)S(1)}, bf16[128,1536]{1,0:T(8,128)(2,1)S(1)}, u32[]{:S(2)}, u32[]{:S(2)}) %collective-permute-start.29) | collective-permute-done | bytes 393248 | tf_op jit(solution)/shard_map/ppermute | solution.py:45
  156.3 0.8 copy-done.18
  157.0 0.8 collective-permute-start.30
  157.8 2.6 %shard_map.122 = bf16[4,128,1536]{2,1,0:T(8,128)(2,1)} custom-call(s32[1]{0:T(128)} %bitcast.12.group, bf16[128,1536]{1,0:T(8,128)(2,1)} %copy-done.10, bf16[128,1536]{1,0:T(8,128)(2,1)} %copy-done.16, bf16[128,1536]{1,0:T(8,128)(2,1)} %copy-done.17, bf16[128,1536]{1,0:T(8,128)(2,1)} %copy-done.18), custom_call_target="tpu_custom_call" | custom-call | tf_op jit(solution)/shard_map/pallas_call | solution.py:514
  160.4 0.9 copy-done.14
  161.3 3.0 %shard_map.123 = bf16[256,1536]{1,0:T(8,128)(2,1)} custom-call(f32[256,1536]{1,0:T(8,128)} %copy-done.11, bf16[256,1536]{1,0:T(8,128)(2,1)} %copy-done.14, bf16[256,1536]{1,0:T(8,128)(2,1)} %collective-permute-done.31.refs_2_), custom_call_target="tpu_custom_call" | custom-call | tf_op jit(solution)/shard_map/pallas_call | solution.py:458
  (81 shorter events, 2.0 us)
Async XLA Ops:
  1.6 15.0 %collective-permute-start.2 = (bf16[32,1536]{1,0:T(8,128)(2,1)S(1)}, bf16[32,1536]{1,0:T(8,128)(2,1)S(1)}, u32[]{:S(2)}, u32[]{:S(2)}) collective-permute-start(bf16[32,1536]{1,0:T(8,128)(2,1)S(1)} %get-tuple-element.72), channel_id=1, source_target_pairs={{0,8},{8,0},{16,24},{24,16},{1,9},{9,1},{17,25},{25,17},{2,10},{10... | collective-permute-start | bytes 294920 | tf_op jit(solution)/shard_map/ppermute | solution.py:45
  2.2 14.5 %collective-permute-start.1 = (bf16[32,1536]{1,0:T(8,128)(2,1)S(1)}, bf16[32,1536]{1,0:T(8,128)(2,1)S(1)}, u32[]{:S(2)}, u32[]{:S(2)}) collective-permute-start(bf16[32,1536]{1,0:T(8,128)(2,1)S(1)} %get-tuple-element.73), channel_id=1, source_target_pairs={{0,16},{8,24},{16,0},{24,8},{1,17},{9,25},{17,1},{25,9},{2,18},{10... | collective-permute-start | bytes 294920 | tf_op jit(solution)/shard_map/ppermute | solution.py:45
  4.7 12.0 %collective-permute-start = (bf16[32,1536]{1,0:T(8,128)(2,1)S(1)}, bf16[32,1536]{1,0:T(8,128)(2,1)S(1)}, u32[]{:S(2)}, u32[]{:S(2)}) collective-permute-start(bf16[32,1536]{1,0:T(8,128)(2,1)S(1)} %get-tuple-element.74), channel_id=1, source_target_pairs={{0,24},{8,16},{16,8},{24,0},{1,25},{9,17},{17,9},{25,1},{2,26},{10... | collective-permute-start | bytes 294920 | tf_op jit(solution)/shard_map/ppermute | solution.py:45
  5.4 8.1 %copy-start.22 = (s32[8]{0:T(128)S(1)}, s32[8]{0:T(128)}, u32[]{:S(2)}) copy-start(s32[8]{0:T(128)} %param.18) | copy-start | bytes 100
  5.4 10.7 %copy-start.20 = (f32[2,1536]{1,0:T(2,128)S(1)}, f32[2,1536]{1,0:T(2,128)}, u32[]{:S(2)}) copy-start(f32[2,1536]{1,0:T(2,128)} %param.12) | copy-start | bytes 36868
  5.4 16.7 %copy-start.19 = (s32[1,256]{1,0:T(1,128)S(1)}, s32[1,256]{1,0:T(1,128)}, u32[]{:S(2)}) copy-start(s32[1,256]{1,0:T(1,128)} %column_ids.1) | copy-start | bytes 3076
  9.1 30.6 %collective-permute-start.6 = (bf16[768,256]{1,0:T(8,128)(2,1)}, bf16[768,256]{1,0:T(8,128)(2,1)S(1)}, u32[]{:S(2)}, u32[]{:S(2)}) collective-permute-start(bf16[768,256]{1,0:T(8,128)(2,1)} %get-tuple-element.40.rest_1_), channel_id=1, source_target_pairs={{0,4},{1,5},{2,6},{3,7},{4,0},{5,1},{6,2},{7,3},{8,12},{9,13},{10,... | collective-permute-start | bytes 1179656 | tf_op jit(solution)/shard_map/ppermute | solution.py:31
  12.0 21.4 %collective-permute-start.9 = (bf16[1536,256]{1,0:T(8,128)(2,1)}, bf16[1536,256]{1,0:T(8,128)(2,1)S(1)}, u32[]{:S(2)}, u32[]{:S(2)}) collective-permute-start(bf16[1536,256]{1,0:T(8,128)(2,1)} %get-tuple-element.37.rest_0_), channel_id=1, source_target_pairs={{0,1},{1,0},{2,3},{3,2},{4,5},{5,4},{6,7},{7,6},{8,9},{9,8},{10,11... | collective-permute-start | bytes 2359304 | tf_op jit(solution)/shard_map/ppermute | solution.py:41
  17.6 17.2 %collective-permute-start.5 = (bf16[32,1536]{1,0:T(8,128)(2,1)S(1)}, bf16[32,1536]{1,0:T(8,128)(2,1)S(1)}, u32[]{:S(2)}, u32[]{:S(2)}) collective-permute-start(bf16[32,1536]{1,0:T(8,128)(2,1)S(1)} %fusion.1), channel_id=1, source_target_pairs={{0,6},{1,7},{2,4},{3,5},{4,2},{5,3},{6,0},{7,1},{8,14},{9,15},{10,... | collective-permute-start | bytes 294920 | tf_op jit(solution)/shard_map/ppermute | solution.py:31
  19.0 19.7 %collective-permute-start.4 = (bf16[32,1536]{1,0:T(8,128)(2,1)S(1)}, bf16[32,1536]{1,0:T(8,128)(2,1)S(1)}, u32[]{:S(2)}, u32[]{:S(2)}) collective-permute-start(bf16[32,1536]{1,0:T(8,128)(2,1)S(1)} %fusion.1), channel_id=1, source_target_pairs={{0,4},{1,5},{2,6},{3,7},{4,0},{5,1},{6,2},{7,3},{8,12},{9,13},{10,... | collective-permute-start | bytes 294920 | tf_op jit(solution)/shard_map/ppermute | solution.py:31
  20.7 18.0 %collective-permute-start.3 = (bf16[32,1536]{1,0:T(8,128)(2,1)S(1)}, bf16[32,1536]{1,0:T(8,128)(2,1)}, u32[]{:S(2)}, u32[]{:S(2)}) collective-permute-start(bf16[32,1536]{1,0:T(8,128)(2,1)S(1)} %fusion.1), channel_id=1, source_target_pairs={{0,2},{1,3},{2,0},{3,1},{4,6},{5,7},{6,4},{7,5},{8,10},{9,11},{10,... | collective-permute-start | bytes 294920 | tf_op jit(solution)/shard_map/ppermute | solution.py:31
  24.4 16.8 %copy-start.6 = (bf16[768,256]{1,0:T(8,128)(2,1)S(1)}, bf16[768,256]{1,0:T(8,128)(2,1)}, u32[]{:S(2)}) copy-start(bf16[768,256]{1,0:T(8,128)(2,1)} %get-tuple-element.40.rest_1_) | copy-start | bytes 1179652
  33.4 29.2 %collective-permute-start.10 = (bf16[1536,256]{1,0:T(8,128)(2,1)S(1)}, bf16[1536,256]{1,0:T(8,128)(2,1)S(1)}, u32[]{:S(2)}, u32[]{:S(2)}) collective-permute-start(bf16[1536,256]{1,0:T(8,128)(2,1)S(1)} %collective-permute-done.9.rest_4_), channel_id=1, source_target_pairs={{0,16},{8,24},{16,0},{24,8},{1,17},{9,25},{17,1},{25,9},{2,18},{10... | collective-permute-start | bytes 2359304 | tf_op jit(solution)/shard_map/ppermute | solution.py:45
  39.7 16.4 %collective-permute-start.7 = (bf16[128,1536]{1,0:T(8,128)(2,1)S(1)}, bf16[128,1536]{1,0:T(8,128)(2,1)}, u32[]{:S(2)}, u32[]{:S(2)}) collective-permute-start(bf16[128,1536]{1,0:T(8,128)(2,1)S(1)} %pad_maximum_fusion.4), channel_id=1, source_target_pairs={{0,16},{1,17},{2,18},{3,19},{4,20},{5,21},{6,22},{7,23},{8,9},{9,8... | collective-permute-start | bytes 1179656 | tf_op jit(solution)/shard_map/ppermute | solution.py:82
  41.3 15.9 %collective-permute-start.8 = (bf16[768,256]{1,0:T(8,128)(2,1)S(1)}, bf16[768,256]{1,0:T(8,128)(2,1)}, u32[]{:S(2)}, u32[]{:S(2)}) collective-permute-start(bf16[768,256]{1,0:T(8,128)(2,1)S(1)} %copy-done.6), channel_id=1, source_target_pairs={{0,1},{1,0},{2,3},{3,2},{4,5},{5,4},{6,7},{7,6},{8,9},{9,8},{10,11... | collective-permute-start | bytes 1179656 | tf_op jit(solution)/shard_map/ppermute | solution.py:41
  42.8 17.4 %collective-permute-start.12 = (bf16[768,256]{1,0:T(8,128)(2,1)S(1)}, bf16[768,256]{1,0:T(8,128)(2,1)S(1)}, u32[]{:S(2)}, u32[]{:S(2)}) collective-permute-start(bf16[768,256]{1,0:T(8,128)(2,1)S(1)} %collective-permute-done.6.rest_2_), channel_id=1, source_target_pairs={{0,16},{1,17},{2,18},{3,19},{4,20},{5,21},{6,22},{7,23},{8,9},{9,8... | collective-permute-start | bytes 1179656 | tf_op jit(solution)/shard_map/ppermute | solution.py:82
  43.3 19.3 %collective-permute-start.11 = (bf16[768,256]{1,0:T(8,128)(2,1)}, bf16[768,256]{1,0:T(8,128)(2,1)S(1)}, u32[]{:S(2)}, u32[]{:S(2)}) collective-permute-start(bf16[768,256]{1,0:T(8,128)(2,1)} %get-tuple-element.45), channel_id=1, source_target_pairs={{0,4},{1,5},{2,6},{3,7},{4,0},{5,1},{6,2},{7,3},{8,12},{9,13},{10,... | collective-permute-start | bytes 1179656 | tf_op jit(solution)/shard_map/ppermute | solution.py:31
  57.1 22.1 %copy-start.13 = (bf16[256,1536]{1,0:T(8,128)(2,1)}, bf16[256,1536]{1,0:T(8,128)(2,1)S(1)}, u32[]{:S(2)}) copy-start(bf16[256,1536]{1,0:T(8,128)(2,1)S(1)} %pad_maximum_fusion.rest_0_) | copy-start | bytes 2359300
  62.6 0.9 copy-start.2
  63.5 12.1 %collective-permute-start.13 = (bf16[256,1536]{1,0:T(8,128)(2,1)S(1)}, bf16[256,1536]{1,0:T(8,128)(2,1)}, u32[]{:S(2)}, u32[]{:S(2)}) collective-permute-start(bf16[256,1536]{1,0:T(8,128)(2,1)S(1)} %pad_maximum_fusion.rest_0_), channel_id=1, source_target_pairs={{0,1},{1,0},{2,3},{3,2},{4,5},{5,4},{6,7},{7,6},{8,24},{9,25},{10,... | collective-permute-start | bytes 2359304 | tf_op jit(solution)/shard_map/ppermute | solution.py:82
  64.1 15.1 %collective-permute-start.14 = (bf16[256,1536]{1,0:T(8,128)(2,1)S(1)}, bf16[256,1536]{1,0:T(8,128)(2,1)S(1)}, u32[]{:S(2)}, u32[]{:S(2)}) collective-permute-start(bf16[256,1536]{1,0:T(8,128)(2,1)S(1)} %pad_maximum_fusion.rest_0_), channel_id=1, source_target_pairs={{0,8},{8,0},{16,24},{24,16},{1,9},{9,1},{17,25},{25,17},{2,10},{10... | collective-permute-start | bytes 2359304 | tf_op jit(solution)/shard_map/ppermute | solution.py:45
  75.6 5.3 %collective-permute-start.15 = (bf16[256,1536]{1,0:T(8,128)(2,1)}, bf16[256,1536]{1,0:T(8,128)(2,1)}, u32[]{:S(2)}, u32[]{:S(2)}) collective-permute-start(bf16[256,1536]{1,0:T(8,128)(2,1)} %collective-permute-done.13.rest_1_), channel_id=1, source_target_pairs={{0,8},{8,0},{16,24},{24,16},{1,9},{9,1},{17,25},{25,17},{2,10},{10... | collective-permute-start | bytes 2359304 | tf_op jit(solution)/shard_map/ppermute | solution.py:45
  76.5 22.9 %collective-permute-start.18 = (bf16[1536,256]{1,0:T(8,128)(2,1)}, bf16[1536,256]{1,0:T(8,128)(2,1)S(1)}, u32[]{:S(2)}, u32[]{:S(2)}) collective-permute-start(bf16[1536,256]{1,0:T(8,128)(2,1)} %pad_maximum_fusion.1), channel_id=1, source_target_pairs={{0,1},{1,0},{2,3},{3,2},{4,5},{5,4},{6,7},{7,6},{8,24},{9,25},{10,... | collective-permute-start | bytes 2359304 | tf_op jit(solution)/shard_map/ppermute | solution.py:82
  77.2 21.8 %collective-permute-start.17 = (bf16[768,256]{1,0:T(8,128)(2,1)S(1)}, bf16[768,256]{1,0:T(8,128)(2,1)S(1)}, u32[]{:S(2)}, u32[]{:S(2)}) collective-permute-start(bf16[768,256]{1,0:T(8,128)(2,1)S(1)} %collective-permute-done.11.rest_0_), channel_id=1, source_target_pairs={{0,16},{1,17},{2,18},{3,19},{4,20},{5,21},{6,22},{7,23},{8,9},{9,8... | collective-permute-start | bytes 1179656 | tf_op jit(solution)/shard_map/ppermute | solution.py:82
  78.5 20.5 %collective-permute-start.19 = (bf16[768,256]{1,0:T(8,128)(2,1)}, bf16[768,256]{1,0:T(8,128)(2,1)}, u32[]{:S(2)}, u32[]{:S(2)}) collective-permute-start(bf16[768,256]{1,0:T(8,128)(2,1)} %collective-permute-done.8.rest_5_), channel_id=1, source_target_pairs={{0,16},{8,24},{16,0},{24,8},{1,17},{9,25},{17,1},{25,9},{2,18},{10... | collective-permute-start | bytes 1179656 | tf_op jit(solution)/shard_map/ppermute | solution.py:45
  79.2 0.9 copy-start.15
  80.1 19.3 %collective-permute-start.16 = (bf16[768,256]{1,0:T(8,128)(2,1)}, bf16[768,256]{1,0:T(8,128)(2,1)S(1)}, u32[]{:S(2)}, u32[]{:S(2)}) collective-permute-start(bf16[768,256]{1,0:T(8,128)(2,1)} %get-tuple-element.49), channel_id=1, source_target_pairs={{0,4},{1,5},{2,6},{3,7},{4,0},{5,1},{6,2},{7,3},{8,12},{9,13},{10,... | collective-permute-start | bytes 1179656 | tf_op jit(solution)/shard_map/ppermute | solution.py:31
  80.9 35.0 %copy-start.7 = (bf16[768,256]{1,0:T(8,128)(2,1)S(1)}, bf16[768,256]{1,0:T(8,128)(2,1)}, u32[]{:S(2)}) copy-start(bf16[768,256]{1,0:T(8,128)(2,1)} %get-tuple-element.40.rest_1_) | copy-start | bytes 1179652
  98.8 2.1 %copy-start.5 = (bf16[256,1536]{1,0:T(8,128)(2,1)S(1)}, bf16[256,1536]{1,0:T(8,128)(2,1)}, u32[]{:S(2)}) copy-start(bf16[256,1536]{1,0:T(8,128)(2,1)} %get-tuple-element.64.left) | copy-start | bytes 2359300
  98.9 17.1 %copy-start.1 = (bf16[1536,256]{1,0:T(8,128)(2,1)S(1)}, bf16[1536,256]{1,0:T(8,128)(2,1)}, u32[]{:S(2)}) copy-start(bf16[1536,256]{1,0:T(8,128)(2,1)} %get-tuple-element.37.rest_0_) | copy-start | bytes 2359300
  98.9 17.1 %copy-start.3 = (bf16[1536,256]{1,0:T(8,128)(2,1)S(1)}, bf16[1536,256]{1,0:T(8,128)(2,1)}, u32[]{:S(2)}) copy-start(bf16[1536,256]{1,0:T(8,128)(2,1)} %copy-done.2) | copy-start | bytes 2359300
  98.9 17.1 %copy-start.4 = (bf16[1536,256]{1,0:T(8,128)(2,1)S(1)}, bf16[1536,256]{1,0:T(8,128)(2,1)}, u32[]{:S(2)}) copy-start(bf16[1536,256]{1,0:T(8,128)(2,1)} %get-tuple-element.51.rest_2_) | copy-start | bytes 2359300
  98.9 17.0 %collective-permute-start.21 = (bf16[256,1536]{1,0:T(8,128)(2,1)}, bf16[256,1536]{1,0:T(8,128)(2,1)S(1)}, u32[]{:S(2)}, u32[]{:S(2)}) collective-permute-start(bf16[256,1536]{1,0:T(8,128)(2,1)} %get-tuple-element.64.left), channel_id=1, source_target_pairs={{0,8},{8,0},{16,24},{24,16},{1,9},{9,1},{17,25},{25,17},{2,10},{10... | collective-permute-start | bytes 2359304 | tf_op jit(solution)/shard_map/ppermute | solution.py:45
  99.4 21.4 %collective-permute-start.23 = (bf16[1536,256]{1,0:T(8,128)(2,1)S(1)}, bf16[1536,256]{1,0:T(8,128)(2,1)S(1)}, u32[]{:S(2)}, u32[]{:S(2)}) collective-permute-start(bf16[1536,256]{1,0:T(8,128)(2,1)S(1)} %pad_maximum_fusion.2), channel_id=1, source_target_pairs={{0,1},{1,0},{2,3},{3,2},{4,5},{5,4},{6,7},{7,6},{8,24},{9,25},{10,... | collective-permute-start | bytes 2359304 | tf_op jit(solution)/shard_map/ppermute | solution.py:82
  100.9 20.2 %collective-permute-start.20 = (bf16[256,1536]{1,0:T(8,128)(2,1)S(1)}, bf16[256,1536]{1,0:T(8,128)(2,1)S(1)}, u32[]{:S(2)}, u32[]{:S(2)}) collective-permute-start(bf16[256,1536]{1,0:T(8,128)(2,1)S(1)} %copy-done.5), channel_id=1, source_target_pairs={{0,2},{1,3},{2,0},{3,1},{4,6},{5,7},{6,4},{7,5},{8,10},{9,11},{10,... | collective-permute-start | bytes 2359304 | tf_op jit(solution)/shard_map/ppermute | solution.py:31
  102.9 12.1 %collective-permute-start.22 = (bf16[768,256]{1,0:T(8,128)(2,1)S(1)}, bf16[768,256]{1,0:T(8,128)(2,1)S(1)}, u32[]{:S(2)}, u32[]{:S(2)}) collective-permute-start(bf16[768,256]{1,0:T(8,128)(2,1)S(1)} %collective-permute-done.16.rest_1_), channel_id=1, source_target_pairs={{0,16},{1,17},{2,18},{3,19},{4,20},{5,21},{6,22},{7,23},{8,9},{9,8... | collective-permute-start | bytes 1179656 | tf_op jit(solution)/shard_map/ppermute | solution.py:82
  115.0 12.1 %collective-permute-start.25 = (bf16[1536,256]{1,0:T(8,128)(2,1)S(1)}, bf16[1536,256]{1,0:T(8,128)(2,1)S(1)}, u32[]{:S(2)}, u32[]{:S(2)}) collective-permute-start(bf16[1536,256]{1,0:T(8,128)(2,1)S(1)} %pad_maximum_fusion.3), channel_id=1, source_target_pairs={{0,1},{1,0},{2,3},{3,2},{4,5},{5,4},{6,7},{7,6},{8,24},{9,25},{10,... | collective-permute-start | bytes 2359304 | tf_op jit(solution)/shard_map/ppermute | solution.py:82
  116.0 1.0 copy-start.8
  117.0 4.5 %copy-start.21 = (s32[16,1]{0,1:T(1,128)S(1)}, s32[16,1]{0,1:T(1,128)}, u32[]{:S(2)}) copy-start(s32[16,1]{0,1:T(1,128)} %param.19) | copy-start | bytes 196
  117.0 4.8 %copy-start = (bf16[256,3072]{1,0:T(8,128)(2,1)S(1)}, bf16[256,3072]{1,0:T(8,128)(2,1)}, u32[]{:S(2)}) copy-start(bf16[256,3072]{1,0:T(8,128)(2,1)} %shard_map.114.projected) | copy-start | bytes 4718596
  120.8 6.3 %copy-start.9 = (bf16[768,256]{1,0:T(8,128)(2,1)S(1)}, bf16[768,256]{1,0:T(8,128)(2,1)}, u32[]{:S(2)}) copy-start(bf16[768,256]{1,0:T(8,128)(2,1)} %get-tuple-element.43.rest_3_) | copy-start | bytes 1179652
  121.1 5.9 %collective-permute-start.24 = (bf16[256,1536]{1,0:T(8,128)(2,1)S(1)}, bf16[256,1536]{1,0:T(8,128)(2,1)S(1)}, u32[]{:S(2)}, u32[]{:S(2)}) collective-permute-start(bf16[256,1536]{1,0:T(8,128)(2,1)S(1)} %collective-permute-done.20.left.rest_0_), channel_id=1, source_target_pairs={{0,8},{8,0},{16,24},{24,16},{1,9},{9,1},{17,25},{25,17},{2,10},{10... | collective-permute-start | bytes 2359304 | tf_op jit(solution)/shard_map/ppermute | solution.py:45
  122.5 8.3 %copy-start.10 = (bf16[128,1536]{1,0:T(8,128)(2,1)}, bf16[128,1536]{1,0:T(8,128)(2,1)S(1)}, u32[]{:S(2)}) copy-start(bf16[128,1536]{1,0:T(8,128)(2,1)S(1)} %get-tuple-element.59.rest_14_.rest_0_) | copy-start | bytes 1179652
  133.4 2.4 %collective-permute-start.26 = (bf16[256,1536]{1,0:T(8,128)(2,1)S(1)}, bf16[256,1536]{1,0:T(8,128)(2,1)S(1)}, u32[]{:S(2)}, u32[]{:S(2)}) collective-permute-start(bf16[256,1536]{1,0:T(8,128)(2,1)S(1)} %get-tuple-element.61), channel_id=1, source_target_pairs={{0,8},{8,0},{16,24},{24,16},{1,9},{9,1},{17,25},{25,17},{2,10},{10... | collective-permute-start | bytes 2359304 | tf_op jit(solution)/shard_map/ppermute | solution.py:45
  135.8 3.0 %copy-start.12 = (bf16[256,1536]{1,0:T(8,128)(2,1)S(1)}, bf16[256,1536]{1,0:T(8,128)(2,1)}, u32[]{:S(2)}) copy-start(bf16[256,1536]{1,0:T(8,128)(2,1)} %get-tuple-element.65.rest_14_) | copy-start | bytes 2359300
  136.9 1.9 %collective-permute-start.27 = (bf16[128,1536]{1,0:T(8,128)(2,1)S(1)}, bf16[128,1536]{1,0:T(8,128)(2,1)S(1)}, u32[]{:S(2)}, u32[]{:S(2)}) collective-permute-start(bf16[128,1536]{1,0:T(8,128)(2,1)S(1)} %get-tuple-element.63), channel_id=1, source_target_pairs={{0,8},{8,0},{16,24},{24,16},{1,9},{9,1},{17,25},{25,17},{2,10},{10... | collective-permute-start | bytes 1179656 | tf_op jit(solution)/shard_map/ppermute | solution.py:45
  137.0 11.9 %collective-permute-start.28 = (bf16[128,1536]{1,0:T(8,128)(2,1)S(1)}, bf16[128,1536]{1,0:T(8,128)(2,1)S(1)}, u32[]{:S(2)}, u32[]{:S(2)}) collective-permute-start(bf16[128,1536]{1,0:T(8,128)(2,1)S(1)} %get-tuple-element.68), channel_id=1, source_target_pairs={{0,16},{8,24},{16,0},{24,8},{1,17},{9,25},{17,1},{25,9},{2,18},{10... | collective-permute-start | bytes 1179656 | tf_op jit(solution)/shard_map/ppermute | solution.py:45
  138.5 17.8 %collective-permute-start.29 = (bf16[128,1536]{1,0:T(8,128)(2,1)S(1)}, bf16[128,1536]{1,0:T(8,128)(2,1)S(1)}, u32[]{:S(2)}, u32[]{:S(2)}) collective-permute-start(bf16[128,1536]{1,0:T(8,128)(2,1)S(1)} %get-tuple-element.69), channel_id=1, source_target_pairs={{0,24},{8,16},{16,8},{24,0},{1,25},{9,17},{17,9},{25,1},{2,26},{10... | collective-permute-start | bytes 1179656 | tf_op jit(solution)/shard_map/ppermute | solution.py:45
  138.7 21.7 %collective-permute-start.31 = (bf16[256,1536]{1,0:T(8,128)(2,1)}, bf16[256,1536]{1,0:T(8,128)(2,1)}, u32[]{:S(2)}, u32[]{:S(2)}) collective-permute-start(bf16[256,1536]{1,0:T(8,128)(2,1)} %add_convert_fusion), channel_id=1, source_target_pairs={{0,2},{1,3},{2,0},{3,1},{4,6},{5,7},{6,4},{7,5},{8,10},{9,11},{10,... | collective-permute-start | bytes 2359304 | tf_op jit(solution)/shard_map/ppermute | solution.py:31
  138.8 3.5 %copy-start.16 = (bf16[128,1536]{1,0:T(8,128)(2,1)}, bf16[128,1536]{1,0:T(8,128)(2,1)S(1)}, u32[]{:S(2)}) copy-start(bf16[128,1536]{1,0:T(8,128)(2,1)S(1)} %collective-permute-done.27.rest_1_) | copy-start | bytes 1179652
  142.3 1.2 copy-start.11
  149.0 7.3 %copy-start.17 = (bf16[128,1536]{1,0:T(8,128)(2,1)}, bf16[128,1536]{1,0:T(8,128)(2,1)S(1)}, u32[]{:S(2)}) copy-start(bf16[128,1536]{1,0:T(8,128)(2,1)S(1)} %collective-permute-done.28.rest_2_) | copy-start | bytes 1179652
  156.3 0.8 copy-start.18
  157.0 3.4 %collective-permute-start.30 = (bf16[256,1536]{1,0:T(8,128)(2,1)}, bf16[256,1536]{1,0:T(8,128)(2,1)S(1)}, u32[]{:S(2)}, u32[]{:S(2)}) collective-permute-start(bf16[256,1536]{1,0:T(8,128)(2,1)} %get-tuple-element.70), channel_id=1, source_target_pairs={{0,8},{8,0},{16,24},{24,16},{1,9},{9,1},{17,25},{25,17},{2,10},{10... | collective-permute-start | bytes 2359304 | tf_op jit(solution)/shard_map/ppermute | solution.py:45
  160.4 0.9 copy-start.14
